TPU v7x, 32 devices: a whole 2x2x4 slice. The times are simulated.
32 devices in a mesh: depth: 4 (over y, x), tile: 8 (over z, core).
Axes of the slice: x: 2, y: 2, z: 4, core: 2. Of those that a mesh axis runs over, the one named last changes fastest.
Arguments:
- density_blocks: bfloat16 [1024, 128, 128], P(('depth', 'tile')), may hold values from -6 to 6
- block_owner: int32 [1024], P(('depth', 'tile')), may hold values from 0 to 8, as said below
- block_place: int32 [1024], P(('depth', 'tile')), may hold values from 0 to 15, as said below
- lens_weights: float32 [16], P('depth'), may hold values from 0.02 to 0.1
- ray_cells: int32 [16, 16384], P('depth', 'tile'), may hold values from 0 to 65535
- ray_angles: float32 [2, 16384], P(None, 'tile'), may hold values from -6 to 6
Outputs:
- exit_states: float32 [4, 6, 16384], P('depth', None, 'tile')
Inputs may be any that keep to these rules, and one draw needn't show every extreme that they name: `block_owner`: in every depth group each tile receives each of its 4 * 4 (plane, quadrant) places from exactly one live entry; no list sends more than 4 blocks to one tile, and in every group some list sends exactly 4 blocks to every tile. `block_place`: empty entries hold 0.
All inputs are finite; a program needn't handle non-finite values.
Results may differ from a plain program's by a relative error of at most 0.0011.
Values may be sent and summed in bfloat16 or wider, within the bound.
No kernel may reach another device: no remote copies, remote signals or barrier semaphores. Data moves between devices by JAX's collectives and lax.ppermute only.
A program may use at most 64 MiB of HBM per device.

v0:
```python
import jax
import jax.numpy as jnp
from jax import lax
from jax.sharding import PartitionSpec as P

HIGHEST = lax.Precision.HIGHEST


def extended(cells, sides, width):
    for axis, dim in sides:
        count = lax.axis_size(axis)
        ends = count - 1
        head = lax.slice_in_dim(cells, 0, width, axis=dim)
        tail = lax.slice_in_dim(cells, cells.shape[dim] - width, cells.shape[dim], axis=dim)
        cells = jnp.concatenate(
            [
                lax.ppermute(tail, axis, [(i, (i + 1) % count) for i in range(ends)]),
                cells,
                lax.ppermute(head, axis, [((i + 1) % count, i) for i in range(ends)]),
            ],
            axis=dim,
        )
    return cells


def carried_in(part, axis, combine, identity):
    place = lax.axis_index(axis)
    gathered = lax.all_gather(part, axis)
    state = jnp.zeros_like(part) + jnp.asarray(identity, part.dtype)

    def one(step, state):
        return combine(state, lax.dynamic_index_in_dim(gathered, step, 0, False))

    return lax.fori_loop(0, place, one, state)


def sine_table(length):
    index = jnp.arange(length, dtype=jnp.float32) + 1.0
    tables = jnp.sin(jnp.pi * index[:, None] * index[None, :] / (length + 1.0))
    return tables * jnp.sqrt(2.0 / (length + 1.0))


def eigen_table(length):
    index = jnp.arange(length, dtype=jnp.float32) + 1.0
    single = 2.0 - 2.0 * jnp.cos(jnp.pi * index / (length + 1.0))
    return -(single[:, None] + single[None, :])


def derive_fields(padded):
    center = padded[..., 1:-1, 1:-1]
    north = padded[..., 2:, 1:-1]
    south = padded[..., :-2, 1:-1]
    east_side = padded[..., 1:-1, 2:]
    west_side = padded[..., 1:-1, :-2]
    second_xx = north - 2.0 * center + south
    second_yy = east_side - 2.0 * center + west_side
    second_xy = 0.25 * (
        padded[..., 2:, 2:] - padded[..., 2:, :-2] - padded[..., :-2, 2:] + padded[..., :-2, :-2]
    )
    return (
        0.5 * (north - south),
        0.5 * (east_side - west_side),
        0.5 * (second_xx + second_yy),
        0.5 * (second_xx - second_yy),
        second_xy,
    )


def compose_maps(earlier, later):
    first_xx, first_xy, first_yx, first_yy = (earlier[0], earlier[1], earlier[2], earlier[3])
    second_xx, second_xy, second_yx, second_yy = (later[0], later[1], later[2], later[3])
    return jnp.stack(
        [
            second_xx * first_xx + second_xy * first_yx,
            second_xx * first_xy + second_xy * first_yy,
            second_yx * first_xx + second_yy * first_yx,
            second_yx * first_xy + second_yy * first_yy,
            earlier[4] + later[4],
            earlier[5] + later[5],
        ],
        0,
    )


def body(density_blocks, block_owner, block_place, lens_weights, ray_cells, ray_angles):
    slot_count = density_blocks.shape[0]
    block_side = density_blocks.shape[1]
    tile_side = 2 * block_side
    plane_count = lens_weights.shape[0]
    ray_count = ray_cells.shape[1]
    tile_count = lax.axis_size("tile")
    capacity = slot_count // tile_count
    live_mask = block_owner < tile_count
    entries = jnp.arange(slot_count, dtype=jnp.int32)
    same_owner = block_owner[:, None] == block_owner[None, :]
    before = entries[None, :] < entries[:, None]
    ranking = jnp.sum((same_owner & before).astype(jnp.int32), axis=1)
    destination = jnp.where(live_mask, block_owner * capacity + ranking, -1)
    chooser = destination[None, :] == entries[:, None]
    packed = (
        jnp.dot(
            chooser.astype(jnp.bfloat16),
            density_blocks.reshape(slot_count, -1),
            preferred_element_type=jnp.float32,
        )
        .astype(jnp.bfloat16)
        .reshape(density_blocks.shape)
    )
    slot_label = jnp.sum(jnp.where(chooser, block_place[None, :] + 1, 0), axis=1) - 1
    label_rows = jnp.broadcast_to(slot_label[:, None], (slot_count, block_side))
    tables = sine_table(tile_side)
    eigenvalues = eigen_table(tile_side)
    arrived, arrived_labels = (
        lax.all_to_all(packed, "tile", split_axis=0, concat_axis=0, tiled=True),
        lax.all_to_all(label_rows, "tile", split_axis=0, concat_axis=0, tiled=True),
    )
    labels = arrived_labels[:, 0]
    places = jnp.arange(4 * plane_count, dtype=jnp.int32)
    placing = (labels[None, :] == places[:, None]).astype(jnp.bfloat16)
    layout = jnp.dot(placing, arrived.reshape(slot_count, -1), preferred_element_type=jnp.float32)
    layout = layout.reshape(plane_count, 2, 2, block_side, block_side).transpose(0, 1, 3, 2, 4)
    layout = layout.reshape(plane_count, tile_side, tile_side)
    half_done = jnp.einsum("pij,jk->pik", layout, tables, precision=HIGHEST)
    spectrum = jnp.einsum("ij,pjk->pik", tables, half_done, precision=HIGHEST)
    scaled = 2.0 * spectrum / eigenvalues
    potential = jnp.einsum("ij,pjk,kl->pil", tables, scaled, tables, precision=HIGHEST)
    bordered = extended(potential, (("tile", 1),), 1)
    bordered = jnp.pad(bordered, ((0, 0), (0, 0), (1, 1)))
    fields = jnp.stack(derive_fields(bordered), axis=2).astype(jnp.bfloat16)
    columns = jnp.arange(tile_side, dtype=jnp.int32)
    unit_row = jnp.ones((ray_count,), jnp.float32)
    zero_row = jnp.zeros((ray_count,), jnp.float32)
    entry_xx, entry_xy, entry_yx, entry_yy = (unit_row, zero_row, zero_row, unit_row)
    angle_x, angle_y = (zero_row, zero_row)
    for plane_index in range(plane_count):
        cell_ids = ray_cells[plane_index]
        row_pick = ((cell_ids // tile_side)[:, None] == columns[None, :]).astype(jnp.bfloat16)
        col_pick = ((cell_ids % tile_side)[:, None] == columns[None, :]).astype(jnp.float32)
        gathered = jnp.dot(
            row_pick,
            fields[plane_index].reshape(tile_side, 5 * tile_side),
            preferred_element_type=jnp.float32,
        )
        sampled = jnp.sum(gathered.reshape(ray_count, 5, tile_side) * col_pick[:, None, :], axis=2)
        bend_x, bend_y = (sampled[:, 0], sampled[:, 1])
        convergence, shear_one, shear_two = (sampled[:, 2], sampled[:, 3], sampled[:, 4])
        plane_weight = lens_weights[plane_index]
        upper_diag = convergence + shear_one
        lower_diag = convergence - shear_one
        entry_xx, entry_xy, entry_yx, entry_yy = (
            entry_xx - plane_weight * (upper_diag * entry_xx + shear_two * entry_yx),
            entry_xy - plane_weight * (upper_diag * entry_xy + shear_two * entry_yy),
            entry_yx - plane_weight * (shear_two * entry_xx + lower_diag * entry_yx),
            entry_yy - plane_weight * (shear_two * entry_xy + lower_diag * entry_yy),
        )
        angle_x = angle_x - plane_weight * bend_x
        angle_y = angle_y - plane_weight * bend_y
    local_map = jnp.stack([entry_xx, entry_xy, entry_yx, entry_yy, angle_x, angle_y], 0)
    identity_map = jnp.stack([unit_row, zero_row, zero_row, unit_row, zero_row, zero_row], 0)
    incoming = carried_in(local_map, "depth", compose_maps, identity_map)
    combined = compose_maps(incoming, local_map)
    exit_rows = jnp.concatenate([combined[:4], combined[4:] + ray_angles], 0)
    return exit_rows[None]


def solution(mesh):
    return jax.shard_map(
        body,
        mesh=mesh,
        in_specs=(
            P(("depth", "tile"), None, None),
            P(("depth", "tile")),
            P(("depth", "tile")),
            P("depth"),
            P("depth", "tile"),
            P(None, "tile"),
        ),
        out_specs=P("depth", None, "tile"),
        check_vma=False,
    )
```

profile of v0, /device:TPU:0, one launch (start us, length us, event | category | flops | bytes accessed | tf_op | source)
XLA Modules:
  0.0 95.9 jit_solution(8430779862547650783)
XLA Ops:
  2.5 6.3 %all-to-all-start = ((s32[8,4,128]{2,1,0:T(4,128)}), s32[8,4,128]{2,1,0:T(4,128)S(1)}, u32[]{:S(2)}, u32[]{:S(2)}) async-start(s32[8,4,128]{2,1,0:T(4,128)} %broadcast_in_dim.30), calls=%async_computation | async-start | bytes 32768 | tf_op jit(solution)/shard_map/all_to_all | solution.py:115
  8.9 2.0 %fusion.15 = bf16[4,8,128,128]{3,1,2,0:T(8,128)(2,1)S(1)} fusion(bf16[4,8,128,128]{3,2,1,0:T(8,128)(2,1)} %bitcast.327, s32[32]{0:T(128)S(1)} %get-tuple-element.99), kind=kOutput, calls=%fused_computation.38 | convolution fusion | flops 34079744 | bytes 2097280 | tf_op jit(solution)/shard_map/dot_general | solution.py:101
  11.0 1.6 %fusion.7 = f32[2048,256]{0,1:T(8,128)} fusion(s32[2048]{0:T(1024)S(1)} %get-tuple-element.92), kind=kLoop, calls=%fused_computation.30 | loop fusion | flops 1048576 | bytes 2105344 | tf_op jit(solution)/shard_map/convert_element_type | solution.py:138
  12.6 1.3 %copy.48 = bf16[4,8,128,128]{3,2,1,0:T(8,128)(2,1)} copy(bf16[4,8,128,128]{3,1,2,0:T(8,128)(2,1)S(1)} %fusion.15) | data formatting | bytes 2097152
  14.5 4.6 %all-to-all-start.1 = ((bf16[32,128,128]{2,1,0:T(8,128)(2,1)}), bf16[32,128,128]{2,1,0:T(8,128)(2,1)S(1)}, u32[]{:S(2)}, u32[]{:S(2)}) async-start(bf16[32,128,128]{2,1,0:T(8,128)(2,1)} %bitcast.71), calls=%async_computation.1 | async-start | bytes 2097152 | tf_op jit(solution)/shard_map/all_to_all | solution.py:114
  19.1 1.6 %fusion.4 = f32[2048,256]{0,1:T(8,128)} fusion(s32[2048]{0:T(1024)S(1)} %get-tuple-element.90), kind=kLoop, calls=%fused_computation.28 | loop fusion | flops 1048576 | bytes 2105344 | tf_op jit(solution)/shard_map/convert_element_type | solution.py:138
  20.7 1.6 %fusion.10 = f32[2048,256]{0,1:T(8,128)} fusion(s32[2048]{0:T(1024)S(1)} %get-tuple-element.88), kind=kLoop, calls=%fused_computation.32 | loop fusion | flops 1048576 | bytes 2105344 | tf_op jit(solution)/shard_map/convert_element_type | solution.py:138
  22.2 1.6 %fusion.13 = f32[2048,256]{0,1:T(8,128)} fusion(s32[2048]{0:T(1024)S(1)} %get-tuple-element.94), kind=kLoop, calls=%fused_computation.34 | loop fusion | flops 1048576 | bytes 2105344 | tf_op jit(solution)/shard_map/convert_element_type | solution.py:138
  23.9 21.7 %all-to-all-done.1 = bf16[32,128,128]{2,1,0:T(8,128)(2,1)S(1)} async-done(((bf16[32,128,128]{2,1,0:T(8,128)(2,1)}), bf16[32,128,128]{2,1,0:T(8,128)(2,1)S(1)}, u32[]{:S(2)}, u32[]{:S(2)}) %all-to-all-start.1) | async-done | bytes 1048608 | tf_op jit(solution)/shard_map/all_to_all | solution.py:114
  49.0 2.0 %fusion.46 = f32[4,256,256]{1,2,0:T(8,128)S(1)} fusion(f32[4,256,256]{2,1,0:T(8,128)S(1)} %reshape.1240, f32[256]{0:T(256)S(1)} %get-tuple-element.101, f32[256]{0:T(256)S(1)} %get-tuple-element.102), kind=kOutput, calls=%fused_computation.83 | convolution fusion | flops 805502976 | bytes 2099200 | tf_op jit(solution)/shard_map/pij,jk->pik/dot_general | solution.py:123
  51.0 1.9 %fusion.17 = f32[4,256,256]{1,2,0:T(8,128)S(1)} fusion(f32[4,256,256]{1,2,0:T(8,128)S(1)} %fusion.46, f32[256,256]{0,1:T(8,128)S(1)} %add_negate_fusion, f32[256]{0:T(256)S(1)} %get-tuple-element.101, f32[256]{0:T(256)S(1)} %get-tuple-element.102), kind=kOutput, calls=%fused_computation.42 | convolution fusion | flops 806027264 | bytes 2361344 | tf_op jit(solution)/shard_map/ij,pjk->pik/dot_general | solution.py:124
  53.0 2.0 %fusion.43 = f32[4,256,256]{1,2,0:T(8,128)S(1)} fusion(f32[4,256,256]{1,2,0:T(8,128)S(1)} %fusion.17, f32[256]{0:T(256)S(1)} %get-tuple-element.101, f32[256]{0:T(256)S(1)} %get-tuple-element.102), kind=kOutput, calls=%fused_computation.80 | convolution fusion | flops 805502976 | bytes 2099200 | tf_op jit(solution)/shard_map/ij,pjk,kl->pil/dot_general | solution.py:126
  55.0 1.9 %fusion.41 = f32[4,256,256]{2,1,0:T(8,128)S(1)} fusion(f32[4,256,256]{1,2,0:T(8,128)S(1)} %fusion.43, f32[256]{0:T(256)S(1)} %get-tuple-element.101, f32[256]{0:T(256)S(1)} %get-tuple-element.102), kind=kOutput, calls=%fused_computation.78 | convolution fusion | flops 805502976 | bytes 2099200 | tf_op jit(solution)/shard_map/ij,pjk,kl->pil/dot_general | solution.py:126
  57.0 1.5 %collective-permute-start = (f32[4,1,256]{2,1,0:T(1,128)S(1)}, f32[4,1,256]{2,1,0:T(1,128)S(1)}, u32[]{:S(2)}, u32[]{:S(2)}) collective-permute-start(f32[4,1,256]{2,1,0:T(1,128)S(1)} %get-tuple-element.59), channel_id=1, source_target_pairs={{1,0},{2,1},{3,2},{4,3},{5,4},{6,5},{7,6},{9,8},{10,9},{11,10},{12... | collective-permute-start | bytes 12296 | tf_op jit(solution)/shard_map/ppermute | solution.py:19
  58.5 3.0 %collective-permute-start.1 = (f32[4,1,256]{2,1,0:T(1,128)S(1)}, f32[4,1,256]{2,1,0:T(1,128)S(1)}, u32[]{:S(2)}, u32[]{:S(2)}) collective-permute-start(f32[4,1,256]{2,1,0:T(1,128)S(1)} %get-tuple-element.60), channel_id=1, source_target_pairs={{0,1},{1,2},{2,3},{3,4},{4,5},{5,6},{6,7},{8,9},{9,10},{10,11},{11... | collective-permute-start | bytes 12296 | tf_op jit(solution)/shard_map/ppermute | solution.py:17
  67.9 1.1 %copy.38 = bf16[1,256,5,256]{1,3,2,0:T(8,128)(2,1)} copy(bf16[1,256,5,256]{3,1,0,2:T(8,128)(2,1)S(1)} %get-tuple-element.55) | data formatting | bytes 1310720 | tf_op jit(solution)/shard_map/slice | solution.py:141
  69.7 3.2 %multiply_reduce_fusion.2 = f32[2048,5]{0,1:T(8,128)S(1)} fusion(f32[2048,256]{0,1:T(8,128)S(1)} %copy-done, s32[2048]{0:T(1024)S(1)} %get-tuple-element.91, bf16[1,256,5,256]{1,3,2,0:T(8,128)(2,1)} %copy.37), kind=kOutput, calls=%fused_computation.15 | convolution fusion | flops 1347934208 | bytes 2801664 | tf_op jit(solution)/shard_map/dot_general | solution.py:139
  73.0 2.0 %multiply_reduce_fusion.3 = f32[2048,5]{0,1:T(8,128)S(1)} fusion(f32[2048,256]{0,1:T(8,128)S(1)} %copy-done.3, s32[2048]{0:T(1024)S(1)} %get-tuple-element.89, bf16[1,256,5,256]{1,3,2,0:T(8,128)(2,1)S(1)} %copy-done.6), kind=kOutput, calls=%fused_computation.16 | convolution fusion | flops 1347934208 | bytes 2801664 | tf_op jit(solution)/shard_map/dot_general | solution.py:139
  75.1 2.0 %multiply_reduce_fusion.1 = f32[2048,5]{0,1:T(8,128)S(1)} fusion(f32[2048,256]{0,1:T(8,128)S(1)} %copy-done.2, s32[2048]{0:T(1024)S(1)} %get-tuple-element.87, bf16[1,256,5,256]{1,3,2,0:T(8,128)(2,1)S(1)} %copy-done.5), kind=kOutput, calls=%fused_computation.14 | convolution fusion | flops 1347934208 | bytes 2801664 | tf_op jit(solution)/shard_map/dot_general | solution.py:139
  77.1 2.1 %multiply_reduce_fusion = f32[2048,5]{0,1:T(8,128)S(1)} fusion(f32[2048,256]{0,1:T(8,128)S(1)} %copy-done.1, s32[2048]{0:T(1024)S(1)} %get-tuple-element.93, bf16[1,256,5,256]{1,3,2,0:T(8,128)(2,1)S(1)} %copy.39), kind=kOutput, calls=%fused_computation.13 | convolution fusion | flops 1347934208 | bytes 2801664 | tf_op jit(solution)/shard_map/dot_general | solution.py:139
  79.2 1.3 %fusion.93 = (f32[1,2048]{1,0:T(1,128)S(1)}, f32[1,2048]{1,0:T(1,128)S(1)}, f32[1,2048]{1,0:T(1,128)S(1)}, f32[1,2048]{1,0:T(1,128)S(1)}, f32[1,2048]{1,0:T(1,128)S(1)}, /*index=5*/f32[1,2048]{1,0:T(1,128)S(1)}) fusion(f32[]{:T(128)} %bitcast.27, f32[2048,5]{0,1:T(8,128)S(1)} %multiply_reduce_fusion.2, f32[2048,5]{0,1:T(8,128)S(1)} %multiply_reduce_fusion.3, ...), kind=kLoop, calls=%fused_computation.178 | loop fusion | flops 57344 | bytes 98312 | tf_op jit(solution)/shard_map/sub | solution.py:153
  81.2 2.6 %fusion.127 = (f32[1,2048]{1,0:T(1,128)S(1)}, f32[1,2048]{1,0:T(1,128)S(1)}) fusion(f32[2048,5]{0,1:T(8,128)S(1)} %multiply_reduce_fusion, f32[2048,5]{0,1:T(8,128)S(1)} %multiply_reduce_fusion.1, f32[2048,5]{0,1:T(8,128)S(1)} %multiply_reduce_fusion.2, f32[2048,5]{0,1:T(8,128)S(1)} %multiply_reduce_fusion.3, f32[]{:T(128)} %bitcast.45, f32[]{:T(128)} %bitcast.36, ...), kind=kLoop, calls=%fused_computation.230 | loop fusion | flops 32768 | bytes 81936 | tf_op jit(solution)/shard_map/sub | solution.py:157
  83.7 1.4 %fusion.75 = (f32[1,2048]{1,0:T(1,128)S(1)}, f32[1,2048]{1,0:T(1,128)S(1)}, f32[1,2048]{1,0:T(1,128)S(1)}, f32[1,2048]{1,0:T(1,128)S(1)}, f32[1,2048]{1,0:T(1,128)S(1)}, /*index=5*/f32[1,2048]{1,0:T(1,128)S(1)}) fusion(f32[]{:T(128)} %bitcast.45, f32[2048,5]{0,1:T(8,128)S(1)} %multiply_reduce_fusion, f32[1,2048]{1,0:T(1,128)S(1)} %get-tuple-element.43, ...), kind=kLoop, calls=%fused_computation.154 | loop fusion | flops 67584 | bytes 131080 | tf_op jit(solution)/shard_map/sub | solution.py:153
  85.9 9.2 %all-gather.1 = f32[4,6,2048]{2,1,0:T(8,128)S(1)} all-gather(f32[1,6,2048]{2,1,0:T(8,128)S(1)} %bitcast.328), channel_id=2, replica_groups=mesh['depth'=4,'tile'=8] {'depth'}, dimensions={0}, use_global_device_ids=true | all-gather | bytes 245760 | tf_op jit(solution)/shard_map/all_gather | solution.py:28
  (64 shorter events, 15.9 us)
Async XLA Ops:
  0.0 10.9 %copy-start.7 = (s32[4,2048]{1,0:T(4,128)S(1)}, s32[4,2048]{1,0:T(4,128)}, u32[]{:S(2)}) copy-start(s32[4,2048]{1,0:T(4,128)} %param.12) | copy-start | bytes 98308
  2.5 12.0 %all-to-all-start = ((s32[8,4,128]{2,1,0:T(4,128)}), s32[8,4,128]{2,1,0:T(4,128)S(1)}, u32[]{:S(2)}, u32[]{:S(2)}) async-start(s32[8,4,128]{2,1,0:T(4,128)} %broadcast_in_dim.30), calls=%async_computation | async-start | bytes 32768 | tf_op jit(solution)/shard_map/all_to_all | solution.py:115
  14.5 31.2 %all-to-all-start.1 = ((bf16[32,128,128]{2,1,0:T(8,128)(2,1)}), bf16[32,128,128]{2,1,0:T(8,128)(2,1)S(1)}, u32[]{:S(2)}, u32[]{:S(2)}) async-start(bf16[32,128,128]{2,1,0:T(8,128)(2,1)} %bitcast.71), calls=%async_computation.1 | async-start | bytes 2097152 | tf_op jit(solution)/shard_map/all_to_all | solution.py:114
  53.0 8.5 %copy-start.9 = (f32[4]{0:T(128)S(1)}, f32[4]{0:T(128)}, u32[]{:S(2)}) copy-start(f32[4]{0:T(128)} %param.11) | copy-start | bytes 52
  57.0 5.2 %collective-permute-start = (f32[4,1,256]{2,1,0:T(1,128)S(1)}, f32[4,1,256]{2,1,0:T(1,128)S(1)}, u32[]{:S(2)}, u32[]{:S(2)}) collective-permute-start(f32[4,1,256]{2,1,0:T(1,128)S(1)} %get-tuple-element.59), channel_id=1, source_target_pairs={{1,0},{2,1},{3,2},{4,3},{5,4},{6,5},{7,6},{9,8},{10,9},{11,10},{12... | collective-permute-start | bytes 12296 | tf_op jit(solution)/shard_map/ppermute | solution.py:19
  58.5 3.8 %collective-permute-start.1 = (f32[4,1,256]{2,1,0:T(1,128)S(1)}, f32[4,1,256]{2,1,0:T(1,128)S(1)}, u32[]{:S(2)}, u32[]{:S(2)}) collective-permute-start(f32[4,1,256]{2,1,0:T(1,128)S(1)} %get-tuple-element.60), channel_id=1, source_target_pairs={{0,1},{1,2},{2,3},{3,4},{4,5},{5,6},{6,7},{8,9},{9,10},{10,11},{11... | collective-permute-start | bytes 12296 | tf_op jit(solution)/shard_map/ppermute | solution.py:17
  67.9 1.8 %copy-start = (f32[2048,256]{0,1:T(8,128)S(1)}, f32[2048,256]{0,1:T(8,128)}, u32[]{:S(2)}) copy-start(f32[2048,256]{0,1:T(8,128)} %fusion.7) | copy-start | bytes 6291460
  69.7 3.3 %copy-start.3 = (f32[2048,256]{0,1:T(8,128)S(1)}, f32[2048,256]{0,1:T(8,128)}, u32[]{:S(2)}) copy-start(f32[2048,256]{0,1:T(8,128)} %fusion.4) | copy-start | bytes 6291460
  69.7 3.3 %copy-start.6 = (bf16[1,256,5,256]{1,3,2,0:T(8,128)(2,1)S(1)}, bf16[1,256,5,256]{1,3,2,0:T(8,128)(2,1)}, u32[]{:S(2)}) copy-start(bf16[1,256,5,256]{1,3,2,0:T(8,128)(2,1)} %copy.36) | copy-start | bytes 1966084
  73.0 2.1 %copy-start.2 = (f32[2048,256]{0,1:T(8,128)S(1)}, f32[2048,256]{0,1:T(8,128)}, u32[]{:S(2)}) copy-start(f32[2048,256]{0,1:T(8,128)} %fusion.10) | copy-start | bytes 6291460
  73.0 2.1 %copy-start.5 = (bf16[1,256,5,256]{1,3,2,0:T(8,128)(2,1)S(1)}, bf16[1,256,5,256]{1,3,2,0:T(8,128)(2,1)}, u32[]{:S(2)}) copy-start(bf16[1,256,5,256]{1,3,2,0:T(8,128)(2,1)} %copy.38) | copy-start | bytes 1966084
  75.0 2.1 %copy-start.1 = (f32[2048,256]{0,1:T(8,128)S(1)}, f32[2048,256]{0,1:T(8,128)}, u32[]{:S(2)}) copy-start(f32[2048,256]{0,1:T(8,128)} %fusion.13) | copy-start | bytes 6291460
  77.1 18.0 %copy-start.4 = (f32[6,2048]{1,0:T(8,128)S(1)}, f32[6,2048]{1,0:T(8,128)}, u32[]{:S(2)}) copy-start(f32[6,2048]{1,0:T(8,128)} %constant.115.clone.1) | copy-start | bytes 147460
  79.2 15.9 %copy-start.8 = (f32[2,2048]{1,0:T(2,128)S(1)}, f32[2,2048]{1,0:T(2,128)}, u32[]{:S(2)}) copy-start(f32[2,2048]{1,0:T(2,128)} %param.13) | copy-start | bytes 49156
where the time goes:
time: 96.6 us; the launch traced here: 95.9 us
  waiting for transfers between devices  22.4 us (23%)
  matrix products  20 us (21%)
  other arithmetic  18 us (19%)
  starting transfers between devices  15.4 us (16%)
  local copies, waits for them, and re-layouts  10.5 us (11%)
  blocking collectives  9.18 us (10%)
    all_to_all x1, waiting for transfers between devices, body(): lax.all_to_all(packed, 'tile', split_axis=0, concat_axis=0, tiled=True)  21.7 us
    dot_general x4, matrix products, body(): jnp.dot(row_pick, fields[plane_index].reshape(tile_side, 5 * tile_side),...  9.39 us
    all_gather x1, blocking collectives, carried_in(): gathered = lax.all_gather(part, axis)  9.18 us
    all_to_all x1, starting transfers between devices, body(): lax.all_to_all(label_rows, 'tile', split_axis=0, concat_axis=0, tiled=True)  6.33 us
    convert_element_type x4, other arithmetic, body(): ((cell_ids % tile_side)[:, None] == columns[None, :]).astype(jnp.float32)  6.31 us
    all_to_all x1, starting transfers between devices, body(): lax.all_to_all(packed, 'tile', split_axis=0, concat_axis=0, tiled=True)  4.57 us
    dot_general x2, matrix products, body(): jnp.einsum('ij,pjk,kl->pil', tables, scaled, tables, precision=HIGHEST)  3.98 us
    slice x5, local copies, waits for them, and re-layouts, body(): fields[plane_index].reshape(tile_side, 5 * tile_side)  3.67 us
  transfers between devices with their start and end apart: 4, of which 3 were waited for; matrix products, arithmetic and copies ran while one was open for 11% of the time, Pallas kernels for 0%

commit v1 on v0

v1 whole, which is shorter than its diff:
```python
import functools

import jax
import jax.numpy as jnp
import ml_dtypes
import numpy as np
from jax import lax
from jax.experimental import pallas as pl
from jax.experimental.pallas import tpu as pltpu
from jax.sharding import PartitionSpec as P

F32 = jnp.float32
BF16 = jnp.bfloat16
LANES = 128
VMEM = pl.BlockSpec(memory_space=pltpu.VMEM)
SMEM = pl.BlockSpec(memory_space=pltpu.SMEM)


def call(kernel, outs, in_specs, scratch=(), limit=48, flops=0, moved=0):
    return pl.pallas_call(
        kernel,
        out_shape=outs,
        in_specs=in_specs,
        out_specs=jax.tree.map(lambda _: VMEM, outs),
        scratch_shapes=list(scratch),
        compiler_params=pltpu.CompilerParams(vmem_limit_bytes=limit << 20),
        cost_estimate=pl.CostEstimate(flops=flops, bytes_accessed=moved, transcendentals=0),
    )


def mul(a, b):
    return jnp.dot(a, b, preferred_element_type=F32)


def halves(a):
    high = a.astype(BF16)
    return high, (a - high.astype(F32)).astype(BF16)


def label_rows(capacity):
    return -(-capacity // 16) * 16


def tables(side):
    index = np.arange(side, dtype=np.float64) + 1.0
    sines = np.sqrt(2.0 / (side + 1.0)) * np.sin(np.pi * index[:, None] * index[None, :] / (side + 1.0))
    high = sines.astype(np.float32).astype(ml_dtypes.bfloat16)
    low = (sines - high.astype(np.float64)).astype(np.float32).astype(ml_dtypes.bfloat16)
    single = 2.0 - 2.0 * np.cos(np.pi * index / (side + 1.0))
    inverse = -2.0 / (single[:, None] + single[None, :])
    across = np.concatenate([high, high, low], axis=1)
    down = np.concatenate([high, high, low], axis=0)
    return across, down, np.concatenate([high, low], axis=0), inverse.astype(np.float32)


def pack_kernel(tile_count, capacity, tile_ref, owner_ref, place_ref, blocks_ref, *rest):
    outs, slot_ref, count_ref = rest[:tile_count], rest[-2], rest[-1]
    slots, side = blocks_ref.shape[0], blocks_ref.shape[1]
    spare = tile_count * capacity
    tile = tile_ref[0]
    for x in range(tile_count + 1):
        count_ref[x] = 0
    for i in range(spare):
        slot_ref[i] = -1
    for e in range(slots):
        owner = owner_ref[e]
        live = owner < tile_count
        chunk = jnp.where(live, owner ^ tile, tile_count)
        count = count_ref[chunk]
        count_ref[chunk] = count + 1
        slot_ref[jnp.where(live, chunk * capacity + count, spare + e)] = e
    rows = label_rows(capacity)
    row = lax.broadcasted_iota(jnp.int32, (rows, side), 0)
    for x in range(tile_count):
        labels = jnp.full((rows, side), -1, jnp.int32)
        for c in range(capacity):
            entry = slot_ref[x * capacity + c]
            safe = jnp.maximum(entry, 0)
            label = jnp.where(entry >= 0, place_ref[safe], -1)
            outs[x][pl.ds(c * side, side), :] = blocks_ref[safe]
            labels = jnp.where(row == c, label, labels)
        outs[x][pl.ds(capacity * side, rows), :] = labels.astype(F32).astype(BF16)


def solve_kernel(capacity, planes, *refs):
    across_ref, down_ref, pair_ref, inverse_ref = refs[:4]
    chunks, (p_ref, c_ref, edge_ref) = refs[4:-3], refs[-3:]
    side = chunks[0].shape[1]
    c_ref[...] = jnp.zeros(c_ref.shape, BF16)
    rows = label_rows(capacity)
    for chunk in chunks:
        labels = chunk[pl.ds(capacity * side, rows), :].astype(F32).astype(jnp.int32)
        for c in range(capacity):
            label = labels[c, 0]

            @pl.when(label >= 0)
            def _():
                top = pl.multiple_of(((label >> 1) & 1) * side, side)
                left = pl.multiple_of((label & 1) * side, side)
                c_ref[label >> 2, pl.ds(top, side), pl.ds(left, side)] = chunk[pl.ds(c * side, side), :]

    across, down, pair, inverse = across_ref[...], down_ref[...], pair_ref[...], inverse_ref[...]
    for k in range(planes):
        mass = c_ref[k]
        half = mul(jnp.concatenate([mass, mass], axis=1), pair)
        high, low = halves(half)
        spectrum = mul(across, jnp.concatenate([high, low, high], axis=0)) * inverse
        high, low = halves(spectrum)
        half = mul(jnp.concatenate([high, low, high], axis=1), down)
        high, low = halves(half)
        potential = mul(across, jnp.concatenate([high, low, high], axis=0))
        p_ref[k] = potential
        edge_ref[pl.ds(k, 1), :] = potential[:1]
        edge_ref[pl.ds(planes + k, 1), :] = potential[2 * side - 1 :]


def shifted(a, axis, step):
    size = a.shape[axis]
    place = lax.broadcasted_iota(jnp.int32, a.shape, axis)
    edge = size - 1 if step > 0 else 0
    return jnp.where(place == edge, 0.0, pltpu.roll(a, (-step) % size, axis))


def pick_kernel(planes, p_ref, c_ref, cells_ref, out_ref):
    side = p_ref.shape[1]
    shift = side.bit_length() - 1
    groups = cells_ref.shape[0] // planes
    width = 2 if groups % 2 == 0 else 1
    sub = lax.broadcasted_iota(jnp.int32, (8, width * LANES), 0)
    column = lax.broadcasted_iota(jnp.int32, (side, width * LANES), 0)
    for k in range(planes):
        p = p_ref[k]
        above, below = shifted(p, 0, -1), shifted(p, 0, 1)
        left, right = shifted(p, 1, -1), shifted(p, 1, 1)
        slope = 0.5 * (below - above)
        fields = (
            slope.astype(BF16),
            (0.5 * (right - left)).astype(BF16),
            c_ref[k],
            (0.5 * ((below + above) - (right + left))).astype(BF16),
            (0.5 * (shifted(slope, 1, 1) - shifted(slope, 1, -1))).astype(BF16),
        )
        for g in range(0, groups, width):
            cells = jnp.concatenate([cells_ref[pl.ds(k * groups + g + w, 1), :] for w in range(width)], axis=1)
            row, col = cells >> shift, cells & (side - 1)
            chosen = (column == col).astype(F32).astype(BF16)
            block, within = row >> 3, sub == (row & 7)
            for f in range(5):
                picked = mul(fields[f], chosen)
                kept = picked[:8]
                for v in range(1, side // 8):
                    kept = jnp.where(block == v, picked[v * 8 : v * 8 + 8], kept)
                value = jnp.sum(jnp.where(within, kept, 0.0), axis=0, keepdims=True)
                for w in range(width):
                    out_ref[pl.ds((k * 5 + f) * groups + g + w, 1), :] = value[:, w * LANES : (w + 1) * LANES]


def taken(table, index):
    parts = table.shape[1] // LANES
    rows = index.shape[0]
    lane, part = index & (LANES - 1), index >> 7
    out = None
    for i in range(parts):
        spread = jnp.broadcast_to(table[:, i * LANES : (i + 1) * LANES], (rows, LANES))
        got = jnp.take_along_axis(spread, lane, axis=1, mode="promise_in_bounds")
        out = got if out is None else jnp.where(part == i, got, out)
    return out


def combine_kernel(planes, side, tile_ref, weights_ref, one_ref, two_ref, cells_ref, first_ref, second_ref, out_ref):
    groups = cells_ref.shape[0] // planes
    shift = side.bit_length() - 1
    even = (tile_ref[0] & 1) == 0
    axx = ayy = jnp.ones((groups, LANES), F32)
    axy = ayx = bx = by = jnp.zeros((groups, LANES), F32)
    for k in range(planes):
        cells = cells_ref[pl.ds(k * groups, groups), :]
        row, col = cells >> shift, cells & (side - 1)
        first, second = first_ref[pl.ds(k, 1), :], second_ref[pl.ds(k, 1), :]
        above, below = jnp.where(even, second, first), jnp.where(even, first, second)
        at_top, at_end = row == 0, row == side - 1
        up, down = taken(above, col), taken(below, col)
        up_x = taken(shifted(above, 1, 1) - shifted(above, 1, -1), col)
        down_x = taken(shifted(below, 1, 1) - shifted(below, 1, -1), col)
        near = jnp.where(at_top, up, 0.0)
        far = jnp.where(at_end, down, 0.0)
        cross = 0.25 * (jnp.where(at_end, down_x, 0.0) - jnp.where(at_top, up_x, 0.0))

        def read(f):
            at = pl.ds((k * 5 + f) * groups, groups)
            return one_ref[at, :] + two_ref[at, :]

        weight = weights_ref[k]
        bend_x, bend_y = read(0) + 0.5 * (far - near), read(1)
        extra = 0.5 * (far + near)
        kappa, shear, mixed = read(2) + extra, read(3) + extra, read(4) + cross
        upper, lower = weight * (kappa + shear), weight * (kappa - shear)
        mixed = weight * mixed
        axx, ayx = axx - (upper * axx + mixed * ayx), ayx - (mixed * axx + lower * ayx)
        axy, ayy = axy - (upper * axy + mixed * ayy), ayy - (mixed * axy + lower * ayy)
        bx, by = bx - weight * bend_x, by - weight * bend_y
    for i, value in enumerate((axx, axy, ayx, ayy, bx, by)):
        out_ref[pl.ds(i * groups, groups), :] = value


def compose_kernel(depth_ref, maps_ref, angles_ref, out_ref):
    count = maps_ref.shape[0]
    groups = maps_ref.shape[1] // 6
    depth = depth_ref[0]

    def part(d, i):
        return maps_ref[d, pl.ds(i * groups, groups), :]

    xx, xy, yx, yy, bx, by = (part(0, i) for i in range(6))
    for d in range(1, count):
        used = d <= depth
        mxx, mxy, myx, myy, mbx, mby = (part(d, i) for i in range(6))
        nxx, nxy = mxx * xx + mxy * yx, mxx * xy + mxy * yy
        nyx, nyy = myx * xx + myy * yx, myx * xy + myy * yy
        new = (nxx, nxy, nyx, nyy, bx + mbx, by + mby)
        xx, xy, yx, yy, bx, by = (jnp.where(used, a, b) for a, b in zip(new, (xx, xy, yx, yy, bx, by)))
    bx = bx + angles_ref[pl.ds(0, groups), :]
    by = by + angles_ref[pl.ds(groups, groups), :]
    for i, value in enumerate((xx, xy, yx, yy, bx, by)):
        for g in range(groups):
            out_ref[0, pl.ds(i, 1), pl.ds(g * LANES, LANES)] = value[g : g + 1]


def body(density_blocks, block_owner, block_place, lens_weights, ray_cells, ray_angles):
    slots, block_side = density_blocks.shape[:2]
    side = 2 * block_side
    planes, rays = ray_cells.shape
    groups = rays // LANES
    tile_count = lax.axis_size("tile")
    capacity = slots // tile_count
    half = tile_count // 2
    tile = lax.axis_index("tile").astype(jnp.int32).reshape(1)
    depth = lax.axis_index("depth").astype(jnp.int32).reshape(1)
    across, down, pair, inverse = (jnp.asarray(t) for t in tables(side))
    cells = ray_cells.reshape(planes * groups, LANES)
    angles = ray_angles.reshape(2 * groups, LANES)

    def swap(array, bits):
        return lax.ppermute(array, "tile", [(i, i ^ bits) for i in range(tile_count)])

    rows = capacity * block_side + label_rows(capacity)
    chunks = call(
        functools.partial(pack_kernel, tile_count, capacity),
        [jax.ShapeDtypeStruct((rows, block_side), BF16)] * tile_count,
        [SMEM, SMEM, SMEM, VMEM],
        [pltpu.SMEM((tile_count * capacity + slots,), jnp.int32), pltpu.SMEM((tile_count + 1,), jnp.int32)],
        moved=2 * density_blocks.size * 2,
    )(tile, block_owner, block_place, density_blocks)
    order = list(range(2, half)) + [1] if half > 1 else []
    theirs = [chunks[half]] + [swap(chunks[s + half], s) for s in order]
    ours = [chunks[0]] + [swap(chunks[s], s) for s in order]
    their_cells = swap(cells, half)

    def solve(received):
        return call(
            functools.partial(solve_kernel, capacity, planes),
            [
                jax.ShapeDtypeStruct((planes, side, side), F32),
                jax.ShapeDtypeStruct((planes, side, side), BF16),
                jax.ShapeDtypeStruct((2 * planes, side), F32),
            ],
            [VMEM] * (4 + half),
            flops=2 * 11 * planes * side**3,
        )(across, down, pair, inverse, *received)

    def pick(potential, mass, at):
        return call(
            functools.partial(pick_kernel, planes),
            [jax.ShapeDtypeStruct((planes * 5 * groups, LANES), F32)],
            [VMEM] * 3,
            flops=2 * 5 * planes * side * side * rays,
        )(potential, mass, at)[0]

    potential, mass, their_edges = solve(theirs)
    other_edges = swap(their_edges, half)
    other_samples = swap(pick(potential, mass, their_cells), half)
    potential, mass, our_edges = solve(ours)
    edges = our_edges + other_edges
    even = tile[0] % 2 == 0
    top, end = edges[:planes], edges[planes:]
    first = swap(jnp.where(even, end, top), 1)
    pairs = [(i, i + 1) for i in range(1, tile_count - 1, 2)]
    second = lax.ppermute(jnp.where(even, top, end), "tile", pairs + [(j, i) for i, j in pairs])
    own_samples = pick(potential, mass, cells)
    local_map = call(
        functools.partial(combine_kernel, planes, side),
        [jax.ShapeDtypeStruct((6 * groups, LANES), F32)],
        [SMEM, SMEM, VMEM, VMEM, VMEM, VMEM, VMEM],
    )(tile, lens_weights, own_samples, other_samples, cells, first, second)[0]
    maps = lax.all_gather(local_map, "depth")
    return call(
        compose_kernel,
        [jax.ShapeDtypeStruct((1, 6, rays), F32)],
        [SMEM, VMEM, VMEM],
    )(depth, maps, angles)[0]


def solution(mesh):
    return jax.shard_map(
        body,
        mesh=mesh,
        in_specs=(
            P(("depth", "tile"), None, None),
            P(("depth", "tile")),
            P(("depth", "tile")),
            P("depth"),
            P("depth", "tile"),
            P(None, "tile"),
        ),
        out_specs=P("depth", None, "tile"),
        check_vma=False,
    )
```

time: 96.6 us -> 57 us (0.59)
  Pallas kernels: 0 us -> 23.9 us
  matrix products: 20 us -> 0 us
  other arithmetic: 18 us -> 0.01 us
  waiting for transfers between devices: 22.4 us -> 7.61 us
  local copies, waits for them, and re-layouts: 10.5 us -> 4.35 us
  starting transfers between devices: 15.4 us -> 11.5 us
    pallas_call x0 -> x7, Pallas kernels: none -> 23.9 us  [the longest x2 13.9 us: pick(): call(functools.partial(pick_kernel, planes), [jax.ShapeDtypeStruct((plane...]
    all_to_all x2 -> x0, waiting for transfers between devices: 22.3 us -> none  [the longest x1 21.7 us: body(): lax.all_to_all(packed, 'tile', split_axis=0, concat_axis=0, tiled=True)]
    dot_general x10 -> x0, matrix products: 20 us -> none  [the longest x4 9.39 us: body(): jnp.dot(row_pick, fields[plane_index].reshape(tile_side, 5 * tile_side),...]
    all_to_all x2 -> x0, starting transfers between devices: 10.9 us -> none  [the longest x1 6.33 us: body(): lax.all_to_all(label_rows, 'tile', split_axis=0, concat_axis=0, tiled=True)]
    ppermute x2 -> x11, waiting for transfers between devices: 0.13 us -> 7.61 us  [the longest x10 7.61 us: swap(): lax.ppermute(array, 'tile', [(i, i ^ bits) for i in range(tile_count)])]
    ppermute x2 -> x11, starting transfers between devices: 4.5 us -> 11.5 us  [the longest x10 10.9 us: swap(): lax.ppermute(array, 'tile', [(i, i ^ bits) for i in range(tile_count)])]
    sub x7 -> x0, other arithmetic: 6.58 us -> none  [the longest x2 2.7 us: body(): entry_yx - plane_weight * (shear_two * entry_xx + lower_diag * entry_yx)]
    convert_element_type x4 -> x0, other arithmetic: 6.31 us -> none  [body(): ((cell_ids % tile_side)[:, None] == columns[None, :]).astype(jnp.float32)]
  transfers between devices with their start and end apart: 4 -> 11, of which waited for: 3 -> 3; matrix products, arithmetic and copies ran while one was open for 11% -> 1% of each run, Pallas kernels for 0% -> 39%
where the time goes in v1:
time: 57 us; the launch traced here: 56.8 us
  Pallas kernels  23.9 us (42%)
  starting transfers between devices  11.5 us (20%)
  blocking collectives  9.18 us (16%)
  waiting for transfers between devices  7.61 us (13%)
  local copies, waits for them, and re-layouts  4.35 us (8%)
    pallas_call x2, Pallas kernels, pick(): call(functools.partial(pick_kernel, planes), [jax.ShapeDtypeStruct((plane...  13.9 us
    ppermute x10, starting transfers between devices, swap(): lax.ppermute(array, 'tile', [(i, i ^ bits) for i in range(tile_count)])  10.9 us
    all_gather x1, blocking collectives, body(): maps = lax.all_gather(local_map, 'depth')  9.18 us
    pallas_call x2, Pallas kernels, solve(): call(functools.partial(solve_kernel, capacity, planes), [jax.ShapeDtypeSt...  8.34 us
    ppermute x10, waiting for transfers between devices, swap(): lax.ppermute(array, 'tile', [(i, i ^ bits) for i in range(tile_count)])  7.61 us
    unnamed x20, local copies, waits for them, and re-layouts  2.87 us
  transfers between devices with their start and end apart: 11, of which 3 were waited for; matrix products, arithmetic and copies ran while one was open for 1% of the time, Pallas kernels for 39%

profile of v1, /device:TPU:0, one launch (start us, length us, event | category | flops | bytes accessed | tf_op | source)
XLA Modules:
  0.0 56.8 jit_solution(3075631931955507319)
XLA Ops:
  0.0 0.7 %copy-done.1 = s32[32]{0:T(128)S(1)} copy-done((s32[32]{0:T(128)S(1)}, s32[32]{0:T(128)}, u32[]{:S(2)}) %copy-start.1) | copy-done | bytes 152
  0.7 0.0 copy-done.2
  0.7 1.2 %copy-done = bf16[32,128,128]{2,1,0:T(8,128)(2,1)S(1)} copy-done((bf16[32,128,128]{2,1,0:T(8,128)(2,1)S(1)}, bf16[32,128,128]{2,1,0:T(8,128)(2,1)}, u32[]{:S(2)}) %copy-start) | copy-done | bytes 1048600
  1.9 0.8 %shard_map.100 = (bf16[528,128]{1,0:T(8,128)(2,1)S(1)}, bf16[528,128]{1,0:T(8,128)(2,1)S(1)}, bf16[528,128]{1,0:T(8,128)(2,1)S(1)}, bf16[528,128]{1,0:T(8,128)(2...) custom-call(s32[1]{0:T(128)} %bitcast.1.tile_ref, ...), custom_call_target="tpu_custom_call" | custom-call | bytes 2097152 | tf_op jit(solution)/shard_map/pallas_call | solution.py:247
  2.7 3.1 %collective-permute-start.3 = (bf16[528,128]{1,0:T(8,128)(2,1)S(1)}, bf16[528,128]{1,0:T(8,128)(2,1)S(1)}, u32[]{:S(2)}, u32[]{:S(2)}) collective-permute-start(bf16[528,128]{1,0:T(8,128)(2,1)S(1)} %get-tuple-element.26), channel_id=1, source_target_pairs={{0,2},{1,3},{2,0},{3,1},{4,6},{5,7},{6,4},{7,5},{8,10},{9,11},{10,... | collective-permute-start | bytes 405512 | tf_op jit(solution)/shard_map/ppermute | solution.py:244
  5.8 0.2 collective-permute-start.5
  6.0 1.9 %collective-permute-start = (bf16[528,128]{1,0:T(8,128)(2,1)S(1)}, bf16[528,128]{1,0:T(8,128)(2,1)S(1)}, u32[]{:S(2)}, u32[]{:S(2)}) collective-permute-start(bf16[528,128]{1,0:T(8,128)(2,1)S(1)} %get-tuple-element.20), channel_id=1, source_target_pairs={{0,2},{1,3},{2,0},{3,1},{4,6},{5,7},{6,4},{7,5},{8,10},{9,11},{10,... | collective-permute-start | bytes 405512 | tf_op jit(solution)/shard_map/ppermute | solution.py:244
  7.9 0.8 %reshape.14.cells_ref = s32[64,128]{1,0:T(8,128)S(1)} reshape(s32[4,2048]{1,0:T(4,128)} %param.14) | data formatting | bytes 65536 | tf_op jit(solution)/shard_map/reshape | solution.py:240
  8.8 1.1 %collective-permute-done.3.refs_5_ = bf16[528,128]{1,0:T(8,128)(2,1)S(1)} collective-permute-done((bf16[528,128]{1,0:T(8,128)(2,1)S(1)}, bf16[528,128]{1,0:T(8,128)(2,1)S(1)}, u32[]{:S(2)}, u32[]{:S(2)}) %collective-permute-start.3) | collective-permute-done | bytes 135200 | tf_op jit(solution)/shard_map/ppermute | solution.py:244
  9.9 2.8 %collective-permute-done.4.refs_6_ = bf16[528,128]{1,0:T(8,128)(2,1)S(1)} collective-permute-done((bf16[528,128]{1,0:T(8,128)(2,1)S(1)}, bf16[528,128]{1,0:T(8,128)(2,1)S(1)}, u32[]{:S(2)}, u32[]{:S(2)}) %collective-permute-start.4) | collective-permute-done | bytes 135200 | tf_op jit(solution)/shard_map/ppermute | solution.py:244
  12.7 2.6 %collective-permute-start.6 = (s32[64,128]{1,0:T(8,128)S(1)}, s32[64,128]{1,0:T(8,128)S(1)}, u32[]{:S(2)}, u32[]{:S(2)}) collective-permute-start(s32[64,128]{1,0:T(8,128)S(1)} %reshape.14.cells_ref), channel_id=1, source_target_pairs={{0,4},{1,5},{2,6},{3,7},{4,0},{5,1},{6,2},{7,3},{8,12},{9,13},{10,... | collective-permute-start | bytes 98312 | tf_op jit(solution)/shard_map/ppermute | solution.py:244
  15.3 0.9 %copy-done.7 = f32[256,256]{1,0:T(8,128)S(1)} copy-done((f32[256,256]{1,0:T(8,128)S(1)}, f32[256,256]{1,0:T(8,128)}, u32[]{:S(2)}) %copy-start.7) | copy-done | bytes 262168
  16.2 4.1 %shard_map.103 = (f32[4,256,256]{2,1,0:T(8,128)S(1)}, bf16[4,256,256]{2,1,0:T(8,128)(2,1)S(1)}, f32[8,256]{1,0:T(8,128)S(1)}) custom-call(bf16[256,768]{1,0:T(8,128)(2,1)S(1)} %copy-done.4, bf16[768,256]{1,0:T(8,128)(2,1)S(1)} %copy-done.5, bf16[512,256]{1,0:T(8,128)(2,1)S(1)} %copy-done.6, f32[256,256]{1,0:T(8,128)S(1)} %copy-done.7, ...), custom_call_target="tpu_custom_call" | custom-call | flops 1476395008 | tf_op jit(solution)/shard_map/pallas_call | solution.py:260
  20.4 6.9 %shard_map.104 = f32[320,128]{1,0:T(8,128)S(1)} custom-call(f32[4,256,256]{2,1,0:T(8,128)S(1)} %get-tuple-element.29.p_ref, bf16[4,256,256]{2,1,0:T(8,128)(2,1)S(1)} %get-tuple-element.30.c_ref, s32[64,128]{1,0:T(8,128)S(1)} %collective-permute-done.6.cells_ref), custom_call_target="tpu_custom_call" | custom-call | flops 5368709120 | tf_op jit(solution)/shard_map/pallas_call | solution.py:272
  27.3 1.1 %collective-permute-start.7 = (f32[320,128]{1,0:T(8,128)S(1)}, f32[320,128]{1,0:T(8,128)S(1)}, u32[]{:S(2)}, u32[]{:S(2)}) collective-permute-start(f32[320,128]{1,0:T(8,128)S(1)} %shard_map.104), channel_id=1, source_target_pairs={{0,4},{1,5},{2,6},{3,7},{4,0},{5,1},{6,2},{7,3},{8,12},{9,13},{10,... | collective-permute-start | bytes 491528 | tf_op jit(solution)/shard_map/ppermute | solution.py:244
  28.4 1.9 %collective-permute-start.8 = (f32[8,256]{1,0:T(8,128)S(1)}, f32[8,256]{1,0:T(8,128)S(1)}, u32[]{:S(2)}, u32[]{:S(2)}) collective-permute-start(f32[8,256]{1,0:T(8,128)S(1)} %get-tuple-element.32), channel_id=1, source_target_pairs={{0,4},{1,5},{2,6},{3,7},{4,0},{5,1},{6,2},{7,3},{8,12},{9,13},{10,... | collective-permute-start | bytes 24584 | tf_op jit(solution)/shard_map/ppermute | solution.py:244
  30.3 4.3 %shard_map.101 = (f32[4,256,256]{2,1,0:T(8,128)S(1)}, bf16[4,256,256]{2,1,0:T(8,128)(2,1)S(1)}, f32[8,256]{1,0:T(8,128)S(1)}) custom-call(bf16[256,768]{1,0:T(8,128)(2,1)S(1)} %copy-done.4, bf16[768,256]{1,0:T(8,128)(2,1)S(1)} %copy-done.5, bf16[512,256]{1,0:T(8,128)(2,1)S(1)} %copy-done.6, f32[256,256]{1,0:T(8,128)S(1)} %copy-done.8, ...), custom_call_target="tpu_custom_call" | custom-call | flops 1476395008 | tf_op jit(solution)/shard_map/pallas_call | solution.py:260
  34.6 3.7 %collective-permute-done.8 = f32[8,256]{1,0:T(8,128)S(1)} collective-permute-done((f32[8,256]{1,0:T(8,128)S(1)}, f32[8,256]{1,0:T(8,128)S(1)}, u32[]{:S(2)}, u32[]{:S(2)}) %collective-permute-start.8) | collective-permute-done | bytes 8224 | tf_op jit(solution)/shard_map/ppermute | solution.py:244
  38.3 0.1 collective-permute-start.9
  38.4 0.7 %collective-permute-start.10 = (f32[4,256]{1,0:T(4,128)S(1)}, f32[4,256]{1,0:T(4,128)S(1)}, u32[]{:S(2)}, u32[]{:S(2)}) collective-permute-start(f32[4,256]{1,0:T(4,128)S(1)} %get-tuple-element.33), channel_id=1, source_target_pairs={{1,2},{3,4},{5,6},{2,1},{4,3},{6,5},{9,10},{11,12},{13,14},{10,9},... | collective-permute-start | bytes 12296 | tf_op jit(solution)/shard_map/ppermute | solution.py:288
  39.0 6.9 %shard_map.102.one_ref = f32[320,128]{1,0:T(8,128)S(1)} custom-call(f32[4,256,256]{2,1,0:T(8,128)S(1)} %get-tuple-element.23.p_ref, bf16[4,256,256]{2,1,0:T(8,128)(2,1)S(1)} %get-tuple-element.24.c_ref, s32[64,128]{1,0:T(8,128)S(1)} %reshape.14.cells_ref), custom_call_target="tpu_custom_call" | custom-call | flops 5368709120 | tf_op jit(solution)/shard_map/pallas_call | solution.py:272
  46.0 0.8 %shard_map.105 = f32[96,128]{1,0:T(8,128)S(1)} custom-call(s32[1]{0:T(128)} %bitcast.1.tile_ref, f32[4]{0:T(128)S(1)} %copy-done.3, f32[320,128]{1,0:T(8,128)S(1)} %shard_map.102.one_ref, f32[320,128]{1,0:T(8,128)S(1)} %collective-permute-done.7.two_ref, s32[64,128]{1,0:T(8,128)S(1)} %reshape.14.cells_ref, f32[4,256]{1,0:T(4,128)S(1)} %collective-permute-done.9.first_ref, ...), custom_call_target="tpu_custom_call" | custom-call | tf_op jit(solution)/shard_map/pallas_call | solution.py:290
  46.9 9.2 %all-gather = f32[384,128]{1,0:T(8,128)S(1)} all-gather(f32[96,128]{1,0:T(8,128)S(1)} %shard_map.105), channel_id=2, replica_groups=mesh['depth'=4,'tile'=8] {'depth'}, dimensions={0}, use_global_device_ids=true | all-gather | bytes 245760 | tf_op jit(solution)/shard_map/all_gather | solution.py:295
  56.1 0.7 %copy.11 = f32[1,6,2048]{2,0,1:T(1,128)} copy(f32[1,6,2048]{2,1,0:T(8,128)S(1)} %shard_map.106) | data formatting | bytes 98304 | tf_op jit(solution)/shard_map/pallas_call | solution.py:296
  (31 shorter events, 0.1 us)
Async XLA Ops:
  0.0 0.7 %copy-start.1 = (s32[32]{0:T(128)S(1)}, s32[32]{0:T(128)}, u32[]{:S(2)}) copy-start(s32[32]{0:T(128)} %owner_ref.1) | copy-start | bytes 388
  0.0 0.7 %copy-start.2 = (s32[32]{0:T(128)S(1)}, s32[32]{0:T(128)}, u32[]{:S(2)}) copy-start(s32[32]{0:T(128)} %place_ref.1) | copy-start | bytes 388
  0.7 1.2 %copy-start = (bf16[32,128,128]{2,1,0:T(8,128)(2,1)S(1)}, bf16[32,128,128]{2,1,0:T(8,128)(2,1)}, u32[]{:S(2)}) copy-start(bf16[32,128,128]{2,1,0:T(8,128)(2,1)} %blocks_ref.1) | copy-start | bytes 3145732
  1.9 13.4 %copy-start.4 = (bf16[256,768]{1,0:T(8,128)(2,1)S(1)}, bf16[256,768]{1,0:T(8,128)(2,1)}, u32[]{:S(2)}) copy-start(bf16[256,768]{1,0:T(8,128)(2,1)} %constant.30.clone.refs_0_) | copy-start | bytes 1179652
  1.9 13.4 %copy-start.5 = (bf16[768,256]{1,0:T(8,128)(2,1)S(1)}, bf16[768,256]{1,0:T(8,128)(2,1)}, u32[]{:S(2)}) copy-start(bf16[768,256]{1,0:T(8,128)(2,1)} %constant.31.clone.refs_1_) | copy-start | bytes 1179652
  1.9 13.4 %copy-start.6 = (bf16[512,256]{1,0:T(8,128)(2,1)S(1)}, bf16[512,256]{1,0:T(8,128)(2,1)}, u32[]{:S(2)}) copy-start(bf16[512,256]{1,0:T(8,128)(2,1)} %constant.32.clone.refs_2_) | copy-start | bytes 786436
  2.7 7.2 %collective-permute-start.3 = (bf16[528,128]{1,0:T(8,128)(2,1)S(1)}, bf16[528,128]{1,0:T(8,128)(2,1)S(1)}, u32[]{:S(2)}, u32[]{:S(2)}) collective-permute-start(bf16[528,128]{1,0:T(8,128)(2,1)S(1)} %get-tuple-element.26), channel_id=1, source_target_pairs={{0,2},{1,3},{2,0},{3,1},{4,6},{5,7},{6,4},{7,5},{8,10},{9,11},{10,... | collective-permute-start | bytes 405512 | tf_op jit(solution)/shard_map/ppermute | solution.py:244
  5.8 6.9 %collective-permute-start.4 = (bf16[528,128]{1,0:T(8,128)(2,1)S(1)}, bf16[528,128]{1,0:T(8,128)(2,1)S(1)}, u32[]{:S(2)}, u32[]{:S(2)}) collective-permute-start(bf16[528,128]{1,0:T(8,128)(2,1)S(1)} %get-tuple-element.27), channel_id=1, source_target_pairs={{0,3},{1,2},{2,1},{3,0},{4,7},{5,6},{6,5},{7,4},{8,11},{9,10},{10,... | collective-permute-start | bytes 405512 | tf_op jit(solution)/shard_map/ppermute | solution.py:244
  5.8 9.5 %collective-permute-start.5 = (bf16[528,128]{1,0:T(8,128)(2,1)S(1)}, bf16[528,128]{1,0:T(8,128)(2,1)S(1)}, u32[]{:S(2)}, u32[]{:S(2)}) collective-permute-start(bf16[528,128]{1,0:T(8,128)(2,1)S(1)} %get-tuple-element.28), channel_id=1, source_target_pairs={{0,1},{1,0},{2,3},{3,2},{4,5},{5,4},{6,7},{7,6},{8,9},{9,8},{10,11... | collective-permute-start | bytes 405512 | tf_op jit(solution)/shard_map/ppermute | solution.py:244
  6.0 24.3 %collective-permute-start = (bf16[528,128]{1,0:T(8,128)(2,1)S(1)}, bf16[528,128]{1,0:T(8,128)(2,1)S(1)}, u32[]{:S(2)}, u32[]{:S(2)}) collective-permute-start(bf16[528,128]{1,0:T(8,128)(2,1)S(1)} %get-tuple-element.20), channel_id=1, source_target_pairs={{0,2},{1,3},{2,0},{3,1},{4,6},{5,7},{6,4},{7,5},{8,10},{9,11},{10,... | collective-permute-start | bytes 405512 | tf_op jit(solution)/shard_map/ppermute | solution.py:244
  7.9 22.4 %collective-permute-start.1 = (bf16[528,128]{1,0:T(8,128)(2,1)S(1)}, bf16[528,128]{1,0:T(8,128)(2,1)S(1)}, u32[]{:S(2)}, u32[]{:S(2)}) collective-permute-start(bf16[528,128]{1,0:T(8,128)(2,1)S(1)} %get-tuple-element.21), channel_id=1, source_target_pairs={{0,3},{1,2},{2,1},{3,0},{4,7},{5,6},{6,5},{7,4},{8,11},{9,10},{10,... | collective-permute-start | bytes 405512 | tf_op jit(solution)/shard_map/ppermute | solution.py:244
  7.9 0.8 %copy-start.9 = (f32[2,2048]{1,0:T(2,128)S(1)}, f32[2,2048]{1,0:T(2,128)}, u32[]{:S(2)}) copy-start(f32[2,2048]{1,0:T(2,128)} %param.15) | copy-start | bytes 49156
  9.9 20.4 %collective-permute-start.2 = (bf16[528,128]{1,0:T(8,128)(2,1)S(1)}, bf16[528,128]{1,0:T(8,128)(2,1)S(1)}, u32[]{:S(2)}, u32[]{:S(2)}) collective-permute-start(bf16[528,128]{1,0:T(8,128)(2,1)S(1)} %get-tuple-element.22), channel_id=1, source_target_pairs={{0,1},{1,0},{2,3},{3,2},{4,5},{5,4},{6,7},{7,6},{8,9},{9,8},{10,11... | collective-permute-start | bytes 405512 | tf_op jit(solution)/shard_map/ppermute | solution.py:244
  12.7 7.7 %collective-permute-start.6 = (s32[64,128]{1,0:T(8,128)S(1)}, s32[64,128]{1,0:T(8,128)S(1)}, u32[]{:S(2)}, u32[]{:S(2)}) collective-permute-start(s32[64,128]{1,0:T(8,128)S(1)} %reshape.14.cells_ref), channel_id=1, source_target_pairs={{0,4},{1,5},{2,6},{3,7},{4,0},{5,1},{6,2},{7,3},{8,12},{9,13},{10,... | collective-permute-start | bytes 98312 | tf_op jit(solution)/shard_map/ppermute | solution.py:244
  15.3 1.0 %copy-start.7 = (f32[256,256]{1,0:T(8,128)S(1)}, f32[256,256]{1,0:T(8,128)}, u32[]{:S(2)}) copy-start(f32[256,256]{1,0:T(8,128)} %constant.33.clone.refs_3_) | copy-start | bytes 786436
  20.3 10.0 %copy-start.8 = (f32[256,256]{1,0:T(8,128)S(1)}, f32[256,256]{1,0:T(8,128)}, u32[]{:S(2)}) copy-start(f32[256,256]{1,0:T(8,128)} %constant.33.clone.refs_3_) | copy-start | bytes 786436
  27.3 18.7 %collective-permute-start.7 = (f32[320,128]{1,0:T(8,128)S(1)}, f32[320,128]{1,0:T(8,128)S(1)}, u32[]{:S(2)}, u32[]{:S(2)}) collective-permute-start(f32[320,128]{1,0:T(8,128)S(1)} %shard_map.104), channel_id=1, source_target_pairs={{0,4},{1,5},{2,6},{3,7},{4,0},{5,1},{6,2},{7,3},{8,12},{9,13},{10,... | collective-permute-start | bytes 491528 | tf_op jit(solution)/shard_map/ppermute | solution.py:244
  28.4 9.8 %collective-permute-start.8 = (f32[8,256]{1,0:T(8,128)S(1)}, f32[8,256]{1,0:T(8,128)S(1)}, u32[]{:S(2)}, u32[]{:S(2)}) collective-permute-start(f32[8,256]{1,0:T(8,128)S(1)} %get-tuple-element.32), channel_id=1, source_target_pairs={{0,4},{1,5},{2,6},{3,7},{4,0},{5,1},{6,2},{7,3},{8,12},{9,13},{10,... | collective-permute-start | bytes 24584 | tf_op jit(solution)/shard_map/ppermute | solution.py:244
  38.3 7.7 %collective-permute-start.9 = (f32[4,256]{1,0:T(4,128)S(1)}, f32[4,256]{1,0:T(4,128)S(1)}, u32[]{:S(2)}, u32[]{:S(2)}) collective-permute-start(f32[4,256]{1,0:T(4,128)S(1)} %get-tuple-element.34), channel_id=1, source_target_pairs={{0,1},{1,0},{2,3},{3,2},{4,5},{5,4},{6,7},{7,6},{8,9},{9,8},{10,11... | collective-permute-start | bytes 12296 | tf_op jit(solution)/shard_map/ppermute | solution.py:244
  38.4 7.6 %collective-permute-start.10 = (f32[4,256]{1,0:T(4,128)S(1)}, f32[4,256]{1,0:T(4,128)S(1)}, u32[]{:S(2)}, u32[]{:S(2)}) collective-permute-start(f32[4,256]{1,0:T(4,128)S(1)} %get-tuple-element.33), channel_id=1, source_target_pairs={{1,2},{3,4},{5,6},{2,1},{4,3},{6,5},{9,10},{11,12},{13,14},{10,9},... | collective-permute-start | bytes 12296 | tf_op jit(solution)/shard_map/ppermute | solution.py:288
  39.0 7.0 %copy-start.3 = (f32[4]{0:T(128)S(1)}, f32[4]{0:T(128)}, u32[]{:S(2)}) copy-start(f32[4]{0:T(128)} %weights_ref.1) | copy-start | bytes 52

commit v2 on v1

--- a/solution.py
+++ b/solution.py
@@ -14,6 +14,7 @@
 LANES = 128
 VMEM = pl.BlockSpec(memory_space=pltpu.VMEM)
 SMEM = pl.BlockSpec(memory_space=pltpu.SMEM)
+HBM = pl.BlockSpec(memory_space=pltpu.HBM)
 
 
 def call(kernel, outs, in_specs, scratch=(), limit=48, flops=0, moved=0):
@@ -48,13 +49,11 @@
     low = (sines - high.astype(np.float64)).astype(np.float32).astype(ml_dtypes.bfloat16)
     single = 2.0 - 2.0 * np.cos(np.pi * index / (side + 1.0))
     inverse = -2.0 / (single[:, None] + single[None, :])
-    across = np.concatenate([high, high, low], axis=1)
-    down = np.concatenate([high, high, low], axis=0)
-    return across, down, np.concatenate([high, low], axis=0), inverse.astype(np.float32)
-
-
-def pack_kernel(tile_count, capacity, tile_ref, owner_ref, place_ref, blocks_ref, *rest):
-    outs, slot_ref, count_ref = rest[:tile_count], rest[-2], rest[-1]
+    return high, low, inverse.astype(np.float32)
+
+
+def pack_kernel(tile_count, capacity, layout, tile_ref, owner_ref, place_ref, blocks_ref, *rest):
+    outs, slot_ref, count_ref = rest[-2 - len(layout) : -2], rest[-2], rest[-1]
     slots, side = blocks_ref.shape[0], blocks_ref.shape[1]
     spare = tile_count * capacity
     tile = tile_ref[0]
@@ -71,20 +70,22 @@
         slot_ref[jnp.where(live, chunk * capacity + count, spare + e)] = e
     rows = label_rows(capacity)
     row = lax.broadcasted_iota(jnp.int32, (rows, side), 0)
-    for x in range(tile_count):
-        labels = jnp.full((rows, side), -1, jnp.int32)
-        for c in range(capacity):
-            entry = slot_ref[x * capacity + c]
-            safe = jnp.maximum(entry, 0)
-            label = jnp.where(entry >= 0, place_ref[safe], -1)
-            outs[x][pl.ds(c * side, side), :] = blocks_ref[safe]
-            labels = jnp.where(row == c, label, labels)
-        outs[x][pl.ds(capacity * side, rows), :] = labels.astype(F32).astype(BF16)
+    for out, members in zip(outs, layout):
+        for i, x in enumerate(members):
+            base = i * (capacity * side + rows)
+            labels = jnp.full((rows, side), -1, jnp.int32)
+            for c in range(capacity):
+                entry = slot_ref[x * capacity + c]
+                safe = jnp.maximum(entry, 0)
+                label = jnp.where(entry >= 0, place_ref[safe], -1)
+                out[pl.ds(base + c * side, side), :] = blocks_ref[safe]
+                labels = jnp.where(row == c, label, labels)
+            out[pl.ds(base + capacity * side, rows), :] = labels.astype(F32).astype(BF16)
 
 
 def solve_kernel(capacity, planes, *refs):
-    across_ref, down_ref, pair_ref, inverse_ref = refs[:4]
-    chunks, (p_ref, c_ref, edge_ref) = refs[4:-3], refs[-3:]
+    high_ref, low_ref, inverse_ref = refs[:3]
+    chunks, (p_ref, c_ref, edge_ref) = refs[3:-3], refs[-3:]
     side = chunks[0].shape[1]
     c_ref[...] = jnp.zeros(c_ref.shape, BF16)
     rows = label_rows(capacity)
@@ -99,16 +100,23 @@
                 left = pl.multiple_of((label & 1) * side, side)
                 c_ref[label >> 2, pl.ds(top, side), pl.ds(left, side)] = chunk[pl.ds(c * side, side), :]
 
-    across, down, pair, inverse = across_ref[...], down_ref[...], pair_ref[...], inverse_ref[...]
+    high, low, inverse = high_ref[...], low_ref[...], inverse_ref[...]
+    across = jnp.concatenate([high, high, low], axis=1)
+    down = jnp.concatenate([high, high, low], axis=0)
+    pair = jnp.concatenate([high, low], axis=0)
+
+    def right(a, b):
+        return mul(jnp.concatenate([a, b, a], axis=1), down)
+
+    def left(a, b):
+        return mul(across, jnp.concatenate([a, b, a], axis=0))
+
+    mass = [c_ref[k] for k in range(planes)]
+    parts = [halves(mul(jnp.concatenate([m, m], axis=1), pair)) for m in mass]
+    parts = [halves(left(*part) * inverse) for part in parts]
+    parts = [halves(right(*part)) for part in parts]
     for k in range(planes):
-        mass = c_ref[k]
-        half = mul(jnp.concatenate([mass, mass], axis=1), pair)
-        high, low = halves(half)
-        spectrum = mul(across, jnp.concatenate([high, low, high], axis=0)) * inverse
-        high, low = halves(spectrum)
-        half = mul(jnp.concatenate([high, low, high], axis=1), down)
-        high, low = halves(half)
-        potential = mul(across, jnp.concatenate([high, low, high], axis=0))
+        potential = left(*parts[k])
         p_ref[k] = potential
         edge_ref[pl.ds(k, 1), :] = potential[:1]
         edge_ref[pl.ds(planes + k, 1), :] = potential[2 * side - 1 :]
@@ -116,12 +124,20 @@
 
 def shifted(a, axis, step):
     size = a.shape[axis]
-    place = lax.broadcasted_iota(jnp.int32, a.shape, axis)
-    edge = size - 1 if step > 0 else 0
-    return jnp.where(place == edge, 0.0, pltpu.roll(a, (-step) % size, axis))
-
-
-def pick_kernel(planes, p_ref, c_ref, cells_ref, out_ref):
+    tile = 8 if axis == 0 and size > 8 else min(size, LANES)
+    rolled = pltpu.roll(a, (-step) % size, axis)
+    at = size - tile if step > 0 else 0
+    last = lax.slice_in_dim(rolled, at, at + tile, axis=axis)
+    place = lax.broadcasted_iota(jnp.int32, last.shape, axis)
+    last = jnp.where(place == (tile - 1 if step > 0 else 0), 0.0, last)
+    if size == tile:
+        return last
+    if step > 0:
+        return jnp.concatenate([lax.slice_in_dim(rolled, 0, at, axis=axis), last], axis=axis)
+    return jnp.concatenate([last, lax.slice_in_dim(rolled, tile, size, axis=axis)], axis=axis)
+
+
+def pick_kernel(planes, p_ref, c_ref, cells_ref, last_ref, out_ref):
     side = p_ref.shape[1]
     shift = side.bit_length() - 1
     groups = cells_ref.shape[0] // planes
@@ -132,27 +148,29 @@
         p = p_ref[k]
         above, below = shifted(p, 0, -1), shifted(p, 0, 1)
         left, right = shifted(p, 1, -1), shifted(p, 1, 1)
-        slope = 0.5 * (below - above)
+        tilt = 0.5 * (right - left)
         fields = (
-            slope.astype(BF16),
-            (0.5 * (right - left)).astype(BF16),
+            (0.5 * (below - above)).astype(BF16),
+            tilt.astype(BF16),
             c_ref[k],
             (0.5 * ((below + above) - (right + left))).astype(BF16),
-            (0.5 * (shifted(slope, 1, 1) - shifted(slope, 1, -1))).astype(BF16),
+            (0.5 * (shifted(tilt, 0, 1) - shifted(tilt, 0, -1))).astype(BF16),
         )
         for g in range(0, groups, width):
             cells = jnp.concatenate([cells_ref[pl.ds(k * groups + g + w, 1), :] for w in range(width)], axis=1)
             row, col = cells >> shift, cells & (side - 1)
             chosen = (column == col).astype(F32).astype(BF16)
             block, within = row >> 3, sub == (row & 7)
+            bits = [(block >> i) & 1 == 1 for i in range((side // 8).bit_length() - 1)]
             for f in range(5):
                 picked = mul(fields[f], chosen)
-                kept = picked[:8]
-                for v in range(1, side // 8):
-                    kept = jnp.where(block == v, picked[v * 8 : v * 8 + 8], kept)
-                value = jnp.sum(jnp.where(within, kept, 0.0), axis=0, keepdims=True)
+                kept = [picked[v * 8 : v * 8 + 8] for v in range(side // 8)]
+                for bit in bits:
+                    kept = [jnp.where(bit, b, a) for a, b in zip(kept[::2], kept[1::2])]
+                value = jnp.sum(jnp.where(within, kept[0], 0.0), axis=0, keepdims=True)
                 for w in range(width):
                     out_ref[pl.ds((k * 5 + f) * groups + g + w, 1), :] = value[:, w * LANES : (w + 1) * LANES]
+    last_ref[...] = out_ref[...].astype(last_ref.dtype)
 
 
 def taken(table, index):
@@ -167,10 +185,12 @@
     return out
 
 
-def combine_kernel(planes, side, tile_ref, weights_ref, one_ref, two_ref, cells_ref, first_ref, second_ref, out_ref):
+def combine_kernel(tile_count, planes, side, tile_ref, weights_ref, one_ref, two_ref, cells_ref, first_ref, second_ref, out_ref):
     groups = cells_ref.shape[0] // planes
     shift = side.bit_length() - 1
-    even = (tile_ref[0] & 1) == 0
+    tile = tile_ref[0]
+    even = (tile & 1) == 0
+    starts, ends = tile == 0, tile == tile_count - 1
     axx = ayy = jnp.ones((groups, LANES), F32)
     axy = ayx = bx = by = jnp.zeros((groups, LANES), F32)
     for k in range(planes):
@@ -178,6 +198,7 @@
         row, col = cells >> shift, cells & (side - 1)
         first, second = first_ref[pl.ds(k, 1), :], second_ref[pl.ds(k, 1), :]
         above, below = jnp.where(even, second, first), jnp.where(even, first, second)
+        above, below = jnp.where(starts, 0.0, above), jnp.where(ends, 0.0, below)
         at_top, at_end = row == 0, row == side - 1
         up, down = taken(above, col), taken(below, col)
         up_x = taken(shifted(above, 1, 1) - shifted(above, 1, -1), col)
@@ -188,7 +209,7 @@
 
         def read(f):
             at = pl.ds((k * 5 + f) * groups, groups)
-            return one_ref[at, :] + two_ref[at, :]
+            return one_ref[at, :] + two_ref[at, :].astype(F32)
 
         weight = weights_ref[k]
         bend_x, bend_y = read(0) + 0.5 * (far - near), read(1)
@@ -222,8 +243,7 @@
     bx = bx + angles_ref[pl.ds(0, groups), :]
     by = by + angles_ref[pl.ds(groups, groups), :]
     for i, value in enumerate((xx, xy, yx, yy, bx, by)):
-        for g in range(groups):
-            out_ref[0, pl.ds(i, 1), pl.ds(g * LANES, LANES)] = value[g : g + 1]
+        out_ref[pl.ds(i * groups, groups), :] = value
 
 
 def body(density_blocks, block_owner, block_place, lens_weights, ray_cells, ray_angles):
@@ -236,7 +256,7 @@
     half = tile_count // 2
     tile = lax.axis_index("tile").astype(jnp.int32).reshape(1)
     depth = lax.axis_index("depth").astype(jnp.int32).reshape(1)
-    across, down, pair, inverse = (jnp.asarray(t) for t in tables(side))
+    high, low, inverse = (jnp.asarray(t) for t in tables(side))
     cells = ray_cells.reshape(planes * groups, LANES)
     angles = ray_angles.reshape(2 * groups, LANES)
 
@@ -244,19 +264,20 @@
         return lax.ppermute(array, "tile", [(i, i ^ bits) for i in range(tile_count)])
 
     rows = capacity * block_side + label_rows(capacity)
-    chunks = call(
-        functools.partial(pack_kernel, tile_count, capacity),
+    order = list(range(2, half)) + [1]
+    layout = [[half + x] for x in order] + [[half]] + [[x] for x in order] + [[0]]
+    packed = call(
+        functools.partial(pack_kernel, tile_count, capacity, layout),
         [jax.ShapeDtypeStruct((rows, block_side), BF16)] * tile_count,
         [SMEM, SMEM, SMEM, VMEM],
         [pltpu.SMEM((tile_count * capacity + slots,), jnp.int32), pltpu.SMEM((tile_count + 1,), jnp.int32)],
-        moved=2 * density_blocks.size * 2,
+        moved=2 * density_blocks.size,
     )(tile, block_owner, block_place, density_blocks)
-    order = list(range(2, half)) + [1] if half > 1 else []
-    theirs = [chunks[half]] + [swap(chunks[s + half], s) for s in order]
-    ours = [chunks[0]] + [swap(chunks[s], s) for s in order]
+    theirs = [swap(chunk, x) for x, chunk in zip(order, packed)] + [packed[half - 1]]
+    ours = [swap(chunk, x) for x, chunk in zip(order, packed[half:])] + [packed[-1]]
     their_cells = swap(cells, half)
 
-    def solve(received):
+    def solve(arrays):
         return call(
             functools.partial(solve_kernel, capacity, planes),
             [
@@ -264,40 +285,41 @@
                 jax.ShapeDtypeStruct((planes, side, side), BF16),
                 jax.ShapeDtypeStruct((2 * planes, side), F32),
             ],
-            [VMEM] * (4 + half),
-            flops=2 * 11 * planes * side**3,
-        )(across, down, pair, inverse, *received)
-
-    def pick(potential, mass, at):
+            [VMEM] * (3 + len(arrays)),
+        )(high, low, inverse, *arrays)
+
+    def pick(potential, mass, at, dtype):
+        shape = (planes * 5 * groups, LANES)
         return call(
             functools.partial(pick_kernel, planes),
-            [jax.ShapeDtypeStruct((planes * 5 * groups, LANES), F32)],
+            [jax.ShapeDtypeStruct(shape, dtype)],
             [VMEM] * 3,
+            [pltpu.VMEM(shape, F32)],
             flops=2 * 5 * planes * side * side * rays,
         )(potential, mass, at)[0]
 
     potential, mass, their_edges = solve(theirs)
-    other_edges = swap(their_edges, half)
-    other_samples = swap(pick(potential, mass, their_cells), half)
+    samples, their_edges = lax.optimization_barrier((pick(potential, mass, their_cells, BF16), their_edges))
+    other_edges, other_samples = swap(their_edges, half), swap(samples, half)
     potential, mass, our_edges = solve(ours)
     edges = our_edges + other_edges
     even = tile[0] % 2 == 0
     top, end = edges[:planes], edges[planes:]
     first = swap(jnp.where(even, end, top), 1)
-    pairs = [(i, i + 1) for i in range(1, tile_count - 1, 2)]
+    pairs = [(i, (i + 1) % tile_count) for i in range(1, tile_count, 2)]
     second = lax.ppermute(jnp.where(even, top, end), "tile", pairs + [(j, i) for i, j in pairs])
-    own_samples = pick(potential, mass, cells)
+    own_samples = pick(potential, mass, cells, F32)
     local_map = call(
-        functools.partial(combine_kernel, planes, side),
+        functools.partial(combine_kernel, tile_count, planes, side),
         [jax.ShapeDtypeStruct((6 * groups, LANES), F32)],
         [SMEM, SMEM, VMEM, VMEM, VMEM, VMEM, VMEM],
     )(tile, lens_weights, own_samples, other_samples, cells, first, second)[0]
     maps = lax.all_gather(local_map, "depth")
     return call(
         compose_kernel,
-        [jax.ShapeDtypeStruct((1, 6, rays), F32)],
+        [jax.ShapeDtypeStruct((6 * groups, LANES), F32)],
         [SMEM, VMEM, VMEM],
-    )(depth, maps, angles)[0]
+    )(depth, maps, angles)[0].reshape(1, 6, rays)
 
 
 def solution(mesh):

time: 57 us -> 48.3 us (0.85)
  waiting for transfers between devices: 7.61 us -> 2.08 us
  Pallas kernels: 23.9 us -> 20.1 us
  starting transfers between devices: 11.5 us -> 15.1 us
  local copies, waits for them, and re-layouts: 4.35 us -> 1.95 us
    ppermute x10, waiting for transfers between devices: 7.61 us -> 2.08 us  [swap(): lax.ppermute(array, 'tile', [(i, i ^ bits) for i in range(tile_count)])]
    pallas_call x2, Pallas kernels: 8.34 us -> 4.97 us  [solve(): call(functools.partial(solve_kernel, capacity, planes), [jax.ShapeDtypeSt...]
    ppermute x1, starting transfers between devices: 0.66 us -> 3.12 us  [body(): lax.ppermute(jnp.where(even, top, end), 'tile', pairs + [(j, i) for i, j...]
    ppermute x10, starting transfers between devices: 10.9 us -> 11.9 us  [swap(): lax.ppermute(array, 'tile', [(i, i ^ bits) for i in range(tile_count)])]
    unnamed x20 -> x18, local copies, waits for them, and re-layouts: 2.87 us -> 1.92 us
    reshape x1, local copies, waits for them, and re-layouts: 0.79 us -> 0.02 us  [body(): cells = ray_cells.reshape(planes * groups, LANES)]
    pallas_call x1 -> x0, local copies, waits for them, and re-layouts: 0.67 us -> none  [body(): call(compose_kernel, [jax.ShapeDtypeStruct((1, 6, rays), F32)], [SMEM, VM...]
  transfers between devices with their start and end apart: 11 -> 11, of which waited for: 3 -> 1; matrix products, arithmetic and copies ran while one was open for 1% -> 0% of each run, Pallas kernels for 39% -> 37%
where the time goes in v2:
time: 48.3 us; the launch traced here: 48.1 us
  Pallas kernels  20.1 us (42%)
  starting transfers between devices  15.1 us (31%)
  blocking collectives  8.74 us (18%)
  waiting for transfers between devices  2.08 us (4%)
  local copies, waits for them, and re-layouts  1.95 us (4%)
    pallas_call x2, Pallas kernels, pick(): call(functools.partial(pick_kernel, planes), [jax.ShapeDtypeStruct(shape,...  12.8 us
    ppermute x10, starting transfers between devices, swap(): lax.ppermute(array, 'tile', [(i, i ^ bits) for i in range(tile_count)])  11.9 us
    all_gather x1, blocking collectives, body(): maps = lax.all_gather(local_map, 'depth')  8.74 us
    pallas_call x2, Pallas kernels, solve(): call(functools.partial(solve_kernel, capacity, planes), [jax.ShapeDtypeSt...  4.97 us
    ppermute x1, starting transfers between devices, body(): lax.ppermute(jnp.where(even, top, end), 'tile', pairs + [(j, i) for i, j...  3.12 us
    ppermute x10, waiting for transfers between devices, swap(): lax.ppermute(array, 'tile', [(i, i ^ bits) for i in range(tile_count)])  2.08 us
    unnamed x18, local copies, waits for them, and re-layouts  1.92 us
  transfers between devices with their start and end apart: 11, of which 1 were waited for; matrix products, arithmetic and copies ran while one was open for 0% of the time, Pallas kernels for 37%

profile of v2, /device:TPU:0, one launch (start us, length us, event | category | flops | bytes accessed | tf_op | source)
XLA Modules:
  0.0 48.1 jit_solution(3608130240721842830)
XLA Ops:
  0.0 0.7 %copy-done.4 = s32[32]{0:T(128)S(1)} copy-done((s32[32]{0:T(128)S(1)}, s32[32]{0:T(128)}, u32[]{:S(2)}) %copy-start.4) | copy-done | bytes 152
  0.7 0.0 copy-done.5
  0.7 1.2 %copy-done = bf16[32,128,128]{2,1,0:T(8,128)(2,1)S(1)} copy-done((bf16[32,128,128]{2,1,0:T(8,128)(2,1)S(1)}, bf16[32,128,128]{2,1,0:T(8,128)(2,1)}, u32[]{:S(2)}) %copy-start) | copy-done | bytes 1048600
  1.9 0.8 %shard_map.91 = (bf16[528,128]{1,0:T(8,128)(2,1)S(1)}, bf16[528,128]{1,0:T(8,128)(2,1)S(1)}, bf16[528,128]{1,0:T(8,128)(2,1)S(1)}, bf16[528,128]{1,0:T(8,128)(2,...) custom-call(s32[1]{0:T(128)} %bitcast.1.tile_ref, ...), custom_call_target="tpu_custom_call" | custom-call | bytes 1048576 | tf_op jit(solution)/shard_map/pallas_call | solution.py:269
  2.7 3.1 %collective-permute-start.3 = (bf16[528,128]{1,0:T(8,128)(2,1)S(1)}, bf16[528,128]{1,0:T(8,128)(2,1)S(1)}, u32[]{:S(2)}, u32[]{:S(2)}) collective-permute-start(bf16[528,128]{1,0:T(8,128)(2,1)S(1)} %get-tuple-element.27), channel_id=1, source_target_pairs={{0,2},{1,3},{2,0},{3,1},{4,6},{5,7},{6,4},{7,5},{8,10},{9,11},{10,... | collective-permute-start | bytes 405512 | tf_op jit(solution)/shard_map/ppermute | solution.py:264
  5.8 0.0 collective-permute-start.4
  5.8 0.2 collective-permute-start.5
  6.0 3.0 %collective-permute-start.6 = (s32[64,128]{1,0:T(8,128)S(1)}, s32[64,128]{1,0:T(8,128)S(1)}, u32[]{:S(2)}, u32[]{:S(2)}) collective-permute-start(s32[64,128]{1,0:T(8,128)S(1)} %reshape.17.cells_ref), channel_id=1, source_target_pairs={{0,4},{1,5},{2,6},{3,7},{4,0},{5,1},{6,2},{7,3},{8,12},{9,13},{10,... | collective-permute-start | bytes 98312 | tf_op jit(solution)/shard_map/ppermute | solution.py:264
  9.0 1.6 %collective-permute-start = (bf16[528,128]{1,0:T(8,128)(2,1)S(1)}, bf16[528,128]{1,0:T(8,128)(2,1)S(1)}, u32[]{:S(2)}, u32[]{:S(2)}) collective-permute-start(bf16[528,128]{1,0:T(8,128)(2,1)S(1)} %get-tuple-element.21), channel_id=1, source_target_pairs={{0,2},{1,3},{2,0},{3,1},{4,6},{5,7},{6,4},{7,5},{8,10},{9,11},{10,... | collective-permute-start | bytes 405512 | tf_op jit(solution)/shard_map/ppermute | solution.py:264
  10.6 2.1 %collective-permute-done.4.refs_4_ = bf16[528,128]{1,0:T(8,128)(2,1)S(1)} collective-permute-done((bf16[528,128]{1,0:T(8,128)(2,1)S(1)}, bf16[528,128]{1,0:T(8,128)(2,1)S(1)}, u32[]{:S(2)}, u32[]{:S(2)}) %collective-permute-start.4) | collective-permute-done | bytes 135200 | tf_op jit(solution)/shard_map/ppermute | solution.py:264
  12.7 0.6 %collective-permute-start.2 = (bf16[528,128]{1,0:T(8,128)(2,1)S(1)}, bf16[528,128]{1,0:T(8,128)(2,1)S(1)}, u32[]{:S(2)}, u32[]{:S(2)}) collective-permute-start(bf16[528,128]{1,0:T(8,128)(2,1)S(1)} %get-tuple-element.23), channel_id=1, source_target_pairs={{0,1},{1,0},{2,3},{3,2},{4,5},{5,4},{6,7},{7,6},{8,9},{9,8},{10,11... | collective-permute-start | bytes 405512 | tf_op jit(solution)/shard_map/ppermute | solution.py:264
  13.3 0.0 collective-permute-done.5.refs_5_
  13.4 2.4 %shard_map.94 = (f32[4,256,256]{2,1,0:T(8,128)S(1)}, bf16[4,256,256]{2,1,0:T(8,128)(2,1)S(1)}, f32[8,256]{1,0:T(8,128)S(1)}) custom-call(bf16[256,256]{1,0:T(8,128)(2,1)S(1)} %copy-done.2, bf16[256,256]{1,0:T(8,128)(2,1)S(1)} %copy-done.3, f32[256,256]{1,0:T(8,128)S(1)} %copy-done.1, bf16[528,128]{1,0:T(8,128)(2,1)S(1)} %collective-permute-done.3.refs_3_, ...), custom_call_target="tpu_custom_call" | custom-call | tf_op jit(solution)/shard_map/pallas_call | solution.py:281
  15.8 0.0 collective-permute-done.6.cells_ref
  15.8 6.4 %shard_map.95 = bf16[320,128]{1,0:T(8,128)(2,1)S(1)} custom-call(f32[4,256,256]{2,1,0:T(8,128)S(1)} %get-tuple-element.31.p_ref, bf16[4,256,256]{2,1,0:T(8,128)(2,1)S(1)} %get-tuple-element.32.c_ref, s32[64,128]{1,0:T(8,128)S(1)} %collective-permute-done.6.cells_ref), custom_call_target="tpu_custom_call" | custom-call | flops 5368709120 | tf_op jit(solution)/shard_map/pallas_call | solution.py:293
  22.2 0.0 copy-start.8
  22.2 2.7 %collective-permute-start.8 = (f32[8,256]{1,0:T(8,128)S(1)}, f32[8,256]{1,0:T(8,128)S(1)}, u32[]{:S(2)}, u32[]{:S(2)}) collective-permute-start(f32[8,256]{1,0:T(8,128)S(1)} %get-tuple-element.36), channel_id=1, source_target_pairs={{0,4},{1,5},{2,6},{3,7},{4,0},{5,1},{6,2},{7,3},{8,12},{9,13},{10,... | collective-permute-start | bytes 24584 | tf_op jit(solution)/shard_map/ppermute | solution.py:264
  24.9 0.7 %collective-permute-start.7 = (bf16[320,128]{1,0:T(8,128)(2,1)S(1)}, bf16[320,128]{1,0:T(8,128)(2,1)S(1)}, u32[]{:S(2)}, u32[]{:S(2)}) collective-permute-start(bf16[320,128]{1,0:T(8,128)(2,1)S(1)} %shard_map.95), channel_id=1, source_target_pairs={{0,4},{1,5},{2,6},{3,7},{4,0},{5,1},{6,2},{7,3},{8,12},{9,13},{10,... | collective-permute-start | bytes 245768 | tf_op jit(solution)/shard_map/ppermute | solution.py:264
  25.6 2.6 %shard_map.92 = (f32[4,256,256]{2,1,0:T(8,128)S(1)}, bf16[4,256,256]{2,1,0:T(8,128)(2,1)S(1)}, f32[8,256]{1,0:T(8,128)S(1)}) custom-call(bf16[256,256]{1,0:T(8,128)(2,1)S(1)} %copy-done.2, bf16[256,256]{1,0:T(8,128)(2,1)S(1)} %copy-done.3, f32[256,256]{1,0:T(8,128)S(1)} %copy-done.1, bf16[528,128]{1,0:T(8,128)(2,1)S(1)} %collective-permute-done.refs_3_, ...), custom_call_target="tpu_custom_call" | custom-call | tf_op jit(solution)/shard_map/pallas_call | solution.py:281
  28.3 3.1 %collective-permute-start.10 = (f32[4,256]{1,0:T(4,128)S(1)}, f32[4,256]{1,0:T(4,128)S(1)}, u32[]{:S(2)}, u32[]{:S(2)}) collective-permute-start(f32[4,256]{1,0:T(4,128)S(1)} %get-tuple-element.37), channel_id=1, source_target_pairs={{1,2},{3,4},{5,6},{7,0},{2,1},{4,3},{6,5},{0,7},{9,10},{11,12},{13... | collective-permute-start | bytes 12296 | tf_op jit(solution)/shard_map/ppermute | solution.py:310
  31.4 6.4 %shard_map.93.one_ref = f32[320,128]{1,0:T(8,128)S(1)} custom-call(f32[4,256,256]{2,1,0:T(8,128)S(1)} %get-tuple-element.25.p_ref, bf16[4,256,256]{2,1,0:T(8,128)(2,1)S(1)} %get-tuple-element.26.c_ref, s32[64,128]{1,0:T(8,128)S(1)} %reshape.17.cells_ref), custom_call_target="tpu_custom_call" | custom-call | flops 5368709120 | tf_op jit(solution)/shard_map/pallas_call | solution.py:293
  37.9 0.8 %shard_map.96 = f32[96,128]{1,0:T(8,128)S(1)} custom-call(s32[1]{0:T(128)} %bitcast.1.tile_ref, f32[4]{0:T(128)S(1)} %copy-done.6, f32[320,128]{1,0:T(8,128)S(1)} %shard_map.93.one_ref, bf16[320,128]{1,0:T(8,128)(2,1)S(1)} %collective-permute-done.7.two_ref, s32[64,128]{1,0:T(8,128)S(1)} %reshape.17.cells_ref, ...), custom_call_target="tpu_custom_call" | custom-call | tf_op jit(solution)/shard_map/pallas_call | solution.py:312
  38.7 8.7 %all-gather = f32[384,128]{1,0:T(8,128)S(1)} all-gather(f32[96,128]{1,0:T(8,128)S(1)} %shard_map.96), channel_id=2, replica_groups=mesh['depth'=4,'tile'=8] {'depth'}, dimensions={0}, use_global_device_ids=true | all-gather | bytes 245760 | tf_op jit(solution)/shard_map/all_gather | solution.py:317
  47.4 0.6 %shard_map.97 = f32[96,128]{1,0:T(8,128)} custom-call(s32[1]{0:T(128)} %bitcast.depth_ref, f32[4,96,128]{2,1,0:T(8,128)S(1)} %bitcast.4, f32[32,128]{1,0:T(8,128)S(1)} %reshape.18.angles_ref), custom_call_target="tpu_custom_call" | custom-call | tf_op jit(solution)/shard_map/pallas_call | solution.py:318
  (28 shorter events, 0.1 us)
Async XLA Ops:
  0.0 0.7 %copy-start.4 = (s32[32]{0:T(128)S(1)}, s32[32]{0:T(128)}, u32[]{:S(2)}) copy-start(s32[32]{0:T(128)} %owner_ref.1) | copy-start | bytes 388
  0.0 0.7 %copy-start.5 = (s32[32]{0:T(128)S(1)}, s32[32]{0:T(128)}, u32[]{:S(2)}) copy-start(s32[32]{0:T(128)} %place_ref.1) | copy-start | bytes 388
  0.7 1.2 %copy-start = (bf16[32,128,128]{2,1,0:T(8,128)(2,1)S(1)}, bf16[32,128,128]{2,1,0:T(8,128)(2,1)}, u32[]{:S(2)}) copy-start(bf16[32,128,128]{2,1,0:T(8,128)(2,1)} %blocks_ref.1) | copy-start | bytes 3145732
  1.9 4.1 %copy-start.7 = (s32[4,2048]{1,0:T(4,128)S(1)}, s32[4,2048]{1,0:T(4,128)}, u32[]{:S(2)}) copy-start(s32[4,2048]{1,0:T(4,128)} %param.13) | copy-start | bytes 98308
  1.9 11.4 %copy-start.1 = (f32[256,256]{1,0:T(8,128)S(1)}, f32[256,256]{1,0:T(8,128)}, u32[]{:S(2)}) copy-start(f32[256,256]{1,0:T(8,128)} %constant.30.clone.refs_2_) | copy-start | bytes 786436
  1.9 11.4 %copy-start.2 = (bf16[256,256]{1,0:T(8,128)(2,1)S(1)}, bf16[256,256]{1,0:T(8,128)(2,1)}, u32[]{:S(2)}) copy-start(bf16[256,256]{1,0:T(8,128)(2,1)} %constant.28.clone.refs_0_) | copy-start | bytes 393220
  1.9 11.4 %copy-start.3 = (bf16[256,256]{1,0:T(8,128)(2,1)S(1)}, bf16[256,256]{1,0:T(8,128)(2,1)}, u32[]{:S(2)}) copy-start(bf16[256,256]{1,0:T(8,128)(2,1)} %constant.29.clone.refs_1_) | copy-start | bytes 393220
  2.7 7.9 %collective-permute-start.3 = (bf16[528,128]{1,0:T(8,128)(2,1)S(1)}, bf16[528,128]{1,0:T(8,128)(2,1)S(1)}, u32[]{:S(2)}, u32[]{:S(2)}) collective-permute-start(bf16[528,128]{1,0:T(8,128)(2,1)S(1)} %get-tuple-element.27), channel_id=1, source_target_pairs={{0,2},{1,3},{2,0},{3,1},{4,6},{5,7},{6,4},{7,5},{8,10},{9,11},{10,... | collective-permute-start | bytes 405512 | tf_op jit(solution)/shard_map/ppermute | solution.py:264
  5.8 6.9 %collective-permute-start.4 = (bf16[528,128]{1,0:T(8,128)(2,1)S(1)}, bf16[528,128]{1,0:T(8,128)(2,1)S(1)}, u32[]{:S(2)}, u32[]{:S(2)}) collective-permute-start(bf16[528,128]{1,0:T(8,128)(2,1)S(1)} %get-tuple-element.28), channel_id=1, source_target_pairs={{0,3},{1,2},{2,1},{3,0},{4,7},{5,6},{6,5},{7,4},{8,11},{9,10},{10,... | collective-permute-start | bytes 405512 | tf_op jit(solution)/shard_map/ppermute | solution.py:264
  5.8 7.5 %collective-permute-start.5 = (bf16[528,128]{1,0:T(8,128)(2,1)S(1)}, bf16[528,128]{1,0:T(8,128)(2,1)S(1)}, u32[]{:S(2)}, u32[]{:S(2)}) collective-permute-start(bf16[528,128]{1,0:T(8,128)(2,1)S(1)} %get-tuple-element.29), channel_id=1, source_target_pairs={{0,1},{1,0},{2,3},{3,2},{4,5},{5,4},{6,7},{7,6},{8,9},{9,8},{10,11... | collective-permute-start | bytes 405512 | tf_op jit(solution)/shard_map/ppermute | solution.py:264
  6.0 9.7 %collective-permute-start.6 = (s32[64,128]{1,0:T(8,128)S(1)}, s32[64,128]{1,0:T(8,128)S(1)}, u32[]{:S(2)}, u32[]{:S(2)}) collective-permute-start(s32[64,128]{1,0:T(8,128)S(1)} %reshape.17.cells_ref), channel_id=1, source_target_pairs={{0,4},{1,5},{2,6},{3,7},{4,0},{5,1},{6,2},{7,3},{8,12},{9,13},{10,... | collective-permute-start | bytes 98312 | tf_op jit(solution)/shard_map/ppermute | solution.py:264
  9.0 16.6 %collective-permute-start = (bf16[528,128]{1,0:T(8,128)(2,1)S(1)}, bf16[528,128]{1,0:T(8,128)(2,1)S(1)}, u32[]{:S(2)}, u32[]{:S(2)}) collective-permute-start(bf16[528,128]{1,0:T(8,128)(2,1)S(1)} %get-tuple-element.21), channel_id=1, source_target_pairs={{0,2},{1,3},{2,0},{3,1},{4,6},{5,7},{6,4},{7,5},{8,10},{9,11},{10,... | collective-permute-start | bytes 405512 | tf_op jit(solution)/shard_map/ppermute | solution.py:264
  10.6 15.0 %collective-permute-start.1 = (bf16[528,128]{1,0:T(8,128)(2,1)S(1)}, bf16[528,128]{1,0:T(8,128)(2,1)S(1)}, u32[]{:S(2)}, u32[]{:S(2)}) collective-permute-start(bf16[528,128]{1,0:T(8,128)(2,1)S(1)} %get-tuple-element.22), channel_id=1, source_target_pairs={{0,3},{1,2},{2,1},{3,0},{4,7},{5,6},{6,5},{7,4},{8,11},{9,10},{10,... | collective-permute-start | bytes 405512 | tf_op jit(solution)/shard_map/ppermute | solution.py:264
  12.7 13.0 %collective-permute-start.2 = (bf16[528,128]{1,0:T(8,128)(2,1)S(1)}, bf16[528,128]{1,0:T(8,128)(2,1)S(1)}, u32[]{:S(2)}, u32[]{:S(2)}) collective-permute-start(bf16[528,128]{1,0:T(8,128)(2,1)S(1)} %get-tuple-element.23), channel_id=1, source_target_pairs={{0,1},{1,0},{2,3},{3,2},{4,5},{5,4},{6,7},{7,6},{8,9},{9,8},{10,11... | collective-permute-start | bytes 405512 | tf_op jit(solution)/shard_map/ppermute | solution.py:264
  22.2 2.7 %copy-start.8 = (f32[2,2048]{1,0:T(2,128)S(1)}, f32[2,2048]{1,0:T(2,128)}, u32[]{:S(2)}) copy-start(f32[2,2048]{1,0:T(2,128)} %param.14) | copy-start | bytes 49156
  22.2 6.0 %collective-permute-start.8 = (f32[8,256]{1,0:T(8,128)S(1)}, f32[8,256]{1,0:T(8,128)S(1)}, u32[]{:S(2)}, u32[]{:S(2)}) collective-permute-start(f32[8,256]{1,0:T(8,128)S(1)} %get-tuple-element.36), channel_id=1, source_target_pairs={{0,4},{1,5},{2,6},{3,7},{4,0},{5,1},{6,2},{7,3},{8,12},{9,13},{10,... | collective-permute-start | bytes 24584 | tf_op jit(solution)/shard_map/ppermute | solution.py:264
  24.9 12.9 %collective-permute-start.7 = (bf16[320,128]{1,0:T(8,128)(2,1)S(1)}, bf16[320,128]{1,0:T(8,128)(2,1)S(1)}, u32[]{:S(2)}, u32[]{:S(2)}) collective-permute-start(bf16[320,128]{1,0:T(8,128)(2,1)S(1)} %shard_map.95), channel_id=1, source_target_pairs={{0,4},{1,5},{2,6},{3,7},{4,0},{5,1},{6,2},{7,3},{8,12},{9,13},{10,... | collective-permute-start | bytes 245768 | tf_op jit(solution)/shard_map/ppermute | solution.py:264
  28.3 9.6 %collective-permute-start.10 = (f32[4,256]{1,0:T(4,128)S(1)}, f32[4,256]{1,0:T(4,128)S(1)}, u32[]{:S(2)}, u32[]{:S(2)}) collective-permute-start(f32[4,256]{1,0:T(4,128)S(1)} %get-tuple-element.37), channel_id=1, source_target_pairs={{1,2},{3,4},{5,6},{7,0},{2,1},{4,3},{6,5},{0,7},{9,10},{11,12},{13... | collective-permute-start | bytes 12296 | tf_op jit(solution)/shard_map/ppermute | solution.py:310
  31.4 6.4 %collective-permute-start.9 = (f32[4,256]{1,0:T(4,128)S(1)}, f32[4,256]{1,0:T(4,128)S(1)}, u32[]{:S(2)}, u32[]{:S(2)}) collective-permute-start(f32[4,256]{1,0:T(4,128)S(1)} %get-tuple-element.38), channel_id=1, source_target_pairs={{0,1},{1,0},{2,3},{3,2},{4,5},{5,4},{6,7},{7,6},{8,9},{9,8},{10,11... | collective-permute-start | bytes 12296 | tf_op jit(solution)/shard_map/ppermute | solution.py:264
  31.4 6.5 %copy-start.6 = (f32[4]{0:T(128)S(1)}, f32[4]{0:T(128)}, u32[]{:S(2)}) copy-start(f32[4]{0:T(128)} %weights_ref.1) | copy-start | bytes 52

commit v3 on v2

--- a/solution.py
+++ b/solution.py
@@ -87,18 +87,17 @@
     high_ref, low_ref, inverse_ref = refs[:3]
     chunks, (p_ref, c_ref, edge_ref) = refs[3:-3], refs[-3:]
     side = chunks[0].shape[1]
-    c_ref[...] = jnp.zeros(c_ref.shape, BF16)
+    for k in range(planes):
+        c_ref[k] = jnp.zeros(c_ref.shape[1:], BF16)
     rows = label_rows(capacity)
     for chunk in chunks:
         labels = chunk[pl.ds(capacity * side, rows), :].astype(F32).astype(jnp.int32)
         for c in range(capacity):
             label = labels[c, 0]
-
-            @pl.when(label >= 0)
-            def _():
-                top = pl.multiple_of(((label >> 1) & 1) * side, side)
-                left = pl.multiple_of((label & 1) * side, side)
-                c_ref[label >> 2, pl.ds(top, side), pl.ds(left, side)] = chunk[pl.ds(c * side, side), :]
+            plane = jnp.where(label >= 0, label >> 2, planes)
+            top = pl.multiple_of(((label >> 1) & 1) * side, side)
+            left = pl.multiple_of((label & 1) * side, side)
+            c_ref[plane, pl.ds(top, side), pl.ds(left, side)] = chunk[pl.ds(c * side, side), :]
 
     high, low, inverse = high_ref[...], low_ref[...], inverse_ref[...]
     across = jnp.concatenate([high, high, low], axis=1)
@@ -118,8 +117,10 @@
     for k in range(planes):
         potential = left(*parts[k])
         p_ref[k] = potential
-        edge_ref[pl.ds(k, 1), :] = potential[:1]
-        edge_ref[pl.ds(planes + k, 1), :] = potential[2 * side - 1 :]
+        for i in range(2 * side // LANES):
+            part = potential[:, i * LANES : (i + 1) * LANES]
+            edge_ref[pl.ds(2 * i * planes + k, 1), :] = part[:1]
+            edge_ref[pl.ds((2 * i + 1) * planes + k, 1), :] = part[2 * side - 1 :]
 
 
 def shifted(a, axis, step):
@@ -137,14 +138,23 @@
     return jnp.concatenate([last, lax.slice_in_dim(rolled, tile, size, axis=axis)], axis=axis)
 
 
-def pick_kernel(planes, p_ref, c_ref, cells_ref, last_ref, out_ref):
+def pick_kernel(planes, used, p_ref, c_ref, cells_ref, *refs):
+    last_ref, out_ref = refs[-2:]
+    start = used[0]
+    if len(refs) > 2:
+        rest = refs[0][...]
+        count = rest.shape[0]
+        for i in range(3):
+            part = rest.astype(BF16)
+            last_ref[pl.ds(out_ref.shape[0] + i * count, count), :] = part
+            rest = rest - part.astype(F32)
     side = p_ref.shape[1]
     shift = side.bit_length() - 1
     groups = cells_ref.shape[0] // planes
     width = 2 if groups % 2 == 0 else 1
     sub = lax.broadcasted_iota(jnp.int32, (8, width * LANES), 0)
     column = lax.broadcasted_iota(jnp.int32, (side, width * LANES), 0)
-    for k in range(planes):
+    for k in used:
         p = p_ref[k]
         above, below = shifted(p, 0, -1), shifted(p, 0, 1)
         left, right = shifted(p, 1, -1), shifted(p, 1, 1)
@@ -169,8 +179,8 @@
                     kept = [jnp.where(bit, b, a) for a, b in zip(kept[::2], kept[1::2])]
                 value = jnp.sum(jnp.where(within, kept[0], 0.0), axis=0, keepdims=True)
                 for w in range(width):
-                    out_ref[pl.ds((k * 5 + f) * groups + g + w, 1), :] = value[:, w * LANES : (w + 1) * LANES]
-    last_ref[...] = out_ref[...].astype(last_ref.dtype)
+                    out_ref[pl.ds(((k - start) * 5 + f) * groups + g + w, 1), :] = value[:, w * LANES : (w + 1) * LANES]
+    last_ref[pl.ds(0, out_ref.shape[0]), :] = out_ref[...].astype(last_ref.dtype)
 
 
 def taken(table, index):
@@ -185,7 +195,21 @@
     return out
 
 
-def combine_kernel(tile_count, planes, side, tile_ref, weights_ref, one_ref, two_ref, cells_ref, first_ref, second_ref, out_ref):
+def edge_kernel(planes, tile_ref, ours_ref, crossed_ref, first_ref, second_ref):
+    count = ours_ref.shape[0]
+    even = (tile_ref[0] & 1) == 0
+    total = ours_ref[...]
+    begin = crossed_ref.shape[0] - 3 * count
+    for i in range(3):
+        total = total + crossed_ref[pl.ds(begin + i * count, count), :].astype(F32)
+    for i in range(count // (2 * planes)):
+        top = total[2 * i * planes : (2 * i + 1) * planes]
+        end = total[(2 * i + 1) * planes : (2 * i + 2) * planes]
+        first_ref[pl.ds(i * planes, planes), :] = jnp.where(even, end, top)
+        second_ref[pl.ds(i * planes, planes), :] = jnp.where(even, top, end)
+
+
+def combine_kernel(tile_count, planes, side, tile_ref, weights_ref, cells_ref, first_ref, second_ref, early_ref, late_ref, two_ref, out_ref):
     groups = cells_ref.shape[0] // planes
     shift = side.bit_length() - 1
     tile = tile_ref[0]
@@ -196,7 +220,10 @@
     for k in range(planes):
         cells = cells_ref[pl.ds(k * groups, groups), :]
         row, col = cells >> shift, cells & (side - 1)
-        first, second = first_ref[pl.ds(k, 1), :], second_ref[pl.ds(k, 1), :]
+        first, second = (
+            jnp.concatenate([ref[pl.ds(i * planes + k, 1), :] for i in range(side // LANES)], axis=1)
+            for ref in (first_ref, second_ref)
+        )
         above, below = jnp.where(even, second, first), jnp.where(even, first, second)
         above, below = jnp.where(starts, 0.0, above), jnp.where(ends, 0.0, below)
         at_top, at_end = row == 0, row == side - 1
@@ -208,8 +235,10 @@
         cross = 0.25 * (jnp.where(at_end, down_x, 0.0) - jnp.where(at_top, up_x, 0.0))
 
         def read(f):
-            at = pl.ds((k * 5 + f) * groups, groups)
-            return one_ref[at, :] + two_ref[at, :].astype(F32)
+            early = early_ref.shape[0] // (5 * groups)
+            one_ref, j = (early_ref, k) if k < early else (late_ref, k - early)
+            other = two_ref[pl.ds((k * 5 + f) * groups, groups), :]
+            return one_ref[pl.ds((j * 5 + f) * groups, groups), :] + other.astype(F32)
 
         weight = weights_ref[k]
         bend_x, bend_y = read(0) + 0.5 * (far - near), read(1)
@@ -282,38 +311,39 @@
             functools.partial(solve_kernel, capacity, planes),
             [
                 jax.ShapeDtypeStruct((planes, side, side), F32),
-                jax.ShapeDtypeStruct((planes, side, side), BF16),
-                jax.ShapeDtypeStruct((2 * planes, side), F32),
+                jax.ShapeDtypeStruct((planes + 1, side, side), BF16),
+                jax.ShapeDtypeStruct((2 * planes * side // LANES, LANES), F32),
             ],
             [VMEM] * (3 + len(arrays)),
         )(high, low, inverse, *arrays)
 
-    def pick(potential, mass, at, dtype):
-        shape = (planes * 5 * groups, LANES)
+    def pick(used, potential, mass, at, dtype, *edges):
+        count = len(used) * 5 * groups
         return call(
-            functools.partial(pick_kernel, planes),
-            [jax.ShapeDtypeStruct(shape, dtype)],
-            [VMEM] * 3,
-            [pltpu.VMEM(shape, F32)],
-            flops=2 * 5 * planes * side * side * rays,
-        )(potential, mass, at)[0]
-
-    potential, mass, their_edges = solve(theirs)
-    samples, their_edges = lax.optimization_barrier((pick(potential, mass, their_cells, BF16), their_edges))
-    other_edges, other_samples = swap(their_edges, half), swap(samples, half)
-    potential, mass, our_edges = solve(ours)
-    edges = our_edges + other_edges
-    even = tile[0] % 2 == 0
-    top, end = edges[:planes], edges[planes:]
-    first = swap(jnp.where(even, end, top), 1)
+            functools.partial(pick_kernel, planes, used),
+            [jax.ShapeDtypeStruct((count + sum(3 * e.shape[0] for e in edges), LANES), dtype)],
+            [VMEM] * (3 + len(edges)),
+            [pltpu.VMEM((count, LANES), F32)],
+            flops=2 * 5 * len(used) * side * side * rays,
+        )(potential, mass, at, *edges)[0]
+
+    potential, mass, edges = solve(theirs)
+    crossed = swap(pick(range(planes), potential, mass, their_cells, BF16, edges), half)
+    potential, mass, edges = solve(ours)
+    cut = planes - planes // 2
+    early = pick(range(cut), potential, mass, cells, F32)
+    crossed, early = lax.optimization_barrier((crossed, early))
+    line = jax.ShapeDtypeStruct((planes * side // LANES, LANES), F32)
+    first, second = call(functools.partial(edge_kernel, planes), [line, line], [SMEM, VMEM, VMEM])(tile, edges, crossed)
+    first = swap(first, 1)
     pairs = [(i, (i + 1) % tile_count) for i in range(1, tile_count, 2)]
-    second = lax.ppermute(jnp.where(even, top, end), "tile", pairs + [(j, i) for i, j in pairs])
-    own_samples = pick(potential, mass, cells, F32)
+    second = lax.ppermute(second, "tile", pairs + [(j, i) for i, j in pairs])
+    late = pick(range(cut, planes), potential, mass, cells, F32)
     local_map = call(
         functools.partial(combine_kernel, tile_count, planes, side),
         [jax.ShapeDtypeStruct((6 * groups, LANES), F32)],
-        [SMEM, SMEM, VMEM, VMEM, VMEM, VMEM, VMEM],
-    )(tile, lens_weights, own_samples, other_samples, cells, first, second)[0]
+        [SMEM, SMEM, VMEM, VMEM, VMEM, VMEM, VMEM, VMEM],
+    )(tile, lens_weights, cells, first, second, early, late, crossed)[0]
     maps = lax.all_gather(local_map, "depth")
     return call(
         compose_kernel,

time: 48.3 us -> 47.1 us (0.975)
  Pallas kernels: 20.1 us -> 19.1 us
    pallas_call x2, Pallas kernels: 4.97 us -> 3.57 us  [solve(): call(functools.partial(solve_kernel, capacity, planes), [jax.ShapeDtypeSt...]
    pallas_call x2 -> x4, Pallas kernels: 12.8 us -> 13.2 us  [the longest x3 13.2 us: pick(): call(functools.partial(pick_kernel, planes, used), [jax.ShapeDtypeStruct(...]
    ppermute x10 -> x9, starting transfers between devices: 11.9 us -> 11.6 us  [swap(): lax.ppermute(array, 'tile', [(i, i ^ bits) for i in range(tile_count)])]
    ppermute x10 -> x9, waiting for transfers between devices: 2.08 us -> 2.05 us  [swap(): lax.ppermute(array, 'tile', [(i, i ^ bits) for i in range(tile_count)])]
  transfers between devices with their start and end apart: 11 -> 10, of which waited for: 1 -> 2; matrix products, arithmetic and copies ran while one was open for 0% -> 0% of each run, Pallas kernels for 37% -> 36%
where the time goes in v3:
time: 47.1 us; the launch traced here: 46.9 us
  Pallas kernels  19.1 us (41%)
  starting transfers between devices  15 us (32%)
  blocking collectives  8.73 us (19%)
  waiting for transfers between devices  2.05 us (4%)
  local copies, waits for them, and re-layouts  1.95 us (4%)
    pallas_call x3, Pallas kernels, pick(): call(functools.partial(pick_kernel, planes, used), [jax.ShapeDtypeStruct(...  13.2 us
    ppermute x9, starting transfers between devices, swap(): lax.ppermute(array, 'tile', [(i, i ^ bits) for i in range(tile_count)])  11.6 us
    all_gather x1, blocking collectives, body(): maps = lax.all_gather(local_map, 'depth')  8.73 us
    pallas_call x2, Pallas kernels, solve(): call(functools.partial(solve_kernel, capacity, planes), [jax.ShapeDtypeSt...  3.57 us
    ppermute x1, starting transfers between devices, body(): second = lax.ppermute(second, 'tile', pairs + [(j, i) for i, j in pairs])  3.42 us
    ppermute x9, waiting for transfers between devices, swap(): lax.ppermute(array, 'tile', [(i, i ^ bits) for i in range(tile_count)])  2.05 us
    unnamed x18, local copies, waits for them, and re-layouts  1.92 us
  transfers between devices with their start and end apart: 10, of which 2 were waited for; matrix products, arithmetic and copies ran while one was open for 0% of the time, Pallas kernels for 36%

profile of v3, /device:TPU:0, one launch (start us, length us, event | category | flops | bytes accessed | tf_op | source)
XLA Modules:
  0.0 46.9 jit_solution(9491021464969776708)
XLA Ops:
  0.0 0.7 %copy-done.4 = s32[32]{0:T(128)S(1)} copy-done((s32[32]{0:T(128)S(1)}, s32[32]{0:T(128)}, u32[]{:S(2)}) %copy-start.4) | copy-done | bytes 152
  0.7 0.0 copy-done.5
  0.7 1.2 %copy-done = bf16[32,128,128]{2,1,0:T(8,128)(2,1)S(1)} copy-done((bf16[32,128,128]{2,1,0:T(8,128)(2,1)S(1)}, bf16[32,128,128]{2,1,0:T(8,128)(2,1)}, u32[]{:S(2)}) %copy-start) | copy-done | bytes 1048600
  1.9 0.8 %shard_map.91 = (bf16[528,128]{1,0:T(8,128)(2,1)S(1)}, bf16[528,128]{1,0:T(8,128)(2,1)S(1)}, bf16[528,128]{1,0:T(8,128)(2,1)S(1)}, bf16[528,128]{1,0:T(8,128)(2,...) custom-call(s32[1]{0:T(128)} %bitcast.1.tile_ref, ...), custom_call_target="tpu_custom_call" | custom-call | bytes 1048576 | tf_op jit(solution)/shard_map/pallas_call | solution.py:298
  2.7 3.1 %collective-permute-start.3 = (bf16[528,128]{1,0:T(8,128)(2,1)S(1)}, bf16[528,128]{1,0:T(8,128)(2,1)S(1)}, u32[]{:S(2)}, u32[]{:S(2)}) collective-permute-start(bf16[528,128]{1,0:T(8,128)(2,1)S(1)} %get-tuple-element.28), channel_id=1, source_target_pairs={{0,2},{1,3},{2,0},{3,1},{4,6},{5,7},{6,4},{7,5},{8,10},{9,11},{10,... | collective-permute-start | bytes 405512 | tf_op jit(solution)/shard_map/ppermute | solution.py:293
  5.8 0.2 collective-permute-start.5
  6.0 3.0 %collective-permute-start.6 = (s32[64,128]{1,0:T(8,128)S(1)}, s32[64,128]{1,0:T(8,128)S(1)}, u32[]{:S(2)}, u32[]{:S(2)}) collective-permute-start(s32[64,128]{1,0:T(8,128)S(1)} %reshape.17.cells_ref), channel_id=1, source_target_pairs={{0,4},{1,5},{2,6},{3,7},{4,0},{5,1},{6,2},{7,3},{8,12},{9,13},{10,... | collective-permute-start | bytes 98312 | tf_op jit(solution)/shard_map/ppermute | solution.py:293
  9.1 1.6 %collective-permute-start = (bf16[528,128]{1,0:T(8,128)(2,1)S(1)}, bf16[528,128]{1,0:T(8,128)(2,1)S(1)}, u32[]{:S(2)}, u32[]{:S(2)}) collective-permute-start(bf16[528,128]{1,0:T(8,128)(2,1)S(1)} %get-tuple-element.23), channel_id=1, source_target_pairs={{0,2},{1,3},{2,0},{3,1},{4,6},{5,7},{6,4},{7,5},{8,10},{9,11},{10,... | collective-permute-start | bytes 405512 | tf_op jit(solution)/shard_map/ppermute | solution.py:293
  10.7 0.1 collective-permute-start.1
  10.7 2.0 %collective-permute-done.4.refs_4_ = bf16[528,128]{1,0:T(8,128)(2,1)S(1)} collective-permute-done((bf16[528,128]{1,0:T(8,128)(2,1)S(1)}, bf16[528,128]{1,0:T(8,128)(2,1)S(1)}, u32[]{:S(2)}, u32[]{:S(2)}) %collective-permute-start.4) | collective-permute-done | bytes 135200 | tf_op jit(solution)/shard_map/ppermute | solution.py:293
  12.7 0.6 %collective-permute-start.2 = (bf16[528,128]{1,0:T(8,128)(2,1)S(1)}, bf16[528,128]{1,0:T(8,128)(2,1)S(1)}, u32[]{:S(2)}, u32[]{:S(2)}) collective-permute-start(bf16[528,128]{1,0:T(8,128)(2,1)S(1)} %get-tuple-element.25), channel_id=1, source_target_pairs={{0,1},{1,0},{2,3},{3,2},{4,5},{5,4},{6,7},{7,6},{8,9},{9,8},{10,11... | collective-permute-start | bytes 405512 | tf_op jit(solution)/shard_map/ppermute | solution.py:293
  13.4 1.8 %shard_map.93 = (f32[4,256,256]{2,1,0:T(8,128)S(1)}, bf16[5,256,256]{2,1,0:T(8,128)(2,1)S(1)}, f32[16,128]{1,0:T(8,128)S(1)}) custom-call(bf16[256,256]{1,0:T(8,128)(2,1)S(1)} %copy-done.2, bf16[256,256]{1,0:T(8,128)(2,1)S(1)} %copy-done.3, f32[256,256]{1,0:T(8,128)S(1)} %copy-done.1, bf16[528,128]{1,0:T(8,128)(2,1)S(1)} %collective-permute-done.3.refs_3_, ...), custom_call_target="tpu_custom_call" | custom-call | tf_op jit(solution)/shard_map/pallas_call | solution.py:310
  15.2 0.0 collective-permute-done.6.cells_ref
  15.2 6.4 %shard_map.94 = bf16[368,128]{1,0:T(8,128)(2,1)S(1)} custom-call(f32[4,256,256]{2,1,0:T(8,128)S(1)} %get-tuple-element.32.p_ref, bf16[5,256,256]{2,1,0:T(8,128)(2,1)S(1)} %get-tuple-element.33.c_ref, s32[64,128]{1,0:T(8,128)S(1)} %collective-permute-done.6.cells_ref, f32[16,128]{1,0:T(8,128)S(1)} %get-tuple-element.34.refs_0_), custom_call_target="tpu_custom_call" | custom-call | flops 5368709120 | tf_op jit(solution)/shard_map/pallas_call | solution.py:322
  21.6 2.7 %collective-permute-start.7 = (bf16[368,128]{1,0:T(8,128)(2,1)S(1)}, bf16[368,128]{1,0:T(8,128)(2,1)S(1)}, u32[]{:S(2)}, u32[]{:S(2)}) collective-permute-start(bf16[368,128]{1,0:T(8,128)(2,1)S(1)} %shard_map.94), channel_id=1, source_target_pairs={{0,4},{1,5},{2,6},{3,7},{4,0},{5,1},{6,2},{7,3},{8,12},{9,13},{10,... | collective-permute-start | bytes 282632 | tf_op jit(solution)/shard_map/ppermute | solution.py:293
  24.3 1.8 %shard_map.92 = (f32[4,256,256]{2,1,0:T(8,128)S(1)}, bf16[5,256,256]{2,1,0:T(8,128)(2,1)S(1)}, f32[16,128]{1,0:T(8,128)S(1)}) custom-call(bf16[256,256]{1,0:T(8,128)(2,1)S(1)} %copy-done.2, bf16[256,256]{1,0:T(8,128)(2,1)S(1)} %copy-done.3, f32[256,256]{1,0:T(8,128)S(1)} %copy-done.1, bf16[528,128]{1,0:T(8,128)(2,1)S(1)} %collective-permute-done.refs_3_, ...), custom_call_target="tpu_custom_call" | custom-call | tf_op jit(solution)/shard_map/pallas_call | solution.py:310
  26.1 3.5 %shard_map.95.early_ref = f32[160,128]{1,0:T(8,128)S(1)} custom-call(f32[4,256,256]{2,1,0:T(8,128)S(1)} %get-tuple-element.35.p_ref, bf16[5,256,256]{2,1,0:T(8,128)(2,1)S(1)} %get-tuple-element.36.c_ref, s32[64,128]{1,0:T(8,128)S(1)} %reshape.17.cells_ref), custom_call_target="tpu_custom_call" | custom-call | flops 2684354560 | tf_op jit(solution)/shard_map/pallas_call | solution.py:322
  29.6 0.1 collective-permute-done.7.crossed_ref.two_ref
  29.7 0.2 collective-permute-start.8
  29.9 3.4 %collective-permute-start.9 = (f32[8,128]{1,0:T(8,128)S(1)}, f32[8,128]{1,0:T(8,128)S(1)}, u32[]{:S(2)}, u32[]{:S(2)}) collective-permute-start(f32[8,128]{1,0:T(8,128)S(1)} %get-tuple-element.39), channel_id=1, source_target_pairs={{1,2},{3,4},{5,6},{7,0},{2,1},{4,3},{6,5},{0,7},{9,10},{11,12},{13... | collective-permute-start | bytes 12296 | tf_op jit(solution)/shard_map/ppermute | solution.py:340
  33.4 3.3 %shard_map.97.late_ref = f32[160,128]{1,0:T(8,128)S(1)} custom-call(f32[4,256,256]{2,1,0:T(8,128)S(1)} %get-tuple-element.35.p_ref, bf16[5,256,256]{2,1,0:T(8,128)(2,1)S(1)} %get-tuple-element.36.c_ref, s32[64,128]{1,0:T(8,128)S(1)} %reshape.17.cells_ref), custom_call_target="tpu_custom_call" | custom-call | flops 2684354560 | tf_op jit(solution)/shard_map/pallas_call | solution.py:322
  36.7 0.8 %shard_map.98 = f32[96,128]{1,0:T(8,128)S(1)} custom-call(s32[1]{0:T(128)} %bitcast.1.tile_ref, f32[4]{0:T(128)S(1)} %copy-done.6, s32[64,128]{1,0:T(8,128)S(1)} %reshape.17.cells_ref, f32[8,128]{1,0:T(8,128)S(1)} %collective-permute-done.8.first_ref, f32[8,128]{1,0:T(8,128)S(1)} %collective-permute-done.9.second_ref, f32[160,128]{1,0:T(8,128)S(1)} %shard_map.95.early_ref, ...), custom_call_target="tpu_custom_call" | custom-call | tf_op jit(solution)/shard_map/pallas_call | solution.py:342
  37.5 8.7 %all-gather = f32[384,128]{1,0:T(8,128)S(1)} all-gather(f32[96,128]{1,0:T(8,128)S(1)} %shard_map.98), channel_id=2, replica_groups=mesh['depth'=4,'tile'=8] {'depth'}, dimensions={0}, use_global_device_ids=true | all-gather | bytes 245760 | tf_op jit(solution)/shard_map/all_gather | solution.py:347
  46.3 0.6 %shard_map.99 = f32[96,128]{1,0:T(8,128)} custom-call(s32[1]{0:T(128)} %bitcast.depth_ref, f32[4,96,128]{2,1,0:T(8,128)S(1)} %bitcast.4, f32[32,128]{1,0:T(8,128)S(1)} %reshape.18.angles_ref), custom_call_target="tpu_custom_call" | custom-call | tf_op jit(solution)/shard_map/pallas_call | solution.py:348
  (26 shorter events, 0.1 us)
Async XLA Ops:
  0.0 0.7 %copy-start.4 = (s32[32]{0:T(128)S(1)}, s32[32]{0:T(128)}, u32[]{:S(2)}) copy-start(s32[32]{0:T(128)} %owner_ref.1) | copy-start | bytes 388
  0.0 0.7 %copy-start.5 = (s32[32]{0:T(128)S(1)}, s32[32]{0:T(128)}, u32[]{:S(2)}) copy-start(s32[32]{0:T(128)} %place_ref.1) | copy-start | bytes 388
  0.7 1.2 %copy-start = (bf16[32,128,128]{2,1,0:T(8,128)(2,1)S(1)}, bf16[32,128,128]{2,1,0:T(8,128)(2,1)}, u32[]{:S(2)}) copy-start(bf16[32,128,128]{2,1,0:T(8,128)(2,1)} %blocks_ref.1) | copy-start | bytes 3145732
  1.9 4.1 %copy-start.7 = (s32[4,2048]{1,0:T(4,128)S(1)}, s32[4,2048]{1,0:T(4,128)}, u32[]{:S(2)}) copy-start(s32[4,2048]{1,0:T(4,128)} %param.13) | copy-start | bytes 98308
  1.9 11.4 %copy-start.1 = (f32[256,256]{1,0:T(8,128)S(1)}, f32[256,256]{1,0:T(8,128)}, u32[]{:S(2)}) copy-start(f32[256,256]{1,0:T(8,128)} %constant.16.clone.refs_2_) | copy-start | bytes 786436
  1.9 11.4 %copy-start.2 = (bf16[256,256]{1,0:T(8,128)(2,1)S(1)}, bf16[256,256]{1,0:T(8,128)(2,1)}, u32[]{:S(2)}) copy-start(bf16[256,256]{1,0:T(8,128)(2,1)} %constant.14.clone.refs_0_) | copy-start | bytes 393220
  1.9 11.4 %copy-start.3 = (bf16[256,256]{1,0:T(8,128)(2,1)S(1)}, bf16[256,256]{1,0:T(8,128)(2,1)}, u32[]{:S(2)}) copy-start(bf16[256,256]{1,0:T(8,128)(2,1)} %constant.15.clone.refs_1_) | copy-start | bytes 393220
  2.7 7.9 %collective-permute-start.3 = (bf16[528,128]{1,0:T(8,128)(2,1)S(1)}, bf16[528,128]{1,0:T(8,128)(2,1)S(1)}, u32[]{:S(2)}, u32[]{:S(2)}) collective-permute-start(bf16[528,128]{1,0:T(8,128)(2,1)S(1)} %get-tuple-element.28), channel_id=1, source_target_pairs={{0,2},{1,3},{2,0},{3,1},{4,6},{5,7},{6,4},{7,5},{8,10},{9,11},{10,... | collective-permute-start | bytes 405512 | tf_op jit(solution)/shard_map/ppermute | solution.py:293
  5.8 6.9 %collective-permute-start.4 = (bf16[528,128]{1,0:T(8,128)(2,1)S(1)}, bf16[528,128]{1,0:T(8,128)(2,1)S(1)}, u32[]{:S(2)}, u32[]{:S(2)}) collective-permute-start(bf16[528,128]{1,0:T(8,128)(2,1)S(1)} %get-tuple-element.29), channel_id=1, source_target_pairs={{0,3},{1,2},{2,1},{3,0},{4,7},{5,6},{6,5},{7,4},{8,11},{9,10},{10,... | collective-permute-start | bytes 405512 | tf_op jit(solution)/shard_map/ppermute | solution.py:293
  5.8 7.5 %collective-permute-start.5 = (bf16[528,128]{1,0:T(8,128)(2,1)S(1)}, bf16[528,128]{1,0:T(8,128)(2,1)S(1)}, u32[]{:S(2)}, u32[]{:S(2)}) collective-permute-start(bf16[528,128]{1,0:T(8,128)(2,1)S(1)} %get-tuple-element.30), channel_id=1, source_target_pairs={{0,1},{1,0},{2,3},{3,2},{4,5},{5,4},{6,7},{7,6},{8,9},{9,8},{10,11... | collective-permute-start | bytes 405512 | tf_op jit(solution)/shard_map/ppermute | solution.py:293
  6.0 4.6 %copy-start.8 = (f32[2,2048]{1,0:T(2,128)S(1)}, f32[2,2048]{1,0:T(2,128)}, u32[]{:S(2)}) copy-start(f32[2,2048]{1,0:T(2,128)} %param.14) | copy-start | bytes 49156
  6.0 9.1 %collective-permute-start.6 = (s32[64,128]{1,0:T(8,128)S(1)}, s32[64,128]{1,0:T(8,128)S(1)}, u32[]{:S(2)}, u32[]{:S(2)}) collective-permute-start(s32[64,128]{1,0:T(8,128)S(1)} %reshape.17.cells_ref), channel_id=1, source_target_pairs={{0,4},{1,5},{2,6},{3,7},{4,0},{5,1},{6,2},{7,3},{8,12},{9,13},{10,... | collective-permute-start | bytes 98312 | tf_op jit(solution)/shard_map/ppermute | solution.py:293
  9.1 15.3 %collective-permute-start = (bf16[528,128]{1,0:T(8,128)(2,1)S(1)}, bf16[528,128]{1,0:T(8,128)(2,1)S(1)}, u32[]{:S(2)}, u32[]{:S(2)}) collective-permute-start(bf16[528,128]{1,0:T(8,128)(2,1)S(1)} %get-tuple-element.23), channel_id=1, source_target_pairs={{0,2},{1,3},{2,0},{3,1},{4,6},{5,7},{6,4},{7,5},{8,10},{9,11},{10,... | collective-permute-start | bytes 405512 | tf_op jit(solution)/shard_map/ppermute | solution.py:293
  10.7 13.6 %collective-permute-start.1 = (bf16[528,128]{1,0:T(8,128)(2,1)S(1)}, bf16[528,128]{1,0:T(8,128)(2,1)S(1)}, u32[]{:S(2)}, u32[]{:S(2)}) collective-permute-start(bf16[528,128]{1,0:T(8,128)(2,1)S(1)} %get-tuple-element.24), channel_id=1, source_target_pairs={{0,3},{1,2},{2,1},{3,0},{4,7},{5,6},{6,5},{7,4},{8,11},{9,10},{10,... | collective-permute-start | bytes 405512 | tf_op jit(solution)/shard_map/ppermute | solution.py:293
  12.7 11.6 %collective-permute-start.2 = (bf16[528,128]{1,0:T(8,128)(2,1)S(1)}, bf16[528,128]{1,0:T(8,128)(2,1)S(1)}, u32[]{:S(2)}, u32[]{:S(2)}) collective-permute-start(bf16[528,128]{1,0:T(8,128)(2,1)S(1)} %get-tuple-element.25), channel_id=1, source_target_pairs={{0,1},{1,0},{2,3},{3,2},{4,5},{5,4},{6,7},{7,6},{8,9},{9,8},{10,11... | collective-permute-start | bytes 405512 | tf_op jit(solution)/shard_map/ppermute | solution.py:293
  21.6 8.1 %collective-permute-start.7 = (bf16[368,128]{1,0:T(8,128)(2,1)S(1)}, bf16[368,128]{1,0:T(8,128)(2,1)S(1)}, u32[]{:S(2)}, u32[]{:S(2)}) collective-permute-start(bf16[368,128]{1,0:T(8,128)(2,1)S(1)} %shard_map.94), channel_id=1, source_target_pairs={{0,4},{1,5},{2,6},{3,7},{4,0},{5,1},{6,2},{7,3},{8,12},{9,13},{10,... | collective-permute-start | bytes 282632 | tf_op jit(solution)/shard_map/ppermute | solution.py:293
  29.7 7.0 %collective-permute-start.8 = (f32[8,128]{1,0:T(8,128)S(1)}, f32[8,128]{1,0:T(8,128)S(1)}, u32[]{:S(2)}, u32[]{:S(2)}) collective-permute-start(f32[8,128]{1,0:T(8,128)S(1)} %get-tuple-element.38), channel_id=1, source_target_pairs={{0,1},{1,0},{2,3},{3,2},{4,5},{5,4},{6,7},{7,6},{8,9},{9,8},{10,11... | collective-permute-start | bytes 12296 | tf_op jit(solution)/shard_map/ppermute | solution.py:293
  29.9 6.8 %copy-start.6 = (f32[4]{0:T(128)S(1)}, f32[4]{0:T(128)}, u32[]{:S(2)}) copy-start(f32[4]{0:T(128)} %weights_ref.1) | copy-start | bytes 52
  29.9 6.8 %collective-permute-start.9 = (f32[8,128]{1,0:T(8,128)S(1)}, f32[8,128]{1,0:T(8,128)S(1)}, u32[]{:S(2)}, u32[]{:S(2)}) collective-permute-start(f32[8,128]{1,0:T(8,128)S(1)} %get-tuple-element.39), channel_id=1, source_target_pairs={{1,2},{3,4},{5,6},{7,0},{2,1},{4,3},{6,5},{0,7},{9,10},{11,12},{13... | collective-permute-start | bytes 12296 | tf_op jit(solution)/shard_map/ppermute | solution.py:340

commit v4 on v3

--- a/solution.py
+++ b/solution.py
@@ -253,10 +253,12 @@
         out_ref[pl.ds(i * groups, groups), :] = value
 
 
-def compose_kernel(depth_ref, maps_ref, angles_ref, out_ref):
-    count = maps_ref.shape[0]
+def compose_kernel(count, depth_ref, *refs):
+    angles_ref, out_ref, maps_ref = refs[count:]
     groups = maps_ref.shape[1] // 6
     depth = depth_ref[0]
+    for i in range(count):
+        maps_ref[depth ^ i] = refs[i][...]
 
     def part(d, i):
         return maps_ref[d, pl.ds(i * groups, groups), :]
@@ -344,12 +346,15 @@
         [jax.ShapeDtypeStruct((6 * groups, LANES), F32)],
         [SMEM, SMEM, VMEM, VMEM, VMEM, VMEM, VMEM, VMEM],
     )(tile, lens_weights, cells, first, second, early, late, crossed)[0]
-    maps = lax.all_gather(local_map, "depth")
+    count = lax.axis_size("depth")
+    maps = [local_map]
+    maps += [lax.ppermute(local_map, "depth", [(i, i ^ d) for i in range(count)]) for d in range(1, count)]
     return call(
-        compose_kernel,
+        functools.partial(compose_kernel, count),
         [jax.ShapeDtypeStruct((6 * groups, LANES), F32)],
-        [SMEM, VMEM, VMEM],
-    )(depth, maps, angles)[0].reshape(1, 6, rays)
+        [SMEM] + [VMEM] * (count + 1),
+        [pltpu.VMEM((count, 6 * groups, LANES), F32)],
+    )(depth, *maps, angles)[0].reshape(1, 6, rays)
 
 
 def solution(mesh):

time: 47.1 us -> 46.4 us (0.985)
  blocking collectives: 8.73 us -> 0 us
  waiting for transfers between devices: 2.05 us -> 6.66 us
  starting transfers between devices: 15 us -> 18.5 us
    all_gather x1 -> x0, blocking collectives: 8.73 us -> none  [body(): maps = lax.all_gather(local_map, 'depth')]
    ppermute x0 -> x3, waiting for transfers between devices: none -> 4.49 us  [body(): lax.ppermute(local_map, 'depth', [(i, i ^ d) for i in range(count)])]
    ppermute x0 -> x3, starting transfers between devices: none -> 3.55 us  [body(): lax.ppermute(local_map, 'depth', [(i, i ^ d) for i in range(count)])]
  transfers between devices with their start and end apart: 10 -> 13, of which waited for: 2 -> 5; matrix products, arithmetic and copies ran while one was open for 0% -> 0% of each run, Pallas kernels for 36% -> 36%
where the time goes in v4:
time: 46.4 us; the launch traced here: 46.3 us
  Pallas kernels  19.1 us (41%)
  starting transfers between devices  18.5 us (40%)
  waiting for transfers between devices  6.66 us (14%)
  local copies, waits for them, and re-layouts  1.95 us (4%)
    pallas_call x3, Pallas kernels, pick(): call(functools.partial(pick_kernel, planes, used), [jax.ShapeDtypeStruct(...  13.2 us
    ppermute x9, starting transfers between devices, swap(): lax.ppermute(array, 'tile', [(i, i ^ bits) for i in range(tile_count)])  11.5 us
    ppermute x3, waiting for transfers between devices, body(): lax.ppermute(local_map, 'depth', [(i, i ^ d) for i in range(count)])  4.49 us
    pallas_call x2, Pallas kernels, solve(): call(functools.partial(solve_kernel, capacity, planes), [jax.ShapeDtypeSt...  3.57 us
    ppermute x3, starting transfers between devices, body(): lax.ppermute(local_map, 'depth', [(i, i ^ d) for i in range(count)])  3.55 us
    ppermute x1, starting transfers between devices, body(): second = lax.ppermute(second, 'tile', pairs + [(j, i) for i, j in pairs])  3.44 us
    ppermute x9, waiting for transfers between devices, swap(): lax.ppermute(array, 'tile', [(i, i ^ bits) for i in range(tile_count)])  2.17 us
    unnamed x18, local copies, waits for them, and re-layouts  1.92 us
  transfers between devices with their start and end apart: 13, of which 5 were waited for; matrix products, arithmetic and copies ran while one was open for 0% of the time, Pallas kernels for 36%

profile of v4, /device:TPU:0, one launch (start us, length us, event | category | flops | bytes accessed | tf_op | source)
XLA Modules:
  0.0 46.3 jit_solution(13775989430573501706)
XLA Ops:
  0.0 0.7 %copy-done.4 = s32[32]{0:T(128)S(1)} copy-done((s32[32]{0:T(128)S(1)}, s32[32]{0:T(128)}, u32[]{:S(2)}) %copy-start.4) | copy-done | bytes 152
  0.7 1.2 %copy-done = bf16[32,128,128]{2,1,0:T(8,128)(2,1)S(1)} copy-done((bf16[32,128,128]{2,1,0:T(8,128)(2,1)S(1)}, bf16[32,128,128]{2,1,0:T(8,128)(2,1)}, u32[]{:S(2)}) %copy-start) | copy-done | bytes 1048600
  1.9 0.8 %shard_map.91 = (bf16[528,128]{1,0:T(8,128)(2,1)S(1)}, bf16[528,128]{1,0:T(8,128)(2,1)S(1)}, bf16[528,128]{1,0:T(8,128)(2,1)S(1)}, bf16[528,128]{1,0:T(8,128)(2,...) custom-call(s32[1]{0:T(128)} %bitcast.1.tile_ref, ...), custom_call_target="tpu_custom_call" | custom-call | bytes 1048576 | tf_op jit(solution)/shard_map/pallas_call | solution.py:300
  2.7 3.1 %collective-permute-start.3 = (bf16[528,128]{1,0:T(8,128)(2,1)S(1)}, bf16[528,128]{1,0:T(8,128)(2,1)S(1)}, u32[]{:S(2)}, u32[]{:S(2)}) collective-permute-start(bf16[528,128]{1,0:T(8,128)(2,1)S(1)} %get-tuple-element.28), channel_id=1, source_target_pairs={{0,2},{1,3},{2,0},{3,1},{4,6},{5,7},{6,4},{7,5},{8,10},{9,11},{10,... | collective-permute-start | bytes 405512 | tf_op jit(solution)/shard_map/ppermute | solution.py:295
  6.0 3.0 %collective-permute-start.6 = (s32[64,128]{1,0:T(8,128)S(1)}, s32[64,128]{1,0:T(8,128)S(1)}, u32[]{:S(2)}, u32[]{:S(2)}) collective-permute-start(s32[64,128]{1,0:T(8,128)S(1)} %reshape.17.cells_ref), channel_id=1, source_target_pairs={{0,4},{1,5},{2,6},{3,7},{4,0},{5,1},{6,2},{7,3},{8,12},{9,13},{10,... | collective-permute-start | bytes 98312 | tf_op jit(solution)/shard_map/ppermute | solution.py:295
  9.0 1.6 %collective-permute-start = (bf16[528,128]{1,0:T(8,128)(2,1)S(1)}, bf16[528,128]{1,0:T(8,128)(2,1)S(1)}, u32[]{:S(2)}, u32[]{:S(2)}) collective-permute-start(bf16[528,128]{1,0:T(8,128)(2,1)S(1)} %get-tuple-element.23), channel_id=1, source_target_pairs={{0,2},{1,3},{2,0},{3,1},{4,6},{5,7},{6,4},{7,5},{8,10},{9,11},{10,... | collective-permute-start | bytes 405512 | tf_op jit(solution)/shard_map/ppermute | solution.py:295
  10.6 2.1 %collective-permute-done.4.refs_4_ = bf16[528,128]{1,0:T(8,128)(2,1)S(1)} collective-permute-done((bf16[528,128]{1,0:T(8,128)(2,1)S(1)}, bf16[528,128]{1,0:T(8,128)(2,1)S(1)}, u32[]{:S(2)}, u32[]{:S(2)}) %collective-permute-start.4) | collective-permute-done | bytes 135200 | tf_op jit(solution)/shard_map/ppermute | solution.py:295
  12.7 0.6 %collective-permute-start.2 = (bf16[528,128]{1,0:T(8,128)(2,1)S(1)}, bf16[528,128]{1,0:T(8,128)(2,1)S(1)}, u32[]{:S(2)}, u32[]{:S(2)}) collective-permute-start(bf16[528,128]{1,0:T(8,128)(2,1)S(1)} %get-tuple-element.25), channel_id=1, source_target_pairs={{0,1},{1,0},{2,3},{3,2},{4,5},{5,4},{6,7},{7,6},{8,9},{9,8},{10,11... | collective-permute-start | bytes 405512 | tf_op jit(solution)/shard_map/ppermute | solution.py:295
  13.4 1.8 %shard_map.93 = (f32[4,256,256]{2,1,0:T(8,128)S(1)}, bf16[5,256,256]{2,1,0:T(8,128)(2,1)S(1)}, f32[16,128]{1,0:T(8,128)S(1)}) custom-call(bf16[256,256]{1,0:T(8,128)(2,1)S(1)} %copy-done.2, bf16[256,256]{1,0:T(8,128)(2,1)S(1)} %copy-done.3, f32[256,256]{1,0:T(8,128)S(1)} %copy-done.1, bf16[528,128]{1,0:T(8,128)(2,1)S(1)} %collective-permute-done.3.refs_3_, ...), custom_call_target="tpu_custom_call" | custom-call | tf_op jit(solution)/shard_map/pallas_call | solution.py:312
  15.2 6.4 %shard_map.94 = bf16[368,128]{1,0:T(8,128)(2,1)S(1)} custom-call(f32[4,256,256]{2,1,0:T(8,128)S(1)} %get-tuple-element.32.p_ref, bf16[5,256,256]{2,1,0:T(8,128)(2,1)S(1)} %get-tuple-element.33.c_ref, s32[64,128]{1,0:T(8,128)S(1)} %collective-permute-done.6.cells_ref, f32[16,128]{1,0:T(8,128)S(1)} %get-tuple-element.34.refs_0_), custom_call_target="tpu_custom_call" | custom-call | flops 5368709120 | tf_op jit(solution)/shard_map/pallas_call | solution.py:324
  21.6 2.7 %collective-permute-start.7 = (bf16[368,128]{1,0:T(8,128)(2,1)S(1)}, bf16[368,128]{1,0:T(8,128)(2,1)S(1)}, u32[]{:S(2)}, u32[]{:S(2)}) collective-permute-start(bf16[368,128]{1,0:T(8,128)(2,1)S(1)} %shard_map.94), channel_id=1, source_target_pairs={{0,4},{1,5},{2,6},{3,7},{4,0},{5,1},{6,2},{7,3},{8,12},{9,13},{10,... | collective-permute-start | bytes 282632 | tf_op jit(solution)/shard_map/ppermute | solution.py:295
  24.3 1.8 %shard_map.92 = (f32[4,256,256]{2,1,0:T(8,128)S(1)}, bf16[5,256,256]{2,1,0:T(8,128)(2,1)S(1)}, f32[16,128]{1,0:T(8,128)S(1)}) custom-call(bf16[256,256]{1,0:T(8,128)(2,1)S(1)} %copy-done.2, bf16[256,256]{1,0:T(8,128)(2,1)S(1)} %copy-done.3, f32[256,256]{1,0:T(8,128)S(1)} %copy-done.1, bf16[528,128]{1,0:T(8,128)(2,1)S(1)} %collective-permute-done.refs_3_, ...), custom_call_target="tpu_custom_call" | custom-call | tf_op jit(solution)/shard_map/pallas_call | solution.py:312
  26.1 3.5 %shard_map.95.early_ref = f32[160,128]{1,0:T(8,128)S(1)} custom-call(f32[4,256,256]{2,1,0:T(8,128)S(1)} %get-tuple-element.35.p_ref, bf16[5,256,256]{2,1,0:T(8,128)(2,1)S(1)} %get-tuple-element.36.c_ref, s32[64,128]{1,0:T(8,128)S(1)} %reshape.17.cells_ref), custom_call_target="tpu_custom_call" | custom-call | flops 2684354560 | tf_op jit(solution)/shard_map/pallas_call | solution.py:324
  29.7 0.2 collective-permute-start.8
  29.9 3.4 %collective-permute-start.9 = (f32[8,128]{1,0:T(8,128)S(1)}, f32[8,128]{1,0:T(8,128)S(1)}, u32[]{:S(2)}, u32[]{:S(2)}) collective-permute-start(f32[8,128]{1,0:T(8,128)S(1)} %get-tuple-element.39), channel_id=1, source_target_pairs={{1,2},{3,4},{5,6},{7,0},{2,1},{4,3},{6,5},{0,7},{9,10},{11,12},{13... | collective-permute-start | bytes 12296 | tf_op jit(solution)/shard_map/ppermute | solution.py:342
  33.4 3.3 %shard_map.97.late_ref = f32[160,128]{1,0:T(8,128)S(1)} custom-call(f32[4,256,256]{2,1,0:T(8,128)S(1)} %get-tuple-element.35.p_ref, bf16[5,256,256]{2,1,0:T(8,128)(2,1)S(1)} %get-tuple-element.36.c_ref, s32[64,128]{1,0:T(8,128)S(1)} %reshape.17.cells_ref), custom_call_target="tpu_custom_call" | custom-call | flops 2684354560 | tf_op jit(solution)/shard_map/pallas_call | solution.py:324
  36.7 0.8 %shard_map.98.refs_0_ = f32[96,128]{1,0:T(8,128)S(1)} custom-call(s32[1]{0:T(128)} %bitcast.1.tile_ref, f32[4]{0:T(128)S(1)} %copy-done.6, s32[64,128]{1,0:T(8,128)S(1)} %reshape.17.cells_ref, f32[8,128]{1,0:T(8,128)S(1)} %collective-permute-done.8.first_ref, f32[8,128]{1,0:T(8,128)S(1)} %collective-permute-done.9.second_ref, ...), custom_call_target="tpu_custom_call" | custom-call | tf_op jit(solution)/shard_map/pallas_call | solution.py:344
  37.5 1.6 %collective-permute-start.10 = (f32[96,128]{1,0:T(8,128)S(1)}, f32[96,128]{1,0:T(8,128)S(1)}, u32[]{:S(2)}, u32[]{:S(2)}) collective-permute-start(f32[96,128]{1,0:T(8,128)S(1)} %shard_map.98.refs_0_), channel_id=1, source_target_pairs={{0,8},{8,0},{16,24},{24,16},{1,9},{9,1},{17,25},{25,17},{2,10},{10... | collective-permute-start | bytes 147464 | tf_op jit(solution)/shard_map/ppermute | solution.py:351
  39.1 1.5 %collective-permute-start.11 = (f32[96,128]{1,0:T(8,128)S(1)}, f32[96,128]{1,0:T(8,128)S(1)}, u32[]{:S(2)}, u32[]{:S(2)}) collective-permute-start(f32[96,128]{1,0:T(8,128)S(1)} %shard_map.98.refs_0_), channel_id=1, source_target_pairs={{0,16},{8,24},{16,0},{24,8},{1,17},{9,25},{17,1},{25,9},{2,18},{10... | collective-permute-start | bytes 147464 | tf_op jit(solution)/shard_map/ppermute | solution.py:351
  40.6 0.5 %collective-permute-start.12 = (f32[96,128]{1,0:T(8,128)S(1)}, f32[96,128]{1,0:T(8,128)S(1)}, u32[]{:S(2)}, u32[]{:S(2)}) collective-permute-start(f32[96,128]{1,0:T(8,128)S(1)} %shard_map.98.refs_0_), channel_id=1, source_target_pairs={{0,24},{8,16},{16,8},{24,0},{1,25},{9,17},{17,9},{25,1},{2,26},{10... | collective-permute-start | bytes 147464 | tf_op jit(solution)/shard_map/ppermute | solution.py:351
  41.1 0.8 %collective-permute-done.10.refs_1_ = f32[96,128]{1,0:T(8,128)S(1)} collective-permute-done((f32[96,128]{1,0:T(8,128)S(1)}, f32[96,128]{1,0:T(8,128)S(1)}, u32[]{:S(2)}, u32[]{:S(2)}) %collective-permute-start.10) | collective-permute-done | bytes 49184 | tf_op jit(solution)/shard_map/ppermute | solution.py:351
  42.0 1.6 %collective-permute-done.11.refs_2_ = f32[96,128]{1,0:T(8,128)S(1)} collective-permute-done((f32[96,128]{1,0:T(8,128)S(1)}, f32[96,128]{1,0:T(8,128)S(1)}, u32[]{:S(2)}, u32[]{:S(2)}) %collective-permute-start.11) | collective-permute-done | bytes 49184 | tf_op jit(solution)/shard_map/ppermute | solution.py:351
  43.6 2.0 %collective-permute-done.12.refs_3_ = f32[96,128]{1,0:T(8,128)S(1)} collective-permute-done((f32[96,128]{1,0:T(8,128)S(1)}, f32[96,128]{1,0:T(8,128)S(1)}, u32[]{:S(2)}, u32[]{:S(2)}) %collective-permute-start.12) | collective-permute-done | bytes 49184 | tf_op jit(solution)/shard_map/ppermute | solution.py:351
  45.6 0.7 %shard_map.99 = f32[96,128]{1,0:T(8,128)} custom-call(s32[1]{0:T(128)} %bitcast.depth_ref, f32[96,128]{1,0:T(8,128)S(1)} %shard_map.98.refs_0_, f32[96,128]{1,0:T(8,128)S(1)} %collective-permute-done.10.refs_1_, f32[96,128]{1,0:T(8,128)S(1)} %collective-permute-done.11.refs_2_, f32[96,128]{1,0:T(8,128)S(1)} %collective-permute-done.12.refs_3_, ...), custom_call_target="tpu_custom_call" | custom-call | tf_op jit(solution)/shard_map/pallas_call | solution.py:352
  (31 shorter events, 0.4 us)
Async XLA Ops:
  0.0 0.7 %copy-start.4 = (s32[32]{0:T(128)S(1)}, s32[32]{0:T(128)}, u32[]{:S(2)}) copy-start(s32[32]{0:T(128)} %owner_ref.1) | copy-start | bytes 388
  0.0 0.7 %copy-start.5 = (s32[32]{0:T(128)S(1)}, s32[32]{0:T(128)}, u32[]{:S(2)}) copy-start(s32[32]{0:T(128)} %place_ref.1) | copy-start | bytes 388
  0.7 1.2 %copy-start = (bf16[32,128,128]{2,1,0:T(8,128)(2,1)S(1)}, bf16[32,128,128]{2,1,0:T(8,128)(2,1)}, u32[]{:S(2)}) copy-start(bf16[32,128,128]{2,1,0:T(8,128)(2,1)} %blocks_ref.1) | copy-start | bytes 3145732
  1.9 4.1 %copy-start.7 = (s32[4,2048]{1,0:T(4,128)S(1)}, s32[4,2048]{1,0:T(4,128)}, u32[]{:S(2)}) copy-start(s32[4,2048]{1,0:T(4,128)} %param.13) | copy-start | bytes 98308
  1.9 11.4 %copy-start.1 = (f32[256,256]{1,0:T(8,128)S(1)}, f32[256,256]{1,0:T(8,128)}, u32[]{:S(2)}) copy-start(f32[256,256]{1,0:T(8,128)} %constant.16.clone.refs_2_) | copy-start | bytes 786436
  1.9 11.4 %copy-start.2 = (bf16[256,256]{1,0:T(8,128)(2,1)S(1)}, bf16[256,256]{1,0:T(8,128)(2,1)}, u32[]{:S(2)}) copy-start(bf16[256,256]{1,0:T(8,128)(2,1)} %constant.14.clone.refs_0_) | copy-start | bytes 393220
  1.9 11.4 %copy-start.3 = (bf16[256,256]{1,0:T(8,128)(2,1)S(1)}, bf16[256,256]{1,0:T(8,128)(2,1)}, u32[]{:S(2)}) copy-start(bf16[256,256]{1,0:T(8,128)(2,1)} %constant.15.clone.refs_1_) | copy-start | bytes 393220
  2.7 7.9 %collective-permute-start.3 = (bf16[528,128]{1,0:T(8,128)(2,1)S(1)}, bf16[528,128]{1,0:T(8,128)(2,1)S(1)}, u32[]{:S(2)}, u32[]{:S(2)}) collective-permute-start(bf16[528,128]{1,0:T(8,128)(2,1)S(1)} %get-tuple-element.28), channel_id=1, source_target_pairs={{0,2},{1,3},{2,0},{3,1},{4,6},{5,7},{6,4},{7,5},{8,10},{9,11},{10,... | collective-permute-start | bytes 405512 | tf_op jit(solution)/shard_map/ppermute | solution.py:295
  5.8 6.9 %collective-permute-start.4 = (bf16[528,128]{1,0:T(8,128)(2,1)S(1)}, bf16[528,128]{1,0:T(8,128)(2,1)S(1)}, u32[]{:S(2)}, u32[]{:S(2)}) collective-permute-start(bf16[528,128]{1,0:T(8,128)(2,1)S(1)} %get-tuple-element.29), channel_id=1, source_target_pairs={{0,3},{1,2},{2,1},{3,0},{4,7},{5,6},{6,5},{7,4},{8,11},{9,10},{10,... | collective-permute-start | bytes 405512 | tf_op jit(solution)/shard_map/ppermute | solution.py:295
  5.8 7.5 %collective-permute-start.5 = (bf16[528,128]{1,0:T(8,128)(2,1)S(1)}, bf16[528,128]{1,0:T(8,128)(2,1)S(1)}, u32[]{:S(2)}, u32[]{:S(2)}) collective-permute-start(bf16[528,128]{1,0:T(8,128)(2,1)S(1)} %get-tuple-element.30), channel_id=1, source_target_pairs={{0,1},{1,0},{2,3},{3,2},{4,5},{5,4},{6,7},{7,6},{8,9},{9,8},{10,11... | collective-permute-start | bytes 405512 | tf_op jit(solution)/shard_map/ppermute | solution.py:295
  6.0 9.1 %collective-permute-start.6 = (s32[64,128]{1,0:T(8,128)S(1)}, s32[64,128]{1,0:T(8,128)S(1)}, u32[]{:S(2)}, u32[]{:S(2)}) collective-permute-start(s32[64,128]{1,0:T(8,128)S(1)} %reshape.17.cells_ref), channel_id=1, source_target_pairs={{0,4},{1,5},{2,6},{3,7},{4,0},{5,1},{6,2},{7,3},{8,12},{9,13},{10,... | collective-permute-start | bytes 98312 | tf_op jit(solution)/shard_map/ppermute | solution.py:295
  9.0 15.3 %collective-permute-start = (bf16[528,128]{1,0:T(8,128)(2,1)S(1)}, bf16[528,128]{1,0:T(8,128)(2,1)S(1)}, u32[]{:S(2)}, u32[]{:S(2)}) collective-permute-start(bf16[528,128]{1,0:T(8,128)(2,1)S(1)} %get-tuple-element.23), channel_id=1, source_target_pairs={{0,2},{1,3},{2,0},{3,1},{4,6},{5,7},{6,4},{7,5},{8,10},{9,11},{10,... | collective-permute-start | bytes 405512 | tf_op jit(solution)/shard_map/ppermute | solution.py:295
  10.6 13.7 %collective-permute-start.1 = (bf16[528,128]{1,0:T(8,128)(2,1)S(1)}, bf16[528,128]{1,0:T(8,128)(2,1)S(1)}, u32[]{:S(2)}, u32[]{:S(2)}) collective-permute-start(bf16[528,128]{1,0:T(8,128)(2,1)S(1)} %get-tuple-element.24), channel_id=1, source_target_pairs={{0,3},{1,2},{2,1},{3,0},{4,7},{5,6},{6,5},{7,4},{8,11},{9,10},{10,... | collective-permute-start | bytes 405512 | tf_op jit(solution)/shard_map/ppermute | solution.py:295
  12.7 11.6 %collective-permute-start.2 = (bf16[528,128]{1,0:T(8,128)(2,1)S(1)}, bf16[528,128]{1,0:T(8,128)(2,1)S(1)}, u32[]{:S(2)}, u32[]{:S(2)}) collective-permute-start(bf16[528,128]{1,0:T(8,128)(2,1)S(1)} %get-tuple-element.25), channel_id=1, source_target_pairs={{0,1},{1,0},{2,3},{3,2},{4,5},{5,4},{6,7},{7,6},{8,9},{9,8},{10,11... | collective-permute-start | bytes 405512 | tf_op jit(solution)/shard_map/ppermute | solution.py:295
  21.6 8.1 %collective-permute-start.7 = (bf16[368,128]{1,0:T(8,128)(2,1)S(1)}, bf16[368,128]{1,0:T(8,128)(2,1)S(1)}, u32[]{:S(2)}, u32[]{:S(2)}) collective-permute-start(bf16[368,128]{1,0:T(8,128)(2,1)S(1)} %shard_map.94), channel_id=1, source_target_pairs={{0,4},{1,5},{2,6},{3,7},{4,0},{5,1},{6,2},{7,3},{8,12},{9,13},{10,... | collective-permute-start | bytes 282632 | tf_op jit(solution)/shard_map/ppermute | solution.py:295
  29.7 7.0 %collective-permute-start.8 = (f32[8,128]{1,0:T(8,128)S(1)}, f32[8,128]{1,0:T(8,128)S(1)}, u32[]{:S(2)}, u32[]{:S(2)}) collective-permute-start(f32[8,128]{1,0:T(8,128)S(1)} %get-tuple-element.38), channel_id=1, source_target_pairs={{0,1},{1,0},{2,3},{3,2},{4,5},{5,4},{6,7},{7,6},{8,9},{9,8},{10,11... | collective-permute-start | bytes 12296 | tf_op jit(solution)/shard_map/ppermute | solution.py:295
  29.9 6.8 %copy-start.6 = (f32[4]{0:T(128)S(1)}, f32[4]{0:T(128)}, u32[]{:S(2)}) copy-start(f32[4]{0:T(128)} %weights_ref.1) | copy-start | bytes 52
  29.9 6.8 %collective-permute-start.9 = (f32[8,128]{1,0:T(8,128)S(1)}, f32[8,128]{1,0:T(8,128)S(1)}, u32[]{:S(2)}, u32[]{:S(2)}) collective-permute-start(f32[8,128]{1,0:T(8,128)S(1)} %get-tuple-element.39), channel_id=1, source_target_pairs={{1,2},{3,4},{5,6},{7,0},{2,1},{4,3},{6,5},{0,7},{9,10},{11,12},{13... | collective-permute-start | bytes 12296 | tf_op jit(solution)/shard_map/ppermute | solution.py:342
  36.7 4.4 %copy-start.8 = (f32[2,2048]{1,0:T(2,128)S(1)}, f32[2,2048]{1,0:T(2,128)}, u32[]{:S(2)}) copy-start(f32[2,2048]{1,0:T(2,128)} %param.14) | copy-start | bytes 49156
  37.5 4.4 %collective-permute-start.10 = (f32[96,128]{1,0:T(8,128)S(1)}, f32[96,128]{1,0:T(8,128)S(1)}, u32[]{:S(2)}, u32[]{:S(2)}) collective-permute-start(f32[96,128]{1,0:T(8,128)S(1)} %shard_map.98.refs_0_), channel_id=1, source_target_pairs={{0,8},{8,0},{16,24},{24,16},{1,9},{9,1},{17,25},{25,17},{2,10},{10... | collective-permute-start | bytes 147464 | tf_op jit(solution)/shard_map/ppermute | solution.py:351
  39.1 4.5 %collective-permute-start.11 = (f32[96,128]{1,0:T(8,128)S(1)}, f32[96,128]{1,0:T(8,128)S(1)}, u32[]{:S(2)}, u32[]{:S(2)}) collective-permute-start(f32[96,128]{1,0:T(8,128)S(1)} %shard_map.98.refs_0_), channel_id=1, source_target_pairs={{0,16},{8,24},{16,0},{24,8},{1,17},{9,25},{17,1},{25,9},{2,18},{10... | collective-permute-start | bytes 147464 | tf_op jit(solution)/shard_map/ppermute | solution.py:351
  40.6 5.0 %collective-permute-start.12 = (f32[96,128]{1,0:T(8,128)S(1)}, f32[96,128]{1,0:T(8,128)S(1)}, u32[]{:S(2)}, u32[]{:S(2)}) collective-permute-start(f32[96,128]{1,0:T(8,128)S(1)} %shard_map.98.refs_0_), channel_id=1, source_target_pairs={{0,24},{8,16},{16,8},{24,0},{1,25},{9,17},{17,9},{25,1},{2,26},{10... | collective-permute-start | bytes 147464 | tf_op jit(solution)/shard_map/ppermute | solution.py:351

commit v5 on v4

--- a/solution.py
+++ b/solution.py
@@ -332,7 +332,7 @@
     potential, mass, edges = solve(theirs)
     crossed = swap(pick(range(planes), potential, mass, their_cells, BF16, edges), half)
     potential, mass, edges = solve(ours)
-    cut = planes - planes // 2
+    cut = planes - planes // 4
     early = pick(range(cut), potential, mass, cells, F32)
     crossed, early = lax.optimization_barrier((crossed, early))
     line = jax.ShapeDtypeStruct((planes * side // LANES, LANES), F32)

time: 46.4 us -> 46 us (level)
  starting transfers between devices: 18.5 us -> 17 us
  waiting for transfers between devices: 6.66 us -> 7.76 us
    ppermute x1, starting transfers between devices: 3.44 us -> 1.88 us  [body(): second = lax.ppermute(second, 'tile', pairs + [(j, i) for i, j in pairs])]
    ppermute x1, waiting for transfers between devices: 0.01 us -> 1.19 us  [body(): second = lax.ppermute(second, 'tile', pairs + [(j, i) for i, j in pairs])]
  transfers between devices with their start and end apart: 13 -> 13, of which waited for: 5 -> 5; matrix products, arithmetic and copies ran while one was open for 0% -> 0% of each run, Pallas kernels for 36% -> 37%
where the time goes in v5:
time: 46 us; the launch traced here: 45.9 us
  Pallas kernels  19.1 us (42%)
  starting transfers between devices  17 us (37%)
  waiting for transfers between devices  7.76 us (17%)
  local copies, waits for them, and re-layouts  1.95 us (4%)
    pallas_call x3, Pallas kernels, pick(): call(functools.partial(pick_kernel, planes, used), [jax.ShapeDtypeStruct(...  13.2 us
    ppermute x9, starting transfers between devices, swap(): lax.ppermute(array, 'tile', [(i, i ^ bits) for i in range(tile_count)])  11.5 us
    ppermute x3, waiting for transfers between devices, body(): lax.ppermute(local_map, 'depth', [(i, i ^ d) for i in range(count)])  4.49 us
    pallas_call x2, Pallas kernels, solve(): call(functools.partial(solve_kernel, capacity, planes), [jax.ShapeDtypeSt...  3.57 us
    ppermute x3, starting transfers between devices, body(): lax.ppermute(local_map, 'depth', [(i, i ^ d) for i in range(count)])  3.55 us
    ppermute x9, waiting for transfers between devices, swap(): lax.ppermute(array, 'tile', [(i, i ^ bits) for i in range(tile_count)])  2.08 us
    unnamed x18, local copies, waits for them, and re-layouts  1.92 us
    ppermute x1, starting transfers between devices, body(): second = lax.ppermute(second, 'tile', pairs + [(j, i) for i, j in pairs])  1.88 us
  transfers between devices with their start and end apart: 13, of which 5 were waited for; matrix products, arithmetic and copies ran while one was open for 0% of the time, Pallas kernels for 37%

profile of v5, /device:TPU:0, one launch (start us, length us, event | category | flops | bytes accessed | tf_op | source)
XLA Modules:
  0.0 45.9 jit_solution(5678381183245111603)
XLA Ops:
  0.0 0.7 %copy-done.4 = s32[32]{0:T(128)S(1)} copy-done((s32[32]{0:T(128)S(1)}, s32[32]{0:T(128)}, u32[]{:S(2)}) %copy-start.4) | copy-done | bytes 152
  0.7 1.2 %copy-done = bf16[32,128,128]{2,1,0:T(8,128)(2,1)S(1)} copy-done((bf16[32,128,128]{2,1,0:T(8,128)(2,1)S(1)}, bf16[32,128,128]{2,1,0:T(8,128)(2,1)}, u32[]{:S(2)}) %copy-start) | copy-done | bytes 1048600
  1.9 0.8 %shard_map.91 = (bf16[528,128]{1,0:T(8,128)(2,1)S(1)}, bf16[528,128]{1,0:T(8,128)(2,1)S(1)}, bf16[528,128]{1,0:T(8,128)(2,1)S(1)}, bf16[528,128]{1,0:T(8,128)(2,...) custom-call(s32[1]{0:T(128)} %bitcast.1.tile_ref, ...), custom_call_target="tpu_custom_call" | custom-call | bytes 1048576 | tf_op jit(solution)/shard_map/pallas_call | solution.py:300
  2.7 3.1 %collective-permute-start.3 = (bf16[528,128]{1,0:T(8,128)(2,1)S(1)}, bf16[528,128]{1,0:T(8,128)(2,1)S(1)}, u32[]{:S(2)}, u32[]{:S(2)}) collective-permute-start(bf16[528,128]{1,0:T(8,128)(2,1)S(1)} %get-tuple-element.28), channel_id=1, source_target_pairs={{0,2},{1,3},{2,0},{3,1},{4,6},{5,7},{6,4},{7,5},{8,10},{9,11},{10,... | collective-permute-start | bytes 405512 | tf_op jit(solution)/shard_map/ppermute | solution.py:295
  6.0 3.0 %collective-permute-start.6 = (s32[64,128]{1,0:T(8,128)S(1)}, s32[64,128]{1,0:T(8,128)S(1)}, u32[]{:S(2)}, u32[]{:S(2)}) collective-permute-start(s32[64,128]{1,0:T(8,128)S(1)} %reshape.17.cells_ref), channel_id=1, source_target_pairs={{0,4},{1,5},{2,6},{3,7},{4,0},{5,1},{6,2},{7,3},{8,12},{9,13},{10,... | collective-permute-start | bytes 98312 | tf_op jit(solution)/shard_map/ppermute | solution.py:295
  9.0 1.6 %collective-permute-start = (bf16[528,128]{1,0:T(8,128)(2,1)S(1)}, bf16[528,128]{1,0:T(8,128)(2,1)S(1)}, u32[]{:S(2)}, u32[]{:S(2)}) collective-permute-start(bf16[528,128]{1,0:T(8,128)(2,1)S(1)} %get-tuple-element.23), channel_id=1, source_target_pairs={{0,2},{1,3},{2,0},{3,1},{4,6},{5,7},{6,4},{7,5},{8,10},{9,11},{10,... | collective-permute-start | bytes 405512 | tf_op jit(solution)/shard_map/ppermute | solution.py:295
  10.6 2.1 %collective-permute-done.4.refs_4_ = bf16[528,128]{1,0:T(8,128)(2,1)S(1)} collective-permute-done((bf16[528,128]{1,0:T(8,128)(2,1)S(1)}, bf16[528,128]{1,0:T(8,128)(2,1)S(1)}, u32[]{:S(2)}, u32[]{:S(2)}) %collective-permute-start.4) | collective-permute-done | bytes 135200 | tf_op jit(solution)/shard_map/ppermute | solution.py:295
  12.7 0.6 %collective-permute-start.2 = (bf16[528,128]{1,0:T(8,128)(2,1)S(1)}, bf16[528,128]{1,0:T(8,128)(2,1)S(1)}, u32[]{:S(2)}, u32[]{:S(2)}) collective-permute-start(bf16[528,128]{1,0:T(8,128)(2,1)S(1)} %get-tuple-element.25), channel_id=1, source_target_pairs={{0,1},{1,0},{2,3},{3,2},{4,5},{5,4},{6,7},{7,6},{8,9},{9,8},{10,11... | collective-permute-start | bytes 405512 | tf_op jit(solution)/shard_map/ppermute | solution.py:295
  13.4 1.8 %shard_map.93 = (f32[4,256,256]{2,1,0:T(8,128)S(1)}, bf16[5,256,256]{2,1,0:T(8,128)(2,1)S(1)}, f32[16,128]{1,0:T(8,128)S(1)}) custom-call(bf16[256,256]{1,0:T(8,128)(2,1)S(1)} %copy-done.2, bf16[256,256]{1,0:T(8,128)(2,1)S(1)} %copy-done.3, f32[256,256]{1,0:T(8,128)S(1)} %copy-done.1, bf16[528,128]{1,0:T(8,128)(2,1)S(1)} %collective-permute-done.3.refs_3_, ...), custom_call_target="tpu_custom_call" | custom-call | tf_op jit(solution)/shard_map/pallas_call | solution.py:312
  15.2 6.4 %shard_map.94 = bf16[368,128]{1,0:T(8,128)(2,1)S(1)} custom-call(f32[4,256,256]{2,1,0:T(8,128)S(1)} %get-tuple-element.32.p_ref, bf16[5,256,256]{2,1,0:T(8,128)(2,1)S(1)} %get-tuple-element.33.c_ref, s32[64,128]{1,0:T(8,128)S(1)} %collective-permute-done.6.cells_ref, f32[16,128]{1,0:T(8,128)S(1)} %get-tuple-element.34.refs_0_), custom_call_target="tpu_custom_call" | custom-call | flops 5368709120 | tf_op jit(solution)/shard_map/pallas_call | solution.py:324
  21.6 2.7 %collective-permute-start.7 = (bf16[368,128]{1,0:T(8,128)(2,1)S(1)}, bf16[368,128]{1,0:T(8,128)(2,1)S(1)}, u32[]{:S(2)}, u32[]{:S(2)}) collective-permute-start(bf16[368,128]{1,0:T(8,128)(2,1)S(1)} %shard_map.94), channel_id=1, source_target_pairs={{0,4},{1,5},{2,6},{3,7},{4,0},{5,1},{6,2},{7,3},{8,12},{9,13},{10,... | collective-permute-start | bytes 282632 | tf_op jit(solution)/shard_map/ppermute | solution.py:295
  24.3 1.8 %shard_map.92 = (f32[4,256,256]{2,1,0:T(8,128)S(1)}, bf16[5,256,256]{2,1,0:T(8,128)(2,1)S(1)}, f32[16,128]{1,0:T(8,128)S(1)}) custom-call(bf16[256,256]{1,0:T(8,128)(2,1)S(1)} %copy-done.2, bf16[256,256]{1,0:T(8,128)(2,1)S(1)} %copy-done.3, f32[256,256]{1,0:T(8,128)S(1)} %copy-done.1, bf16[528,128]{1,0:T(8,128)(2,1)S(1)} %collective-permute-done.refs_3_, ...), custom_call_target="tpu_custom_call" | custom-call | tf_op jit(solution)/shard_map/pallas_call | solution.py:312
  26.1 5.0 %shard_map.95.early_ref = f32[240,128]{1,0:T(8,128)S(1)} custom-call(f32[4,256,256]{2,1,0:T(8,128)S(1)} %get-tuple-element.35.p_ref, bf16[5,256,256]{2,1,0:T(8,128)(2,1)S(1)} %get-tuple-element.36.c_ref, s32[64,128]{1,0:T(8,128)S(1)} %reshape.17.cells_ref), custom_call_target="tpu_custom_call" | custom-call | flops 4026531840 | tf_op jit(solution)/shard_map/pallas_call | solution.py:324
  31.5 1.9 %collective-permute-start.9 = (f32[8,128]{1,0:T(8,128)S(1)}, f32[8,128]{1,0:T(8,128)S(1)}, u32[]{:S(2)}, u32[]{:S(2)}) collective-permute-start(f32[8,128]{1,0:T(8,128)S(1)} %get-tuple-element.39), channel_id=1, source_target_pairs={{1,2},{3,4},{5,6},{7,0},{2,1},{4,3},{6,5},{0,7},{9,10},{11,12},{13... | collective-permute-start | bytes 12296 | tf_op jit(solution)/shard_map/ppermute | solution.py:342
  33.4 1.7 %shard_map.97.late_ref = f32[80,128]{1,0:T(8,128)S(1)} custom-call(f32[4,256,256]{2,1,0:T(8,128)S(1)} %get-tuple-element.35.p_ref, bf16[5,256,256]{2,1,0:T(8,128)(2,1)S(1)} %get-tuple-element.36.c_ref, s32[64,128]{1,0:T(8,128)S(1)} %reshape.17.cells_ref), custom_call_target="tpu_custom_call" | custom-call | flops 1342177280 | tf_op jit(solution)/shard_map/pallas_call | solution.py:324
  35.1 1.2 %collective-permute-done.9.second_ref = f32[8,128]{1,0:T(8,128)S(1)} collective-permute-done((f32[8,128]{1,0:T(8,128)S(1)}, f32[8,128]{1,0:T(8,128)S(1)}, u32[]{:S(2)}, u32[]{:S(2)}) %collective-permute-start.9) | collective-permute-done | bytes 4128 | tf_op jit(solution)/shard_map/ppermute | solution.py:342
  36.3 0.8 %shard_map.98.refs_0_ = f32[96,128]{1,0:T(8,128)S(1)} custom-call(s32[1]{0:T(128)} %bitcast.1.tile_ref, f32[4]{0:T(128)S(1)} %copy-done.6, s32[64,128]{1,0:T(8,128)S(1)} %reshape.17.cells_ref, f32[8,128]{1,0:T(8,128)S(1)} %collective-permute-done.8.first_ref, f32[8,128]{1,0:T(8,128)S(1)} %collective-permute-done.9.second_ref, ...), custom_call_target="tpu_custom_call" | custom-call | tf_op jit(solution)/shard_map/pallas_call | solution.py:344
  37.2 1.6 %collective-permute-start.10 = (f32[96,128]{1,0:T(8,128)S(1)}, f32[96,128]{1,0:T(8,128)S(1)}, u32[]{:S(2)}, u32[]{:S(2)}) collective-permute-start(f32[96,128]{1,0:T(8,128)S(1)} %shard_map.98.refs_0_), channel_id=1, source_target_pairs={{0,8},{8,0},{16,24},{24,16},{1,9},{9,1},{17,25},{25,17},{2,10},{10... | collective-permute-start | bytes 147464 | tf_op jit(solution)/shard_map/ppermute | solution.py:351
  38.7 1.5 %collective-permute-start.11 = (f32[96,128]{1,0:T(8,128)S(1)}, f32[96,128]{1,0:T(8,128)S(1)}, u32[]{:S(2)}, u32[]{:S(2)}) collective-permute-start(f32[96,128]{1,0:T(8,128)S(1)} %shard_map.98.refs_0_), channel_id=1, source_target_pairs={{0,16},{8,24},{16,0},{24,8},{1,17},{9,25},{17,1},{25,9},{2,18},{10... | collective-permute-start | bytes 147464 | tf_op jit(solution)/shard_map/ppermute | solution.py:351
  40.2 0.5 %collective-permute-start.12 = (f32[96,128]{1,0:T(8,128)S(1)}, f32[96,128]{1,0:T(8,128)S(1)}, u32[]{:S(2)}, u32[]{:S(2)}) collective-permute-start(f32[96,128]{1,0:T(8,128)S(1)} %shard_map.98.refs_0_), channel_id=1, source_target_pairs={{0,24},{8,16},{16,8},{24,0},{1,25},{9,17},{17,9},{25,1},{2,26},{10... | collective-permute-start | bytes 147464 | tf_op jit(solution)/shard_map/ppermute | solution.py:351
  40.7 0.6 %collective-permute-done.10.refs_1_ = f32[96,128]{1,0:T(8,128)S(1)} collective-permute-done((f32[96,128]{1,0:T(8,128)S(1)}, f32[96,128]{1,0:T(8,128)S(1)}, u32[]{:S(2)}, u32[]{:S(2)}) %collective-permute-start.10) | collective-permute-done | bytes 49184 | tf_op jit(solution)/shard_map/ppermute | solution.py:351
  41.3 2.0 %collective-permute-done.11.refs_2_ = f32[96,128]{1,0:T(8,128)S(1)} collective-permute-done((f32[96,128]{1,0:T(8,128)S(1)}, f32[96,128]{1,0:T(8,128)S(1)}, u32[]{:S(2)}, u32[]{:S(2)}) %collective-permute-start.11) | collective-permute-done | bytes 49184 | tf_op jit(solution)/shard_map/ppermute | solution.py:351
  43.3 1.9 %collective-permute-done.12.refs_3_ = f32[96,128]{1,0:T(8,128)S(1)} collective-permute-done((f32[96,128]{1,0:T(8,128)S(1)}, f32[96,128]{1,0:T(8,128)S(1)}, u32[]{:S(2)}, u32[]{:S(2)}) %collective-permute-start.12) | collective-permute-done | bytes 49184 | tf_op jit(solution)/shard_map/ppermute | solution.py:351
  45.2 0.7 %shard_map.99 = f32[96,128]{1,0:T(8,128)} custom-call(s32[1]{0:T(128)} %bitcast.depth_ref, f32[96,128]{1,0:T(8,128)S(1)} %shard_map.98.refs_0_, f32[96,128]{1,0:T(8,128)S(1)} %collective-permute-done.10.refs_1_, f32[96,128]{1,0:T(8,128)S(1)} %collective-permute-done.11.refs_2_, f32[96,128]{1,0:T(8,128)S(1)} %collective-permute-done.12.refs_3_, ...), custom_call_target="tpu_custom_call" | custom-call | tf_op jit(solution)/shard_map/pallas_call | solution.py:352
  (31 shorter events, 0.6 us)
Async XLA Ops:
  0.0 0.7 %copy-start.4 = (s32[32]{0:T(128)S(1)}, s32[32]{0:T(128)}, u32[]{:S(2)}) copy-start(s32[32]{0:T(128)} %owner_ref.1) | copy-start | bytes 388
  0.0 0.7 %copy-start.5 = (s32[32]{0:T(128)S(1)}, s32[32]{0:T(128)}, u32[]{:S(2)}) copy-start(s32[32]{0:T(128)} %place_ref.1) | copy-start | bytes 388
  0.7 1.2 %copy-start = (bf16[32,128,128]{2,1,0:T(8,128)(2,1)S(1)}, bf16[32,128,128]{2,1,0:T(8,128)(2,1)}, u32[]{:S(2)}) copy-start(bf16[32,128,128]{2,1,0:T(8,128)(2,1)} %blocks_ref.1) | copy-start | bytes 3145732
  1.9 4.1 %copy-start.7 = (s32[4,2048]{1,0:T(4,128)S(1)}, s32[4,2048]{1,0:T(4,128)}, u32[]{:S(2)}) copy-start(s32[4,2048]{1,0:T(4,128)} %param.13) | copy-start | bytes 98308
  1.9 11.4 %copy-start.1 = (f32[256,256]{1,0:T(8,128)S(1)}, f32[256,256]{1,0:T(8,128)}, u32[]{:S(2)}) copy-start(f32[256,256]{1,0:T(8,128)} %constant.16.clone.refs_2_) | copy-start | bytes 786436
  1.9 11.4 %copy-start.2 = (bf16[256,256]{1,0:T(8,128)(2,1)S(1)}, bf16[256,256]{1,0:T(8,128)(2,1)}, u32[]{:S(2)}) copy-start(bf16[256,256]{1,0:T(8,128)(2,1)} %constant.14.clone.refs_0_) | copy-start | bytes 393220
  1.9 11.4 %copy-start.3 = (bf16[256,256]{1,0:T(8,128)(2,1)S(1)}, bf16[256,256]{1,0:T(8,128)(2,1)}, u32[]{:S(2)}) copy-start(bf16[256,256]{1,0:T(8,128)(2,1)} %constant.15.clone.refs_1_) | copy-start | bytes 393220
  2.7 7.9 %collective-permute-start.3 = (bf16[528,128]{1,0:T(8,128)(2,1)S(1)}, bf16[528,128]{1,0:T(8,128)(2,1)S(1)}, u32[]{:S(2)}, u32[]{:S(2)}) collective-permute-start(bf16[528,128]{1,0:T(8,128)(2,1)S(1)} %get-tuple-element.28), channel_id=1, source_target_pairs={{0,2},{1,3},{2,0},{3,1},{4,6},{5,7},{6,4},{7,5},{8,10},{9,11},{10,... | collective-permute-start | bytes 405512 | tf_op jit(solution)/shard_map/ppermute | solution.py:295
  5.8 6.9 %collective-permute-start.4 = (bf16[528,128]{1,0:T(8,128)(2,1)S(1)}, bf16[528,128]{1,0:T(8,128)(2,1)S(1)}, u32[]{:S(2)}, u32[]{:S(2)}) collective-permute-start(bf16[528,128]{1,0:T(8,128)(2,1)S(1)} %get-tuple-element.29), channel_id=1, source_target_pairs={{0,3},{1,2},{2,1},{3,0},{4,7},{5,6},{6,5},{7,4},{8,11},{9,10},{10,... | collective-permute-start | bytes 405512 | tf_op jit(solution)/shard_map/ppermute | solution.py:295
  5.8 7.5 %collective-permute-start.5 = (bf16[528,128]{1,0:T(8,128)(2,1)S(1)}, bf16[528,128]{1,0:T(8,128)(2,1)S(1)}, u32[]{:S(2)}, u32[]{:S(2)}) collective-permute-start(bf16[528,128]{1,0:T(8,128)(2,1)S(1)} %get-tuple-element.30), channel_id=1, source_target_pairs={{0,1},{1,0},{2,3},{3,2},{4,5},{5,4},{6,7},{7,6},{8,9},{9,8},{10,11... | collective-permute-start | bytes 405512 | tf_op jit(solution)/shard_map/ppermute | solution.py:295
  6.0 9.1 %collective-permute-start.6 = (s32[64,128]{1,0:T(8,128)S(1)}, s32[64,128]{1,0:T(8,128)S(1)}, u32[]{:S(2)}, u32[]{:S(2)}) collective-permute-start(s32[64,128]{1,0:T(8,128)S(1)} %reshape.17.cells_ref), channel_id=1, source_target_pairs={{0,4},{1,5},{2,6},{3,7},{4,0},{5,1},{6,2},{7,3},{8,12},{9,13},{10,... | collective-permute-start | bytes 98312 | tf_op jit(solution)/shard_map/ppermute | solution.py:295
  9.0 15.3 %collective-permute-start = (bf16[528,128]{1,0:T(8,128)(2,1)S(1)}, bf16[528,128]{1,0:T(8,128)(2,1)S(1)}, u32[]{:S(2)}, u32[]{:S(2)}) collective-permute-start(bf16[528,128]{1,0:T(8,128)(2,1)S(1)} %get-tuple-element.23), channel_id=1, source_target_pairs={{0,2},{1,3},{2,0},{3,1},{4,6},{5,7},{6,4},{7,5},{8,10},{9,11},{10,... | collective-permute-start | bytes 405512 | tf_op jit(solution)/shard_map/ppermute | solution.py:295
  10.6 13.7 %collective-permute-start.1 = (bf16[528,128]{1,0:T(8,128)(2,1)S(1)}, bf16[528,128]{1,0:T(8,128)(2,1)S(1)}, u32[]{:S(2)}, u32[]{:S(2)}) collective-permute-start(bf16[528,128]{1,0:T(8,128)(2,1)S(1)} %get-tuple-element.24), channel_id=1, source_target_pairs={{0,3},{1,2},{2,1},{3,0},{4,7},{5,6},{6,5},{7,4},{8,11},{9,10},{10,... | collective-permute-start | bytes 405512 | tf_op jit(solution)/shard_map/ppermute | solution.py:295
  12.7 11.6 %collective-permute-start.2 = (bf16[528,128]{1,0:T(8,128)(2,1)S(1)}, bf16[528,128]{1,0:T(8,128)(2,1)S(1)}, u32[]{:S(2)}, u32[]{:S(2)}) collective-permute-start(bf16[528,128]{1,0:T(8,128)(2,1)S(1)} %get-tuple-element.25), channel_id=1, source_target_pairs={{0,1},{1,0},{2,3},{3,2},{4,5},{5,4},{6,7},{7,6},{8,9},{9,8},{10,11... | collective-permute-start | bytes 405512 | tf_op jit(solution)/shard_map/ppermute | solution.py:295
  21.6 9.6 %collective-permute-start.7 = (bf16[368,128]{1,0:T(8,128)(2,1)S(1)}, bf16[368,128]{1,0:T(8,128)(2,1)S(1)}, u32[]{:S(2)}, u32[]{:S(2)}) collective-permute-start(bf16[368,128]{1,0:T(8,128)(2,1)S(1)} %shard_map.94), channel_id=1, source_target_pairs={{0,4},{1,5},{2,6},{3,7},{4,0},{5,1},{6,2},{7,3},{8,12},{9,13},{10,... | collective-permute-start | bytes 282632 | tf_op jit(solution)/shard_map/ppermute | solution.py:295
  31.2 3.9 %collective-permute-start.8 = (f32[8,128]{1,0:T(8,128)S(1)}, f32[8,128]{1,0:T(8,128)S(1)}, u32[]{:S(2)}, u32[]{:S(2)}) collective-permute-start(f32[8,128]{1,0:T(8,128)S(1)} %get-tuple-element.38), channel_id=1, source_target_pairs={{0,1},{1,0},{2,3},{3,2},{4,5},{5,4},{6,7},{7,6},{8,9},{9,8},{10,11... | collective-permute-start | bytes 12296 | tf_op jit(solution)/shard_map/ppermute | solution.py:295
  31.5 4.8 %copy-start.6 = (f32[4]{0:T(128)S(1)}, f32[4]{0:T(128)}, u32[]{:S(2)}) copy-start(f32[4]{0:T(128)} %weights_ref.1) | copy-start | bytes 52
  31.5 4.8 %collective-permute-start.9 = (f32[8,128]{1,0:T(8,128)S(1)}, f32[8,128]{1,0:T(8,128)S(1)}, u32[]{:S(2)}, u32[]{:S(2)}) collective-permute-start(f32[8,128]{1,0:T(8,128)S(1)} %get-tuple-element.39), channel_id=1, source_target_pairs={{1,2},{3,4},{5,6},{7,0},{2,1},{4,3},{6,5},{0,7},{9,10},{11,12},{13... | collective-permute-start | bytes 12296 | tf_op jit(solution)/shard_map/ppermute | solution.py:342
  36.3 4.4 %copy-start.8 = (f32[2,2048]{1,0:T(2,128)S(1)}, f32[2,2048]{1,0:T(2,128)}, u32[]{:S(2)}) copy-start(f32[2,2048]{1,0:T(2,128)} %param.14) | copy-start | bytes 49156
  37.2 4.2 %collective-permute-start.10 = (f32[96,128]{1,0:T(8,128)S(1)}, f32[96,128]{1,0:T(8,128)S(1)}, u32[]{:S(2)}, u32[]{:S(2)}) collective-permute-start(f32[96,128]{1,0:T(8,128)S(1)} %shard_map.98.refs_0_), channel_id=1, source_target_pairs={{0,8},{8,0},{16,24},{24,16},{1,9},{9,1},{17,25},{25,17},{2,10},{10... | collective-permute-start | bytes 147464 | tf_op jit(solution)/shard_map/ppermute | solution.py:351
  38.7 4.6 %collective-permute-start.11 = (f32[96,128]{1,0:T(8,128)S(1)}, f32[96,128]{1,0:T(8,128)S(1)}, u32[]{:S(2)}, u32[]{:S(2)}) collective-permute-start(f32[96,128]{1,0:T(8,128)S(1)} %shard_map.98.refs_0_), channel_id=1, source_target_pairs={{0,16},{8,24},{16,0},{24,8},{1,17},{9,25},{17,1},{25,9},{2,18},{10... | collective-permute-start | bytes 147464 | tf_op jit(solution)/shard_map/ppermute | solution.py:351
  40.2 5.0 %collective-permute-start.12 = (f32[96,128]{1,0:T(8,128)S(1)}, f32[96,128]{1,0:T(8,128)S(1)}, u32[]{:S(2)}, u32[]{:S(2)}) collective-permute-start(f32[96,128]{1,0:T(8,128)S(1)} %shard_map.98.refs_0_), channel_id=1, source_target_pairs={{0,24},{8,16},{16,8},{24,0},{1,25},{9,17},{17,9},{25,1},{2,26},{10... | collective-permute-start | bytes 147464 | tf_op jit(solution)/shard_map/ppermute | solution.py:351

commit v6 on v5

--- a/solution.py
+++ b/solution.py
@@ -166,14 +166,16 @@
             (0.5 * ((below + above) - (right + left))).astype(BF16),
             (0.5 * (shifted(tilt, 0, 1) - shifted(tilt, 0, -1))).astype(BF16),
         )
+        stacked = jnp.concatenate(fields, axis=0)
         for g in range(0, groups, width):
             cells = jnp.concatenate([cells_ref[pl.ds(k * groups + g + w, 1), :] for w in range(width)], axis=1)
             row, col = cells >> shift, cells & (side - 1)
             chosen = (column == col).astype(F32).astype(BF16)
             block, within = row >> 3, sub == (row & 7)
             bits = [(block >> i) & 1 == 1 for i in range((side // 8).bit_length() - 1)]
+            every = mul(stacked, chosen)
             for f in range(5):
-                picked = mul(fields[f], chosen)
+                picked = every[f * side : (f + 1) * side]
                 kept = [picked[v * 8 : v * 8 + 8] for v in range(side // 8)]
                 for bit in bits:
                     kept = [jnp.where(bit, b, a) for a, b in zip(kept[::2], kept[1::2])]

time: 46 us -> 45.9 us (level)
  transfers between devices with their start and end apart: 13 -> 13, of which waited for: 5 -> 5; matrix products, arithmetic and copies ran while one was open for 0% -> 0% of each run, Pallas kernels for 37% -> 36%
where the time goes in v6:
time: 45.9 us; the launch traced here: 45.7 us
  Pallas kernels  18.9 us (41%)
  starting transfers between devices  17 us (37%)
  waiting for transfers between devices  7.75 us (17%)
  local copies, waits for them, and re-layouts  1.95 us (4%)
    pallas_call x3, Pallas kernels, pick(): call(functools.partial(pick_kernel, planes, used), [jax.ShapeDtypeStruct(...  13 us
    ppermute x9, starting transfers between devices, swap(): lax.ppermute(array, 'tile', [(i, i ^ bits) for i in range(tile_count)])  11.5 us
    ppermute x3, waiting for transfers between devices, body(): lax.ppermute(local_map, 'depth', [(i, i ^ d) for i in range(count)])  4.5 us
    pallas_call x2, Pallas kernels, solve(): call(functools.partial(solve_kernel, capacity, planes), [jax.ShapeDtypeSt...  3.57 us
    ppermute x3, starting transfers between devices, body(): lax.ppermute(local_map, 'depth', [(i, i ^ d) for i in range(count)])  3.55 us
    ppermute x9, waiting for transfers between devices, swap(): lax.ppermute(array, 'tile', [(i, i ^ bits) for i in range(tile_count)])  2.08 us
    ppermute x1, starting transfers between devices, body(): second = lax.ppermute(second, 'tile', pairs + [(j, i) for i, j in pairs])  1.93 us
    unnamed x18, local copies, waits for them, and re-layouts  1.92 us
  transfers between devices with their start and end apart: 13, of which 5 were waited for; matrix products, arithmetic and copies ran while one was open for 0% of the time, Pallas kernels for 36%

profile of v6, /device:TPU:0, one launch (start us, length us, event | category | flops | bytes accessed | tf_op | source)
XLA Modules:
  0.0 45.7 jit_solution(12693877102956471230)
XLA Ops:
  0.0 0.7 %copy-done.4 = s32[32]{0:T(128)S(1)} copy-done((s32[32]{0:T(128)S(1)}, s32[32]{0:T(128)}, u32[]{:S(2)}) %copy-start.4) | copy-done | bytes 152
  0.7 1.2 %copy-done = bf16[32,128,128]{2,1,0:T(8,128)(2,1)S(1)} copy-done((bf16[32,128,128]{2,1,0:T(8,128)(2,1)S(1)}, bf16[32,128,128]{2,1,0:T(8,128)(2,1)}, u32[]{:S(2)}) %copy-start) | copy-done | bytes 1048600
  1.9 0.8 %shard_map.91 = (bf16[528,128]{1,0:T(8,128)(2,1)S(1)}, bf16[528,128]{1,0:T(8,128)(2,1)S(1)}, bf16[528,128]{1,0:T(8,128)(2,1)S(1)}, bf16[528,128]{1,0:T(8,128)(2,...) custom-call(s32[1]{0:T(128)} %bitcast.1.tile_ref, ...), custom_call_target="tpu_custom_call" | custom-call | bytes 1048576 | tf_op jit(solution)/shard_map/pallas_call | solution.py:302
  2.7 3.1 %collective-permute-start.3 = (bf16[528,128]{1,0:T(8,128)(2,1)S(1)}, bf16[528,128]{1,0:T(8,128)(2,1)S(1)}, u32[]{:S(2)}, u32[]{:S(2)}) collective-permute-start(bf16[528,128]{1,0:T(8,128)(2,1)S(1)} %get-tuple-element.28), channel_id=1, source_target_pairs={{0,2},{1,3},{2,0},{3,1},{4,6},{5,7},{6,4},{7,5},{8,10},{9,11},{10,... | collective-permute-start | bytes 405512 | tf_op jit(solution)/shard_map/ppermute | solution.py:297
  6.0 3.0 %collective-permute-start.6 = (s32[64,128]{1,0:T(8,128)S(1)}, s32[64,128]{1,0:T(8,128)S(1)}, u32[]{:S(2)}, u32[]{:S(2)}) collective-permute-start(s32[64,128]{1,0:T(8,128)S(1)} %reshape.17.cells_ref), channel_id=1, source_target_pairs={{0,4},{1,5},{2,6},{3,7},{4,0},{5,1},{6,2},{7,3},{8,12},{9,13},{10,... | collective-permute-start | bytes 98312 | tf_op jit(solution)/shard_map/ppermute | solution.py:297
  9.0 1.6 %collective-permute-start = (bf16[528,128]{1,0:T(8,128)(2,1)S(1)}, bf16[528,128]{1,0:T(8,128)(2,1)S(1)}, u32[]{:S(2)}, u32[]{:S(2)}) collective-permute-start(bf16[528,128]{1,0:T(8,128)(2,1)S(1)} %get-tuple-element.23), channel_id=1, source_target_pairs={{0,2},{1,3},{2,0},{3,1},{4,6},{5,7},{6,4},{7,5},{8,10},{9,11},{10,... | collective-permute-start | bytes 405512 | tf_op jit(solution)/shard_map/ppermute | solution.py:297
  10.6 2.1 %collective-permute-done.4.refs_4_ = bf16[528,128]{1,0:T(8,128)(2,1)S(1)} collective-permute-done((bf16[528,128]{1,0:T(8,128)(2,1)S(1)}, bf16[528,128]{1,0:T(8,128)(2,1)S(1)}, u32[]{:S(2)}, u32[]{:S(2)}) %collective-permute-start.4) | collective-permute-done | bytes 135200 | tf_op jit(solution)/shard_map/ppermute | solution.py:297
  12.7 0.6 %collective-permute-start.2 = (bf16[528,128]{1,0:T(8,128)(2,1)S(1)}, bf16[528,128]{1,0:T(8,128)(2,1)S(1)}, u32[]{:S(2)}, u32[]{:S(2)}) collective-permute-start(bf16[528,128]{1,0:T(8,128)(2,1)S(1)} %get-tuple-element.25), channel_id=1, source_target_pairs={{0,1},{1,0},{2,3},{3,2},{4,5},{5,4},{6,7},{7,6},{8,9},{9,8},{10,11... | collective-permute-start | bytes 405512 | tf_op jit(solution)/shard_map/ppermute | solution.py:297
  13.4 1.8 %shard_map.93 = (f32[4,256,256]{2,1,0:T(8,128)S(1)}, bf16[5,256,256]{2,1,0:T(8,128)(2,1)S(1)}, f32[16,128]{1,0:T(8,128)S(1)}) custom-call(bf16[256,256]{1,0:T(8,128)(2,1)S(1)} %copy-done.2, bf16[256,256]{1,0:T(8,128)(2,1)S(1)} %copy-done.3, f32[256,256]{1,0:T(8,128)S(1)} %copy-done.1, bf16[528,128]{1,0:T(8,128)(2,1)S(1)} %collective-permute-done.3.refs_3_, ...), custom_call_target="tpu_custom_call" | custom-call | tf_op jit(solution)/shard_map/pallas_call | solution.py:314
  15.2 6.3 %shard_map.94 = bf16[368,128]{1,0:T(8,128)(2,1)S(1)} custom-call(f32[4,256,256]{2,1,0:T(8,128)S(1)} %get-tuple-element.32.p_ref, bf16[5,256,256]{2,1,0:T(8,128)(2,1)S(1)} %get-tuple-element.33.c_ref, s32[64,128]{1,0:T(8,128)S(1)} %collective-permute-done.6.cells_ref, f32[16,128]{1,0:T(8,128)S(1)} %get-tuple-element.34.refs_0_), custom_call_target="tpu_custom_call" | custom-call | flops 5368709120 | tf_op jit(solution)/shard_map/pallas_call | solution.py:326
  21.5 2.7 %collective-permute-start.7 = (bf16[368,128]{1,0:T(8,128)(2,1)S(1)}, bf16[368,128]{1,0:T(8,128)(2,1)S(1)}, u32[]{:S(2)}, u32[]{:S(2)}) collective-permute-start(bf16[368,128]{1,0:T(8,128)(2,1)S(1)} %shard_map.94), channel_id=1, source_target_pairs={{0,4},{1,5},{2,6},{3,7},{4,0},{5,1},{6,2},{7,3},{8,12},{9,13},{10,... | collective-permute-start | bytes 282632 | tf_op jit(solution)/shard_map/ppermute | solution.py:297
  24.2 1.8 %shard_map.92 = (f32[4,256,256]{2,1,0:T(8,128)S(1)}, bf16[5,256,256]{2,1,0:T(8,128)(2,1)S(1)}, f32[16,128]{1,0:T(8,128)S(1)}) custom-call(bf16[256,256]{1,0:T(8,128)(2,1)S(1)} %copy-done.2, bf16[256,256]{1,0:T(8,128)(2,1)S(1)} %copy-done.3, f32[256,256]{1,0:T(8,128)S(1)} %copy-done.1, bf16[528,128]{1,0:T(8,128)(2,1)S(1)} %collective-permute-done.refs_3_, ...), custom_call_target="tpu_custom_call" | custom-call | tf_op jit(solution)/shard_map/pallas_call | solution.py:314
  26.0 5.0 %shard_map.95.early_ref = f32[240,128]{1,0:T(8,128)S(1)} custom-call(f32[4,256,256]{2,1,0:T(8,128)S(1)} %get-tuple-element.35.p_ref, bf16[5,256,256]{2,1,0:T(8,128)(2,1)S(1)} %get-tuple-element.36.c_ref, s32[64,128]{1,0:T(8,128)S(1)} %reshape.17.cells_ref), custom_call_target="tpu_custom_call" | custom-call | flops 4026531840 | tf_op jit(solution)/shard_map/pallas_call | solution.py:326
  31.3 1.9 %collective-permute-start.9 = (f32[8,128]{1,0:T(8,128)S(1)}, f32[8,128]{1,0:T(8,128)S(1)}, u32[]{:S(2)}, u32[]{:S(2)}) collective-permute-start(f32[8,128]{1,0:T(8,128)S(1)} %get-tuple-element.39), channel_id=1, source_target_pairs={{1,2},{3,4},{5,6},{7,0},{2,1},{4,3},{6,5},{0,7},{9,10},{11,12},{13... | collective-permute-start | bytes 12296 | tf_op jit(solution)/shard_map/ppermute | solution.py:344
  33.3 1.7 %shard_map.97.late_ref = f32[80,128]{1,0:T(8,128)S(1)} custom-call(f32[4,256,256]{2,1,0:T(8,128)S(1)} %get-tuple-element.35.p_ref, bf16[5,256,256]{2,1,0:T(8,128)(2,1)S(1)} %get-tuple-element.36.c_ref, s32[64,128]{1,0:T(8,128)S(1)} %reshape.17.cells_ref), custom_call_target="tpu_custom_call" | custom-call | flops 1342177280 | tf_op jit(solution)/shard_map/pallas_call | solution.py:326
  35.0 1.2 %collective-permute-done.9.second_ref = f32[8,128]{1,0:T(8,128)S(1)} collective-permute-done((f32[8,128]{1,0:T(8,128)S(1)}, f32[8,128]{1,0:T(8,128)S(1)}, u32[]{:S(2)}, u32[]{:S(2)}) %collective-permute-start.9) | collective-permute-done | bytes 4128 | tf_op jit(solution)/shard_map/ppermute | solution.py:344
  36.2 0.8 %shard_map.98.refs_0_ = f32[96,128]{1,0:T(8,128)S(1)} custom-call(s32[1]{0:T(128)} %bitcast.1.tile_ref, f32[4]{0:T(128)S(1)} %copy-done.6, s32[64,128]{1,0:T(8,128)S(1)} %reshape.17.cells_ref, f32[8,128]{1,0:T(8,128)S(1)} %collective-permute-done.8.first_ref, f32[8,128]{1,0:T(8,128)S(1)} %collective-permute-done.9.second_ref, ...), custom_call_target="tpu_custom_call" | custom-call | tf_op jit(solution)/shard_map/pallas_call | solution.py:346
  37.0 1.6 %collective-permute-start.10 = (f32[96,128]{1,0:T(8,128)S(1)}, f32[96,128]{1,0:T(8,128)S(1)}, u32[]{:S(2)}, u32[]{:S(2)}) collective-permute-start(f32[96,128]{1,0:T(8,128)S(1)} %shard_map.98.refs_0_), channel_id=1, source_target_pairs={{0,8},{8,0},{16,24},{24,16},{1,9},{9,1},{17,25},{25,17},{2,10},{10... | collective-permute-start | bytes 147464 | tf_op jit(solution)/shard_map/ppermute | solution.py:353
  38.6 1.5 %collective-permute-start.11 = (f32[96,128]{1,0:T(8,128)S(1)}, f32[96,128]{1,0:T(8,128)S(1)}, u32[]{:S(2)}, u32[]{:S(2)}) collective-permute-start(f32[96,128]{1,0:T(8,128)S(1)} %shard_map.98.refs_0_), channel_id=1, source_target_pairs={{0,16},{8,24},{16,0},{24,8},{1,17},{9,25},{17,1},{25,9},{2,18},{10... | collective-permute-start | bytes 147464 | tf_op jit(solution)/shard_map/ppermute | solution.py:353
  40.1 0.5 %collective-permute-start.12 = (f32[96,128]{1,0:T(8,128)S(1)}, f32[96,128]{1,0:T(8,128)S(1)}, u32[]{:S(2)}, u32[]{:S(2)}) collective-permute-start(f32[96,128]{1,0:T(8,128)S(1)} %shard_map.98.refs_0_), channel_id=1, source_target_pairs={{0,24},{8,16},{16,8},{24,0},{1,25},{9,17},{17,9},{25,1},{2,26},{10... | collective-permute-start | bytes 147464 | tf_op jit(solution)/shard_map/ppermute | solution.py:353
  40.6 0.6 %collective-permute-done.10.refs_1_ = f32[96,128]{1,0:T(8,128)S(1)} collective-permute-done((f32[96,128]{1,0:T(8,128)S(1)}, f32[96,128]{1,0:T(8,128)S(1)}, u32[]{:S(2)}, u32[]{:S(2)}) %collective-permute-start.10) | collective-permute-done | bytes 49184 | tf_op jit(solution)/shard_map/ppermute | solution.py:353
  41.1 2.0 %collective-permute-done.11.refs_2_ = f32[96,128]{1,0:T(8,128)S(1)} collective-permute-done((f32[96,128]{1,0:T(8,128)S(1)}, f32[96,128]{1,0:T(8,128)S(1)}, u32[]{:S(2)}, u32[]{:S(2)}) %collective-permute-start.11) | collective-permute-done | bytes 49184 | tf_op jit(solution)/shard_map/ppermute | solution.py:353
  43.2 1.9 %collective-permute-done.12.refs_3_ = f32[96,128]{1,0:T(8,128)S(1)} collective-permute-done((f32[96,128]{1,0:T(8,128)S(1)}, f32[96,128]{1,0:T(8,128)S(1)}, u32[]{:S(2)}, u32[]{:S(2)}) %collective-permute-start.12) | collective-permute-done | bytes 49184 | tf_op jit(solution)/shard_map/ppermute | solution.py:353
  45.1 0.7 %shard_map.99 = f32[96,128]{1,0:T(8,128)} custom-call(s32[1]{0:T(128)} %bitcast.depth_ref, f32[96,128]{1,0:T(8,128)S(1)} %shard_map.98.refs_0_, f32[96,128]{1,0:T(8,128)S(1)} %collective-permute-done.10.refs_1_, f32[96,128]{1,0:T(8,128)S(1)} %collective-permute-done.11.refs_2_, f32[96,128]{1,0:T(8,128)S(1)} %collective-permute-done.12.refs_3_, ...), custom_call_target="tpu_custom_call" | custom-call | tf_op jit(solution)/shard_map/pallas_call | solution.py:354
  (31 shorter events, 0.6 us)
Async XLA Ops:
  0.0 0.7 %copy-start.4 = (s32[32]{0:T(128)S(1)}, s32[32]{0:T(128)}, u32[]{:S(2)}) copy-start(s32[32]{0:T(128)} %owner_ref.1) | copy-start | bytes 388
  0.0 0.7 %copy-start.5 = (s32[32]{0:T(128)S(1)}, s32[32]{0:T(128)}, u32[]{:S(2)}) copy-start(s32[32]{0:T(128)} %place_ref.1) | copy-start | bytes 388
  0.7 1.2 %copy-start = (bf16[32,128,128]{2,1,0:T(8,128)(2,1)S(1)}, bf16[32,128,128]{2,1,0:T(8,128)(2,1)}, u32[]{:S(2)}) copy-start(bf16[32,128,128]{2,1,0:T(8,128)(2,1)} %blocks_ref.1) | copy-start | bytes 3145732
  1.9 4.1 %copy-start.7 = (s32[4,2048]{1,0:T(4,128)S(1)}, s32[4,2048]{1,0:T(4,128)}, u32[]{:S(2)}) copy-start(s32[4,2048]{1,0:T(4,128)} %param.13) | copy-start | bytes 98308
  1.9 11.4 %copy-start.1 = (f32[256,256]{1,0:T(8,128)S(1)}, f32[256,256]{1,0:T(8,128)}, u32[]{:S(2)}) copy-start(f32[256,256]{1,0:T(8,128)} %constant.16.clone.refs_2_) | copy-start | bytes 786436
  1.9 11.4 %copy-start.2 = (bf16[256,256]{1,0:T(8,128)(2,1)S(1)}, bf16[256,256]{1,0:T(8,128)(2,1)}, u32[]{:S(2)}) copy-start(bf16[256,256]{1,0:T(8,128)(2,1)} %constant.14.clone.refs_0_) | copy-start | bytes 393220
  1.9 11.4 %copy-start.3 = (bf16[256,256]{1,0:T(8,128)(2,1)S(1)}, bf16[256,256]{1,0:T(8,128)(2,1)}, u32[]{:S(2)}) copy-start(bf16[256,256]{1,0:T(8,128)(2,1)} %constant.15.clone.refs_1_) | copy-start | bytes 393220
  2.7 7.9 %collective-permute-start.3 = (bf16[528,128]{1,0:T(8,128)(2,1)S(1)}, bf16[528,128]{1,0:T(8,128)(2,1)S(1)}, u32[]{:S(2)}, u32[]{:S(2)}) collective-permute-start(bf16[528,128]{1,0:T(8,128)(2,1)S(1)} %get-tuple-element.28), channel_id=1, source_target_pairs={{0,2},{1,3},{2,0},{3,1},{4,6},{5,7},{6,4},{7,5},{8,10},{9,11},{10,... | collective-permute-start | bytes 405512 | tf_op jit(solution)/shard_map/ppermute | solution.py:297
  5.8 6.9 %collective-permute-start.4 = (bf16[528,128]{1,0:T(8,128)(2,1)S(1)}, bf16[528,128]{1,0:T(8,128)(2,1)S(1)}, u32[]{:S(2)}, u32[]{:S(2)}) collective-permute-start(bf16[528,128]{1,0:T(8,128)(2,1)S(1)} %get-tuple-element.29), channel_id=1, source_target_pairs={{0,3},{1,2},{2,1},{3,0},{4,7},{5,6},{6,5},{7,4},{8,11},{9,10},{10,... | collective-permute-start | bytes 405512 | tf_op jit(solution)/shard_map/ppermute | solution.py:297
  5.8 7.5 %collective-permute-start.5 = (bf16[528,128]{1,0:T(8,128)(2,1)S(1)}, bf16[528,128]{1,0:T(8,128)(2,1)S(1)}, u32[]{:S(2)}, u32[]{:S(2)}) collective-permute-start(bf16[528,128]{1,0:T(8,128)(2,1)S(1)} %get-tuple-element.30), channel_id=1, source_target_pairs={{0,1},{1,0},{2,3},{3,2},{4,5},{5,4},{6,7},{7,6},{8,9},{9,8},{10,11... | collective-permute-start | bytes 405512 | tf_op jit(solution)/shard_map/ppermute | solution.py:297
  6.0 9.1 %collective-permute-start.6 = (s32[64,128]{1,0:T(8,128)S(1)}, s32[64,128]{1,0:T(8,128)S(1)}, u32[]{:S(2)}, u32[]{:S(2)}) collective-permute-start(s32[64,128]{1,0:T(8,128)S(1)} %reshape.17.cells_ref), channel_id=1, source_target_pairs={{0,4},{1,5},{2,6},{3,7},{4,0},{5,1},{6,2},{7,3},{8,12},{9,13},{10,... | collective-permute-start | bytes 98312 | tf_op jit(solution)/shard_map/ppermute | solution.py:297
  9.0 15.2 %collective-permute-start = (bf16[528,128]{1,0:T(8,128)(2,1)S(1)}, bf16[528,128]{1,0:T(8,128)(2,1)S(1)}, u32[]{:S(2)}, u32[]{:S(2)}) collective-permute-start(bf16[528,128]{1,0:T(8,128)(2,1)S(1)} %get-tuple-element.23), channel_id=1, source_target_pairs={{0,2},{1,3},{2,0},{3,1},{4,6},{5,7},{6,4},{7,5},{8,10},{9,11},{10,... | collective-permute-start | bytes 405512 | tf_op jit(solution)/shard_map/ppermute | solution.py:297
  10.6 13.6 %collective-permute-start.1 = (bf16[528,128]{1,0:T(8,128)(2,1)S(1)}, bf16[528,128]{1,0:T(8,128)(2,1)S(1)}, u32[]{:S(2)}, u32[]{:S(2)}) collective-permute-start(bf16[528,128]{1,0:T(8,128)(2,1)S(1)} %get-tuple-element.24), channel_id=1, source_target_pairs={{0,3},{1,2},{2,1},{3,0},{4,7},{5,6},{6,5},{7,4},{8,11},{9,10},{10,... | collective-permute-start | bytes 405512 | tf_op jit(solution)/shard_map/ppermute | solution.py:297
  12.7 11.5 %collective-permute-start.2 = (bf16[528,128]{1,0:T(8,128)(2,1)S(1)}, bf16[528,128]{1,0:T(8,128)(2,1)S(1)}, u32[]{:S(2)}, u32[]{:S(2)}) collective-permute-start(bf16[528,128]{1,0:T(8,128)(2,1)S(1)} %get-tuple-element.25), channel_id=1, source_target_pairs={{0,1},{1,0},{2,3},{3,2},{4,5},{5,4},{6,7},{7,6},{8,9},{9,8},{10,11... | collective-permute-start | bytes 405512 | tf_op jit(solution)/shard_map/ppermute | solution.py:297
  21.5 9.5 %collective-permute-start.7 = (bf16[368,128]{1,0:T(8,128)(2,1)S(1)}, bf16[368,128]{1,0:T(8,128)(2,1)S(1)}, u32[]{:S(2)}, u32[]{:S(2)}) collective-permute-start(bf16[368,128]{1,0:T(8,128)(2,1)S(1)} %shard_map.94), channel_id=1, source_target_pairs={{0,4},{1,5},{2,6},{3,7},{4,0},{5,1},{6,2},{7,3},{8,12},{9,13},{10,... | collective-permute-start | bytes 282632 | tf_op jit(solution)/shard_map/ppermute | solution.py:297
  31.0 3.9 %collective-permute-start.8 = (f32[8,128]{1,0:T(8,128)S(1)}, f32[8,128]{1,0:T(8,128)S(1)}, u32[]{:S(2)}, u32[]{:S(2)}) collective-permute-start(f32[8,128]{1,0:T(8,128)S(1)} %get-tuple-element.38), channel_id=1, source_target_pairs={{0,1},{1,0},{2,3},{3,2},{4,5},{5,4},{6,7},{7,6},{8,9},{9,8},{10,11... | collective-permute-start | bytes 12296 | tf_op jit(solution)/shard_map/ppermute | solution.py:297
  31.3 4.8 %copy-start.6 = (f32[4]{0:T(128)S(1)}, f32[4]{0:T(128)}, u32[]{:S(2)}) copy-start(f32[4]{0:T(128)} %weights_ref.1) | copy-start | bytes 52
  31.3 4.8 %collective-permute-start.9 = (f32[8,128]{1,0:T(8,128)S(1)}, f32[8,128]{1,0:T(8,128)S(1)}, u32[]{:S(2)}, u32[]{:S(2)}) collective-permute-start(f32[8,128]{1,0:T(8,128)S(1)} %get-tuple-element.39), channel_id=1, source_target_pairs={{1,2},{3,4},{5,6},{7,0},{2,1},{4,3},{6,5},{0,7},{9,10},{11,12},{13... | collective-permute-start | bytes 12296 | tf_op jit(solution)/shard_map/ppermute | solution.py:344
  36.1 4.4 %copy-start.8 = (f32[2,2048]{1,0:T(2,128)S(1)}, f32[2,2048]{1,0:T(2,128)}, u32[]{:S(2)}) copy-start(f32[2,2048]{1,0:T(2,128)} %param.14) | copy-start | bytes 49156
  37.0 4.2 %collective-permute-start.10 = (f32[96,128]{1,0:T(8,128)S(1)}, f32[96,128]{1,0:T(8,128)S(1)}, u32[]{:S(2)}, u32[]{:S(2)}) collective-permute-start(f32[96,128]{1,0:T(8,128)S(1)} %shard_map.98.refs_0_), channel_id=1, source_target_pairs={{0,8},{8,0},{16,24},{24,16},{1,9},{9,1},{17,25},{25,17},{2,10},{10... | collective-permute-start | bytes 147464 | tf_op jit(solution)/shard_map/ppermute | solution.py:353
  38.6 4.6 %collective-permute-start.11 = (f32[96,128]{1,0:T(8,128)S(1)}, f32[96,128]{1,0:T(8,128)S(1)}, u32[]{:S(2)}, u32[]{:S(2)}) collective-permute-start(f32[96,128]{1,0:T(8,128)S(1)} %shard_map.98.refs_0_), channel_id=1, source_target_pairs={{0,16},{8,24},{16,0},{24,8},{1,17},{9,25},{17,1},{25,9},{2,18},{10... | collective-permute-start | bytes 147464 | tf_op jit(solution)/shard_map/ppermute | solution.py:353
  40.1 5.0 %collective-permute-start.12 = (f32[96,128]{1,0:T(8,128)S(1)}, f32[96,128]{1,0:T(8,128)S(1)}, u32[]{:S(2)}, u32[]{:S(2)}) collective-permute-start(f32[96,128]{1,0:T(8,128)S(1)} %shard_map.98.refs_0_), channel_id=1, source_target_pairs={{0,24},{8,16},{16,8},{24,0},{1,25},{9,17},{17,9},{25,1},{2,26},{10... | collective-permute-start | bytes 147464 | tf_op jit(solution)/shard_map/ppermute | solution.py:353
